TPU v7x, 512 devices: a whole 4x4x16 slice. The times are simulated.
512 devices in a mesh: segment: 4 (over y_lo, core), ctx: 32 (over z, y_hi), head: 4 (over x).
Axes of the slice: x: 4, y: 4 (y_hi: 2, y_lo: 2; y = y_hi * 2 + y_lo), z: 16, core: 2. Of those that a mesh axis runs over, the one named last changes fastest.
Arguments:
- hidden: bfloat16 [4, 8192, 2880], P('segment', 'ctx', 'head'), may hold values from -450 to 450
- merge_weight: bfloat16 [3, 2880, 2880], P(None, 'head', 'segment'), may hold values from -0.0625 to 0.0625
- query_weight: bfloat16 [5760, 2048], P('ctx', ('segment', 'head')), may hold values from -1 to 1
- key_weight: bfloat16 [5760, 256], P('ctx', 'segment'), may hold values from -8 to 8
- value_weight: bfloat16 [5760, 256], P('ctx', 'segment'), may hold values from -0.078125 to 0.078125
- block_order: int32 [64], replicated, may hold values from 0 to 63, each once
Outputs:
- attended: bfloat16 [8192, 2048], P('ctx', ('segment', 'head'))
Inputs may be any that keep to these rules, and one draw needn't show every extreme that they name: `block_order`: a permutation of the sequence blocks.
All inputs are finite; a program needn't handle non-finite values.
Results may differ from a plain program's by a relative error of at most 0.023.
The roundings to bfloat16 on the way count: a program that leaves them out, or rounds other values in their place, can miss the bound.
Values may be sent and summed in bfloat16 or wider, within the bound.
No kernel may reach another device: no remote copies, remote signals or barrier semaphores. Data moves between devices by JAX's collectives and lax.ppermute only.
A program may use at most 64 MiB of HBM per device.

v0:
```python
import math

import jax
import jax.numpy as jnp
from jax import lax
from jax.sharding import PartitionSpec as P

HD = 64


def normalize(matrix):
    widened = matrix.astype(jnp.float32)
    return widened * lax.rsqrt(jnp.mean(widened * widened, axis=-1, keepdims=True) + 1e-06)


def seq_positions(row_ids, order, block_len):
    block_ids = jnp.arange(order.shape[0], dtype=jnp.int32)
    matches = (row_ids // block_len)[:, None] == block_ids[None, :]
    block_first = jnp.sum(jnp.where(matches, order[None, :], 0), axis=1)
    return block_first * block_len + row_ids % block_len


def attend_block(carry, query_heads, query_pos, key_blk, value_blk, key_pos):
    run_max, run_total, accum = carry
    tok_rows, heads_count, head_size = query_heads.shape
    scores = (
        jnp.einsum("tgd,nd->tgn", query_heads, key_blk, preferred_element_type=jnp.float32) * 0.125
    )
    allowed = key_pos[None, None, :] <= query_pos[:, None, None]
    scores = jnp.where(allowed, scores, -1e30)
    new_max = jnp.maximum(run_max, jnp.max(scores, axis=2))
    rescale = jnp.exp(run_max - new_max)
    unscaled = jnp.where(allowed, jnp.exp(scores - new_max[:, :, None]), 0.0)
    run_total = run_total * rescale + jnp.sum(unscaled, axis=2)
    mixed_rows = jnp.einsum(
        "tgn,nd->tgd", unscaled.astype(jnp.bfloat16), value_blk, preferred_element_type=jnp.float32
    )
    grown = accum.reshape(tok_rows, heads_count, head_size) * rescale[:, :, None] + mixed_rows
    return (new_max, run_total, grown.reshape(tok_rows, heads_count * head_size))


def body(hidden, merge_weight, query_weight, key_weight, value_weight, block_order):
    tok_rows = hidden.shape[1]
    block_len = tok_rows // 2
    segments = lax.axis_size("segment")
    heads_here = lax.axis_size("head")
    segment_id = lax.axis_index("segment")
    head_id = lax.axis_index("head")
    ctx_id = lax.axis_index("ctx")
    sections = lax.all_gather(hidden, "segment", axis=0, tiled=True)
    partial_value = jnp.einsum(
        "ktf,kfc->tc", sections[:3], merge_weight, preferred_element_type=jnp.float32
    )
    col_piece = partial_value.shape[1] // heads_here
    summed = lax.psum(partial_value, "head")
    merged_part = lax.dynamic_slice_in_dim(summed, head_id * col_piece, col_piece, 1)
    merged_part = merged_part.astype(jnp.bfloat16)
    embed_part = lax.dynamic_slice_in_dim(sections[3], segment_id * col_piece, col_piece, 1)
    merged_all, embed_mixed = (
        lax.all_gather(merged_part, ("segment", "head"), axis=1, tiled=True),
        lax.all_gather(embed_part, ("segment", "head"), axis=1, tiled=True),
    )
    embed_all = embed_mixed.reshape(tok_rows, segments, heads_here, col_piece).transpose(0, 2, 1, 3)
    embed_all = embed_all.reshape(tok_rows, segments * heads_here * col_piece)
    draft_input = jnp.concatenate([normalize(embed_all), normalize(merged_all)], axis=1).astype(
        jnp.bfloat16
    )
    query_piece = lax.all_gather(query_weight, "ctx", axis=0, tiled=True)
    key_piece = lax.all_gather(key_weight, "ctx", axis=0, tiled=True)
    value_piece = lax.all_gather(value_weight, "ctx", axis=0, tiled=True)
    query_acc = jnp.dot(draft_input, query_piece, preferred_element_type=jnp.float32)
    key_acc = jnp.dot(draft_input, key_piece, preferred_element_type=jnp.float32)
    value_acc = jnp.dot(draft_input, value_piece, preferred_element_type=jnp.float32)
    query_acc, key_acc, value_acc = (query_acc, key_acc, value_acc)
    query_heads = query_acc.astype(jnp.bfloat16).reshape(tok_rows, -1, HD)
    key_vectors = key_acc.astype(jnp.bfloat16)
    value_vectors = value_acc.astype(jnp.bfloat16)
    heads_count = query_heads.shape[1]
    query_pos = seq_positions(
        ctx_id * tok_rows + jnp.arange(tok_rows, dtype=jnp.int32), block_order, block_len
    )
    initial_attn = (
        jnp.full((tok_rows, heads_count), -1e30, jnp.float32),
        jnp.zeros((tok_rows, heads_count), jnp.float32),
        jnp.zeros((tok_rows, heads_count * HD), jnp.float32),
    )
    key_piece = lax.all_gather(key_vectors, "ctx", axis=0, tiled=True)
    value_piece = lax.all_gather(value_vectors, "ctx", axis=0, tiled=True)
    row_count = key_piece.shape[0]
    key_step = math.gcd(row_count, 512)

    def one_block(turn_index, carried):
        offset = turn_index * key_step
        key_blk = lax.dynamic_slice_in_dim(key_piece, offset, key_step, 0)
        value_blk = lax.dynamic_slice_in_dim(value_piece, offset, key_step, 0)
        key_pos = seq_positions(
            offset + jnp.arange(key_step, dtype=jnp.int32), block_order, block_len
        )
        return attend_block(carried, query_heads, query_pos, key_blk, value_blk, key_pos)

    run_max, run_total, accum = lax.fori_loop(0, row_count // key_step, one_block, initial_attn)
    output = accum.reshape(tok_rows, heads_count, HD) / run_total[:, :, None]
    return output.reshape(tok_rows, heads_count * HD).astype(jnp.bfloat16)


def solution(mesh):
    return jax.shard_map(
        body,
        mesh=mesh,
        in_specs=(
            P("segment", "ctx", "head"),
            P(None, "head", "segment"),
            P("ctx", ("segment", "head")),
            P("ctx", "segment"),
            P("ctx", "segment"),
            P(),
        ),
        out_specs=P("ctx", ("segment", "head")),
        check_vma=False,
    )
```

profile of v0, /device:TPU:6, one launch (start us, length us, event | category | flops | bytes accessed | tf_op | source)
XLA Modules:
  0.0 691.6 jit_solution(7909298819602587909)
XLA Ops:
  7.3 38.2 %all-gather.12.cloned.1.call-done = bf16[4,256,720]{1,2,0:T(8,128)(2,1)} async-done(((bf16[1,256,720]{1,2,0:T(8,128)(2,1)}), bf16[4,256,720]{1,2,0:T(8,128)(2,1)}) %all-gather.12.cloned.1.call-update) | async-done | bytes 1474576 | tf_op jit(solution)/shard_map/all_gather | solution.py:50
  47.5 3.6 convolution_bitcast_fusion
  51.0 26.4 %all-reduce.1 = bf16[256,720]{0,1:T(8,128)(2,1)} all-reduce(f32[256,720]{0,1:T(8,128)} %convolution_bitcast_fusion), channel_id=1, replica_groups=mesh['segment'=4,'ctx'=32,'head'=4] {'head'}, use_global_device_ids=true, to_apply=%region_1.0 | all-reduce | flops 184320 | bytes 1105920 | tf_op jit(solution)/shard_map/psum | solution.py:55
  79.7 83.0 %all-gather.4 = bf16[32,180,64]{1,2,0:T(8,128)(2,1)S(1)} all-gather(bf16[1,180,64]{1,2,0:T(8,128)(2,1)S(1)} %bitcast.59), channel_id=1, replica_groups=mesh['segment'=4,'ctx'=32,'head'=4] {'ctx'}, dimensions={0}, use_global_device_ids=true | all-gather | bytes 760320 | tf_op jit(solution)/shard_map/all_gather | solution.py:70
  164.2 3.1 reshape.158
  167.3 31.9 %multiply_reduce_fusion.1 = (f32[256]{0:T(256)S(1)}, f32[256,2880]{0,1:T(8,128)}) fusion(bf16[1,256,2880]{1,0,2:T(2,128)(2,1)} %all-gather.18.cloned.1.call-done), kind=kLoop, calls=%fused_computation.39 | loop fusion | flops 2211584 | bytes 4424704 | tf_op jit(solution)/shard_map/reduce_sum | solution.py:13
  199.3 4.0 reshape.145
  203.3 3.8 copy.26
  207.1 4.1 reshape.144
  211.2 3.4 reshape.159
  214.6 2.4 multiply_reduce_fusion
  222.5 77.8 %all-gather.2 = bf16[32,180,64]{1,2,0:T(8,128)(2,1)S(1)} all-gather(bf16[1,180,64]{1,2,0:T(8,128)(2,1)S(1)} %bitcast.60), channel_id=1, replica_groups=mesh['segment'=4,'ctx'=32,'head'=4] {'ctx'}, dimensions={0}, use_global_device_ids=true | all-gather | bytes 760320 | tf_op jit(solution)/shard_map/all_gather | solution.py:69
  301.9 3.2 reshape.154
  305.0 3.3 convolution_convert_fusion.2
  308.5 9.9 %all-gather.22.cloned.1.call-done = bf16[32,180,128]{2,1,0:T(8,128)(2,1)} async-done(((bf16[1,180,128]{2,1,0:T(8,128)(2,1)}), bf16[32,180,128]{2,1,0:T(8,128)(2,1)}) %all-gather.22.cloned.1.call-update) | async-done | bytes 1474576 | tf_op jit(solution)/shard_map/all_gather | solution.py:68
  318.4 3.3 reshape.156
  321.7 3.0 convolution_convert_fusion
  324.7 127.2 %all-gather.16.cloned.1.call-done = bf16[8192,64]{0,1:T(8,128)(2,1)} async-done(((bf16[256,64]{0,1:T(8,128)(2,1)}), bf16[8192,64]{0,1:T(8,128)(2,1)}) %all-gather.16.cloned.1.call-update) | async-done | bytes 1048592 | tf_op jit(solution)/shard_map/all_gather | solution.py:88
  451.9 132.5 %all-gather.14.cloned.1.call-done = bf16[8192,64]{0,1:T(8,128)(2,1)} async-done(((bf16[256,64]{0,1:T(8,128)(2,1)}), bf16[8192,64]{0,1:T(8,128)(2,1)}) %all-gather.14.cloned.1.call-update) | async-done | bytes 1048592 | tf_op jit(solution)/shard_map/all_gather | solution.py:87
  585.1 98.0 %while.20 = (s32[]{:T(128)}, f32[256,2]{0,1:T(2,128)S(1)}, f32[256,2]{0,1:T(2,128)S(1)}, f32[256,128]{0,1:T(8,128)}, s32[64]{0:T(128)S(1)}, /*index=5*/s32[256]{...) while((s32[]{:T(128)}, f32[256,2]{0,1:T(2,128)S(1)}, ...), condition=%wide.region_8.9_spmd.clone, body=%wide.region_4.8_spmd.clone.sunk | while | flops 69780480 | bytes 4175302 | solution.py:101
  585.4 2.2 fusion.48
  589.0 2.2 convolution_add_fusion.2
  591.5 2.2 fusion.48
  595.1 2.2 convolution_add_fusion.2
  597.6 2.2 fusion.48
  601.3 2.2 convolution_add_fusion.2
  603.7 2.2 fusion.48
  607.4 2.2 convolution_add_fusion.2
  609.9 2.2 fusion.48
  613.5 2.2 convolution_add_fusion.2
  616.0 2.2 fusion.48
  619.6 2.2 convolution_add_fusion.2
  622.1 2.2 fusion.48
  625.7 2.2 convolution_add_fusion.2
  628.2 2.2 fusion.48
  631.9 2.2 convolution_add_fusion.2
  638.0 2.2 convolution_add_fusion.2
  640.5 2.2 fusion.48
  644.1 2.2 convolution_add_fusion.2
  650.2 2.2 convolution_add_fusion.2
  652.7 2.2 fusion.48
  656.4 2.2 convolution_add_fusion.2
  662.5 2.2 convolution_add_fusion.2
  665.0 2.2 fusion.48
  668.6 2.2 convolution_add_fusion.2
  674.7 2.2 convolution_add_fusion.2
  677.2 2.2 fusion.48
  680.8 2.2 convolution_add_fusion.2
  (183 shorter events, 52.3 us)
Async XLA Ops:
  6.5 40.9 %copy-start = (bf16[3,720,720]{2,1,0:T(8,128)(2,1)S(1)}, bf16[3,720,720]{2,1,0:T(8,128)(2,1)}, u32[]{:S(2)}) copy-start(bf16[3,720,720]{2,1,0:T(8,128)(2,1)} %param.9) | copy-start | bytes 9331204
  6.5 39.0 %all-gather.12.cloned.1.call-start = ((), (), s32[]{:S(2)}) async-start(), calls=%async_computation | async-start | bytes 1843200 | tf_op jit(solution)/shard_map/all_gather | solution.py:50
  7.3 160.1 %all-gather.18.cloned.1.call-start = ((), (), s32[]{:S(2)}) async-start(), calls=%async_computation.3 | async-start | bytes 3133440 | tf_op jit(solution)/shard_map/all_gather | solution.py:61
  47.4 163.8 %all-gather.20.cloned.1.call-start = ((), (), s32[]{:S(2)}) async-start(), calls=%async_computation.4 | async-start | bytes 1601536 | tf_op jit(solution)/shard_map/all_gather | solution.py:60
  47.5 32.2 %copy-start.6 = (bf16[180,64]{0,1:T(8,128)(2,1)S(1)}, bf16[180,64]{0,1:T(8,128)(2,1)}, u32[]{:S(2)}) copy-start(bf16[180,64]{0,1:T(8,128)(2,1)} %param.12) | copy-start | bytes 69124
  79.0 239.4 %all-gather.22.cloned.1.call-start = ((), (), s32[]{:S(2)}) async-start(), calls=%async_computation.5 | async-start | bytes 1554432 | tf_op jit(solution)/shard_map/all_gather | solution.py:68
  79.6 372.3 %all-gather.16.cloned.1.call-start = ((), (), s32[]{:S(2)}) async-start(), calls=%async_computation.2 | async-start | bytes 1081344 | tf_op jit(solution)/shard_map/all_gather | solution.py:88
  214.6 2.7 copy-start.1
  217.0 1.9 copy-start.2
  218.9 1.1 copy-start.3
  218.9 2.2 copy-start.5
  220.1 1.1 copy-start.4
  221.2 1.3 copy-start.7
  222.4 362.0 %all-gather.14.cloned.1.call-start = ((), (), s32[]{:S(2)}) async-start(), calls=%async_computation.1 | async-start | bytes 1081344 | tf_op jit(solution)/shard_map/all_gather | solution.py:87
  305.0 3.4 copy-start.8
Sparse Core Ops, SparseCore 0:
  9.5 36.0 all-gather.11
  47.6 58.7 all-gather.17
  108.5 55.7 all-gather.19
  167.3 151.0 all-gather.21
  321.2 130.6 all-gather.15
  454.7 129.7 all-gather.13
where the time goes:
time: 694 us; the launch traced here: 692 us
  waiting for transfers between devices  309 us (45%)
  blocking collectives  187 us (27%)
  matrix products  81 us (12%)
  other arithmetic  63.7 us (9%)
  local copies, waits for them, and re-layouts  36.5 us (5%)
  between operations  13.6 us (2%)
    all_gather x1, waiting for transfers between devices, body(): key_piece = lax.all_gather(key_vectors, 'ctx', axis=0, tiled=True)  133 us
    all_gather x1, waiting for transfers between devices, body(): value_piece = lax.all_gather(value_vectors, 'ctx', axis=0, tiled=True)  127 us
    all_gather x1, blocking collectives, body(): value_piece = lax.all_gather(value_weight, 'ctx', axis=0, tiled=True)  83 us
    all_gather x1, blocking collectives, body(): key_piece = lax.all_gather(key_weight, 'ctx', axis=0, tiled=True)  77.8 us
    all_gather x1, waiting for transfers between devices, body(): sections = lax.all_gather(hidden, 'segment', axis=0, tiled=True)  38.2 us
    dot_general x16, matrix products, attend_block(): jnp.einsum('tgn,nd->tgd', unscaled.astype(jnp.bfloat16), value_blk, prefe...  35.4 us
    dot_general x16, matrix products, attend_block(): jnp.einsum('tgd,nd->tgn', query_heads, key_blk, preferred_element_type=jn...  34.5 us
    reduce_sum x2, other arithmetic, normalize(): jnp.mean(widened * widened, axis=-1, keepdims=True) + 1e-06  34.3 us
  transfers between devices with their start and end apart: 6, of which 4 were waited for; matrix products, arithmetic and copies ran while one was open for 11% of the time, Pallas kernels for 0%

commit v1 on v0

v1 whole, which is shorter than its diff:
```python
import jax
import jax.numpy as jnp
from jax import lax
from jax.experimental import pallas as pl
from jax.experimental.pallas import tpu as pltpu
from jax.sharding import Mesh, PartitionSpec as P

HD = 64
BLK = 128
SEG = ("yl", "core")
CTX = ("z", "yh")
VMEM = pl.BlockSpec(memory_space=pltpu.VMEM)
DIM0 = (((0,), (0,)), ((), ()))


def project_kernel(rows_ref, weights_ref, quarter_ref, query_ref, kv_ref, sent_ref):
    n_x, n_seg, _, chunk, tokens = rows_ref.shape
    width = n_x * n_seg * chunk
    scales = []
    for kind in range(2):
        total = jnp.zeros((1, tokens), jnp.float32)
        for i in range(n_x):
            for s in range(n_seg):
                part = rows_ref[i, s, kind].astype(jnp.float32)
                total = total + jnp.sum(part * part, axis=0, keepdims=True)
        scales.append(lax.rsqrt(total / width + 1e-06))
    acc = jnp.zeros((weights_ref.shape[2], tokens), jnp.float32)
    for kind in range(2):
        for i in range(n_x):
            for s in range(n_seg):
                at = i * n_seg + s if kind == 0 else n_x * n_seg + s * n_x + i
                normed = (rows_ref[i, s, kind].astype(jnp.float32) * scales[kind]).astype(jnp.bfloat16)
                acc = acc + lax.dot_general(weights_ref[at], normed, DIM0, preferred_element_type=jnp.float32)
    half = acc.shape[0] // 2
    query_ref[...] = acc[:half].astype(jnp.bfloat16)
    kv_ref[...] = acc[half:].T.astype(jnp.bfloat16)
    size = sent_ref.shape[1]
    start = pl.multiple_of(quarter_ref[0] * size, size)
    quarter = kv_ref[pl.ds(start, size), :]
    for i in range(sent_ref.shape[0]):
        sent_ref[i] = quarter


def attend_kernel(query_ref, own_ref, all_ref, bias_ref, out_ref):
    zeros = jnp.zeros((HD, BLK), jnp.bfloat16)
    pieces = []
    for a in range(2):
        for g in range(2):
            piece = query_ref[g * HD : (g + 1) * HD, a * BLK : (a + 1) * BLK] * jnp.bfloat16(0.125)
            pieces.append(jnp.concatenate([piece, zeros], axis=0))
    queries = jnp.concatenate(pieces, axis=1)
    lanes = queries.shape[1]
    key_row = lax.broadcasted_iota(jnp.int32, (BLK, lanes // 2), 0)
    query_row = lax.broadcasted_iota(jnp.int32, (BLK, lanes // 2), 1) % BLK
    tops, totals, accums = [], [], []
    for a in range(2):
        own = own_ref[a * BLK : (a + 1) * BLK, :]
        scores = jnp.dot(own, queries[:, a * 2 * BLK : (a + 1) * 2 * BLK], preferred_element_type=jnp.float32)
        scores = jnp.where(key_row <= query_row, scores, -1e30)
        top = jnp.max(scores, axis=0, keepdims=True)
        weights = jnp.exp(scores - top)
        tops.append(top)
        totals.append(jnp.sum(weights, axis=0, keepdims=True))
        accums.append(lax.dot_general(own, weights.astype(jnp.bfloat16), DIM0, preferred_element_type=jnp.float32))
    top, total, accum = (jnp.concatenate(v, axis=1) for v in (tops, totals, accums))
    groups, chunk, _ = all_ref.shape
    step = 16

    def one(turn, carry):
        top, total, accum = carry
        first = pl.multiple_of(turn * step, step)
        keys = all_ref[pl.ds(first, step)].reshape(step * chunk, 2 * HD)
        bias = bias_ref[pl.ds(first, step), :]
        scores = jnp.dot(keys, queries, preferred_element_type=jnp.float32)
        scores = scores.reshape(step, chunk, lanes)
        highest = jnp.max(scores, axis=1) + bias
        new_top = jnp.maximum(top, jnp.max(highest, axis=0, keepdims=True))
        weights = jnp.exp(scores + (bias - new_top)[:, None, :])
        rescale = jnp.exp(top - new_top)
        total = total * rescale + jnp.sum(weights.reshape(step * chunk, lanes), axis=0, keepdims=True)
        mixed = lax.dot_general(
            keys,
            weights.reshape(step * chunk, lanes).astype(jnp.bfloat16),
            DIM0,
            preferred_element_type=jnp.float32,
        )
        return new_top, total, accum * rescale + mixed

    top, total, accum = lax.fori_loop(0, groups // step, one, (top, total, accum))
    result = accum[HD:] / total
    for a in range(2):
        left = result[:, 2 * a * BLK : (2 * a + 1) * BLK]
        right = result[:, (2 * a + 1) * BLK : (2 * a + 2) * BLK]
        out_ref[a * BLK : (a + 1) * BLK, :] = jnp.concatenate([left, right], axis=0).T.astype(jnp.bfloat16)


def body(hidden, merge_weight, query_weight, key_weight, value_weight, block_order):
    tokens, features = hidden.shape[1:]
    n_x, n_seg = lax.axis_size("x"), lax.axis_size(SEG)
    n_ctx = lax.axis_size(CTX)
    x_id, seg_id, ctx_id = lax.axis_index("x"), lax.axis_index(SEG), lax.axis_index(CTX)
    chunk = features // n_seg

    weights = jnp.concatenate([query_weight, key_weight, value_weight], axis=1)
    weights = lax.all_gather(weights, "yh", axis=0)
    weights = lax.all_gather(weights, "z", axis=0)
    weights = weights.reshape(n_ctx, *weights.shape[2:])

    turned = hidden[0].T
    half = features // 2
    low = lax.all_gather(turned[:half], SEG, axis=0)
    high = lax.all_gather(turned[half:], SEG, axis=0)
    sections = jnp.concatenate([low, high], axis=1)
    partial = jnp.einsum("kft,kfc->ct", sections[:3], merge_weight, preferred_element_type=jnp.float32)
    parts = lax.all_to_all(partial.reshape(n_x, chunk, tokens), "x", 0, 0)
    merged = jnp.sum(parts, axis=0).astype(jnp.bfloat16)
    embed = lax.dynamic_slice_in_dim(sections[3], seg_id * chunk, chunk, 0)
    rows = jnp.stack([embed, merged])
    rows = lax.all_gather(rows, SEG, axis=0)
    rows = lax.all_to_all(jnp.broadcast_to(rows, (n_x, *rows.shape)), "x", 0, 0)

    quarter = tokens // n_x
    query, own_kv, sent = pl.pallas_call(
        project_kernel,
        out_shape=(
            jax.ShapeDtypeStruct((2 * HD, tokens), jnp.bfloat16),
            jax.ShapeDtypeStruct((tokens, 2 * HD), jnp.bfloat16),
            jax.ShapeDtypeStruct((n_ctx, quarter, 2 * HD), jnp.bfloat16),
        ),
        in_specs=[VMEM, VMEM, pl.BlockSpec(memory_space=pltpu.SMEM)],
        out_specs=(VMEM, VMEM, VMEM),
        compiler_params=pltpu.CompilerParams(vmem_limit_bytes=40 << 20),
        name="project",
    )(rows, weights, x_id.reshape(1))

    taken = lax.all_to_all(sent, ("yh", "z"), 0, 0)
    taken = lax.all_to_all(jnp.broadcast_to(taken, (n_x, *taken.shape)), "x", 0, 0)
    taken = taken.reshape(n_x * n_ctx, quarter, 2 * HD)

    n_z, n_yh = lax.axis_size("z"), lax.axis_size("yh")
    placed = block_order.reshape(n_z, n_yh, 2).transpose(2, 1, 0)
    placed = jnp.repeat(placed, n_x // 2, axis=0).reshape(n_x * n_ctx)
    mine = lax.dynamic_slice_in_dim(block_order, ctx_id * 2, 2, 0)
    mine = jnp.repeat(mine, 2 * BLK)
    bias = jnp.where(placed[:, None] < mine[None, :], 0.0, -1e30).astype(jnp.float32)

    return pl.pallas_call(
        attend_kernel,
        out_shape=jax.ShapeDtypeStruct((tokens, 2 * HD), jnp.bfloat16),
        in_specs=[VMEM, VMEM, VMEM, VMEM],
        out_specs=VMEM,
        compiler_params=pltpu.CompilerParams(vmem_limit_bytes=40 << 20),
        name="attend",
    )(query, own_kv, taken, bias)


def solution(mesh):
    shape = mesh.shape
    grid = mesh.devices.reshape(2, shape["segment"] // 2, shape["ctx"] // 2, 2, shape["head"])
    fine = Mesh(grid, ("yl", "core", "z", "yh", "x"))
    return jax.shard_map(
        body,
        mesh=fine,
        in_specs=(
            P(SEG, CTX, "x"),
            P(None, "x", SEG),
            P(CTX, (*SEG, "x")),
            P(CTX, SEG),
            P(CTX, SEG),
            P(),
        ),
        out_specs=P(CTX, (*SEG, "x")),
        check_vma=False,
    )
```

time: 694 us -> 219 us (0.32)
  the two profiles are of different devices: /device:TPU:6 before, /device:TPU:8 now
where the time goes in v1:
time: 219 us; the launch traced here: 218 us
  blocking collectives  81 us (37%)
  waiting for transfers between devices  71.7 us (33%)
  local copies, waits for them, and re-layouts  19.5 us (9%)
  between operations  13.5 us (6%)
  starting transfers between devices  13.2 us (6%)
  Pallas kernels  13 us (6%)
  other arithmetic  3.88 us (2%)
  matrix products  2.33 us (1%)
    all_to_all x1, blocking collectives, body(): taken = lax.all_to_all(sent, ('yh', 'z'), 0, 0)  45.3 us
    all_to_all x1, waiting for transfers between devices, body(): rows = lax.all_to_all(jnp.broadcast_to(rows, (n_x, *rows.shape)), 'x', 0, 0)  36.3 us
    all_to_all x1, waiting for transfers between devices, body(): lax.all_to_all(jnp.broadcast_to(taken, (n_x, *taken.shape)), 'x', 0, 0)  23.5 us
    all_gather x1, blocking collectives, body(): low = lax.all_gather(turned[:half], SEG, axis=0)  12.7 us
    all_to_all x1, waiting for transfers between devices, body(): parts = lax.all_to_all(partial.reshape(n_x, chunk, tokens), 'x', 0, 0)  11.8 us
    pallas_call x1, Pallas kernels, body(): pl.pallas_call(attend_kernel, out_shape=jax.ShapeDtypeStruct((tokens, 2 *...  11.2 us
    all_gather x1, blocking collectives, body(): high = lax.all_gather(turned[half:], SEG, axis=0)  8.44 us
    all_gather x1, blocking collectives, body(): rows = lax.all_gather(rows, SEG, axis=0)  7.75 us
  transfers between devices with their start and end apart: 4, of which 3 were waited for; matrix products, arithmetic and copies ran while one was open for 7% of the time, Pallas kernels for 0%

profile of v1, /device:TPU:8, one launch (start us, length us, event | category | flops | bytes accessed | tf_op | source)
XLA Modules:
  0.0 218.1 jit_solution(12423579341138686872)
XLA Ops:
  6.5 0.0 copy-start
  6.5 0.0 all-gather.8.cloned.1.call-start
  6.5 1.0 copy.17
  7.6 0.9 copy.18
  8.4 0.9 maximum_bitcast_fusion
  9.3 6.9 %all-gather.5 = bf16[2,180,256]{2,1,0:T(8,128)(2,1)} all-gather(bf16[1,180,256]{2,1,0:T(8,128)(2,1)S(1)} %maximum_bitcast_fusion), channel_id=5, replica_groups=mesh['yl'=2,'core'=2,'z'=16,'yh'=2,'x'=4] {'yh'}, dimensions={0}, use_global_device_ids=true | all-gather | bytes 276480 | tf_op jit(solution)/shard_map/all_gather | solution.py:105
  16.2 0.0 all-gather.8.cloned.1.call-update
  16.2 1.0 fusion.9
  17.3 12.7 %all-gather = bf16[1440,256]{1,0:T(8,128)(2,1)S(1)} all-gather(bf16[360,256]{1,0:T(8,128)(2,1)S(1)} %get-tuple-element.11), channel_id=2, replica_groups=mesh['yl'=2,'core'=2,'z'=16,'yh'=2,'x'=4] {'yl','core'}, dimensions={0}, use_global_device_ids=true | all-gather | bytes 921600 | tf_op jit(solution)/shard_map/all_gather | solution.py:111
  29.9 0.0 copy-start.4
  29.9 8.4 %all-gather.1 = bf16[1440,256]{1,0:T(8,128)(2,1)S(1)} all-gather(bf16[360,256]{1,0:T(8,128)(2,1)S(1)} %get-tuple-element.12), channel_id=3, replica_groups=mesh['yl'=2,'core'=2,'z'=16,'yh'=2,'x'=4] {'yl','core'}, dimensions={0}, use_global_device_ids=true | all-gather | bytes 921600 | tf_op jit(solution)/shard_map/all_gather | solution.py:112
  38.4 0.0 copy-start.5
  38.4 0.0 copy-done.4
  38.4 0.9 copy-done.5
  39.3 0.0 copy-done
  39.3 2.3 %fusion.4 = f32[720,256]{1,0:T(8,128)} fusion(bf16[3,720,720]{2,1,0:T(8,128)(2,1)S(1)} %copy-done, bf16[4,360,256]{2,1,0:T(8,128)(2,1)S(1)} %bitcast.25, bf16[4,360,256]{2,1,0:T(8,128)(2,1)S(1)} %bitcast.23), kind=kOutput, calls=%fused_computation.4 | convolution fusion | flops 799211520 | bytes 5322240 | tf_op jit(solution)/shard_map/kft,kfc->ct/dot_general | solution.py:114
  41.6 2.0 reshape.27
  43.7 4.2 %all-to-all-start = ((f32[4,180,256]{2,1,0:T(8,128)}), f32[4,180,256]{2,1,0:T(8,128)}, u32[]{:S(2)}, u32[]{:S(2)}) async-start(f32[4,180,256]{2,1,0:T(8,128)} %reshape.27), calls=%async_computation | async-start | bytes 1507328 | tf_op jit(solution)/shard_map/all_to_all | solution.py:115
  47.9 1.0 fusion.7
  48.9 11.8 %all-to-all-done = f32[4,180,256]{2,1,0:T(8,128)} async-done(((f32[4,180,256]{2,1,0:T(8,128)}), f32[4,180,256]{2,1,0:T(8,128)}, u32[]{:S(2)}, u32[]{:S(2)}) %all-to-all-start) | async-done | bytes 737312 | tf_op jit(solution)/shard_map/all_to_all | solution.py:115
  60.7 1.2 reduce_sum.9
  61.9 7.8 %all-gather.2 = bf16[8,180,256]{2,1,0:T(8,128)(2,1)S(1)} all-gather(bf16[2,180,256]{2,1,0:T(8,128)(2,1)S(1)} %pad_maximum_fusion), channel_id=4, replica_groups=mesh['yl'=2,'core'=2,'z'=16,'yh'=2,'x'=4] {'yl','core'}, dimensions={0}, use_global_device_ids=true | all-gather | bytes 921600 | tf_op jit(solution)/shard_map/all_gather | solution.py:119
  69.6 0.4 copy.16
  70.0 2.4 %broadcast_in_dim.20 = bf16[4,4,2,180,256]{4,1,3,2,0:T(4,128)(2,1)} broadcast(bf16[4,2,180,256]{3,0,2,1:T(4,128)(2,1)S(1)} %copy.16), dimensions={1,2,3,4} | broadcast | bytes 3686400 | tf_op jit(solution)/shard_map/broadcast_in_dim | solution.py:120
  72.4 4.6 %all-to-all-start.1 = ((bf16[4,4,2,180,256]{4,1,3,2,0:T(4,128)(2,1)}), bf16[4,4,2,180,256]{4,1,3,2,0:T(4,128)(2,1)}, u32[]{:S(2)}, u32[]{:S(2)}) async-start(bf16[4,4,2,180,256]{4,1,3,2,0:T(4,128)(2,1)} %broadcast_in_dim.20), calls=%async_computation.1 | async-start | bytes 5898240 | tf_op jit(solution)/shard_map/all_to_all | solution.py:120
  77.0 36.3 %all-to-all-done.1 = bf16[4,4,2,180,256]{4,1,3,2,0:T(4,128)(2,1)} async-done(((bf16[4,4,2,180,256]{4,1,3,2,0:T(4,128)(2,1)}), bf16[4,4,2,180,256]{4,1,3,2,0:T(4,128)(2,1)}, u32[]{:S(2)}, u32[]{:S(2)}) %all-to-all-start.1) | async-done | bytes 2949152 | tf_op jit(solution)/shard_map/all_to_all | solution.py:120
  113.3 3.9 %copy.19.rows_ref = bf16[4,4,2,180,256]{4,3,2,1,0:T(8,128)(2,1)} copy(bf16[4,4,2,180,256]{4,1,3,2,0:T(4,128)(2,1)} %all-to-all-done.1) | data formatting | bytes 5898240 | tf_op jit(solution)/shard_map/all_to_all | solution.py:120
  117.2 0.0 all-gather.8.cloned.1.call-done.weights_ref
  117.2 0.0 copy-start.1
  117.2 1.9 copy-done.1
  119.0 0.0 copy-start.2
  119.1 1.9 copy-done.2
  120.9 1.9 project.1
  122.8 45.3 %all_to_all.20 = bf16[32,64,128]{2,1,0:T(8,128)(2,1)S(1)} all-to-all(bf16[32,64,128]{2,1,0:T(8,128)(2,1)S(1)} %get-tuple-element.10), channel_id=1, replica_groups=mesh['yl'=2,'core'=2,'z'=16,'yh'=2,'x'=4] {'yh','z'}, dimensions={0} | all-to-all | bytes 1048576 | tf_op jit(solution)/shard_map/all_to_all | solution.py:136
  168.1 0.0 copy-start.6
  168.1 1.8 broadcast_in_dim.21
  169.9 4.4 %all-to-all-start.3 = ((bf16[4,32,64,128]{3,2,1,0:T(8,128)(2,1)}), bf16[4,32,64,128]{3,2,1,0:T(8,128)(2,1)}, u32[]{:S(2)}, u32[]{:S(2)}) async-start(bf16[4,32,64,128]{3,2,1,0:T(8,128)(2,1)} %broadcast_in_dim.21), calls=%async_computation.3 | async-start | bytes 4194304 | tf_op jit(solution)/shard_map/all_to_all | solution.py:137
  174.4 0.0 copy-done.6
  174.4 0.1 reshape.31
  174.5 0.1 dynamic_slice.7
  174.6 0.1 broadcast_bitcast_fusion
  174.7 0.1 copy.20
  174.7 0.1 lt.24
  174.8 0.8 compare_select_fusion.bias_ref
  175.6 23.5 %all-to-all-done.3 = bf16[4,32,64,128]{3,2,1,0:T(8,128)(2,1)} async-done(((bf16[4,32,64,128]{3,2,1,0:T(8,128)(2,1)}), bf16[4,32,64,128]{3,2,1,0:T(8,128)(2,1)}, u32[]{:S(2)}, u32[]{:S(2)}) %all-to-all-start.3) | async-done | bytes 2097184 | tf_op jit(solution)/shard_map/all_to_all | solution.py:137
  199.2 0.0 copy-start.3
  199.2 0.9 copy-done.3
  200.1 11.2 %attend.1 = bf16[256,128]{1,0:T(8,128)(2,1)} custom-call(bf16[128,256]{1,0:T(8,128)(2,1)S(1)} %get-tuple-element.8.query_ref, bf16[256,128]{1,0:T(8,128)(2,1)S(1)} %get-tuple-element.9.own_ref, bf16[128,64,128]{2,1,0:T(8,128)(2,1)} %bitcast.11.all_ref, f32[128,512]{1,0:T(8,128)S(1)} %copy-done.3), custom_call_target="tpu_custom_call" | custom-call | tf_op jit(solution)/shard_map/attend/pallas_call | solution.py:147
  (3 shorter events, 0.0 us)
Async XLA Ops:
  6.5 32.7 %copy-start = (bf16[3,720,720]{2,1,0:T(8,128)(2,1)S(1)}, bf16[3,720,720]{2,1,0:T(8,128)(2,1)}, u32[]{:S(2)}) copy-start(bf16[3,720,720]{2,1,0:T(8,128)(2,1)} %param.7) | copy-start | bytes 9331204
  6.5 110.7 %all-gather.8.cloned.1.call-start = ((), (), s32[]{:S(2)}) async-start(), calls=%async_computation.4 | async-start | bytes 3203072 | tf_op jit(solution)/shard_map/all_gather | solution.py:106
  29.9 8.4 %copy-start.4 = (bf16[1440,256]{1,0:T(8,128)(2,1)}, bf16[1440,256]{1,0:T(8,128)(2,1)S(1)}, u32[]{:S(2)}) copy-start(bf16[1440,256]{1,0:T(8,128)(2,1)S(1)} %all-gather) | copy-start | bytes 2211844
  38.4 0.9 copy-start.5
  43.7 17.0 %all-to-all-start = ((f32[4,180,256]{2,1,0:T(8,128)}), f32[4,180,256]{2,1,0:T(8,128)}, u32[]{:S(2)}, u32[]{:S(2)}) async-start(f32[4,180,256]{2,1,0:T(8,128)} %reshape.27), calls=%async_computation | async-start | bytes 1507328 | tf_op jit(solution)/shard_map/all_to_all | solution.py:115
  72.4 40.9 %all-to-all-start.1 = ((bf16[4,4,2,180,256]{4,1,3,2,0:T(4,128)(2,1)}), bf16[4,4,2,180,256]{4,1,3,2,0:T(4,128)(2,1)}, u32[]{:S(2)}, u32[]{:S(2)}) async-start(bf16[4,4,2,180,256]{4,1,3,2,0:T(4,128)(2,1)} %broadcast_in_dim.20), calls=%async_computation.1 | async-start | bytes 5898240 | tf_op jit(solution)/shard_map/all_to_all | solution.py:120
  117.2 1.9 copy-start.1
  119.0 1.9 copy-start.2
  168.1 6.3 %copy-start.6 = (s32[64]{0:T(128)S(1)}, s32[64]{0:T(128)}, u32[]{:S(2)}) copy-start(s32[64]{0:T(128)} %param.11) | copy-start | bytes 772
  169.9 29.3 %all-to-all-start.3 = ((bf16[4,32,64,128]{3,2,1,0:T(8,128)(2,1)}), bf16[4,32,64,128]{3,2,1,0:T(8,128)(2,1)}, u32[]{:S(2)}, u32[]{:S(2)}) async-start(bf16[4,32,64,128]{3,2,1,0:T(8,128)(2,1)} %broadcast_in_dim.21), calls=%async_computation.3 | async-start | bytes 4194304 | tf_op jit(solution)/shard_map/all_to_all | solution.py:137
  199.2 1.0 copy-start.3
Sparse Core Ops, SparseCore 0:
  16.3 80.3 all-gather.7

commit v2 on v1

v2 whole, which is shorter than its diff:
```python
import jax
import jax.numpy as jnp
from jax import lax
from jax.experimental import pallas as pl
from jax.experimental.pallas import tpu as pltpu
from jax.sharding import Mesh, PartitionSpec as P

HD = 64
BLK = 128
SEG = ("yl", "core")
CTX = ("z", "yh")
VMEM = pl.BlockSpec(memory_space=pltpu.VMEM)
DIM0 = (((0,), (0,)), ((), ()))


def pack_kernel(query_ref, key_ref, value_ref, out_ref):
    turned = jnp.concatenate([key_ref[...], value_ref[...]], axis=0).astype(jnp.float32)
    out_ref[:, : query_ref.shape[1]] = query_ref[...]
    out_ref[:, query_ref.shape[1] :] = turned.T.astype(jnp.bfloat16)


def merge_kernel(low_ref, high_ref, weight_ref, place_ref, partial_ref, embed_ref, hold_ref):
    split, total = low_ref.shape[1], weight_ref.shape[1]
    chunks, chunk, _ = partial_ref.shape
    hold_ref[:split] = low_ref[3].astype(jnp.float32)
    hold_ref[split:] = high_ref[3].astype(jnp.float32)
    embed_ref[...] = jnp.zeros_like(embed_ref)
    for half in range(2):
        first, second = hold_ref[pl.ds(half * chunk, chunk), :], hold_ref[pl.ds((2 + half) * chunk, chunk), :]
        block = jnp.where(place_ref[0] == 0, first, second).astype(jnp.bfloat16)
        for i in range(chunks):
            embed_ref[2 * i + half, :chunk] = block
    acc = None
    for k in range(3):
        for ref, rows in ((low_ref, slice(0, split)), (high_ref, slice(split, total))):
            term = lax.dot_general(weight_ref[k, rows, :], ref[k], DIM0, preferred_element_type=jnp.float32)
            acc = term if acc is None else acc + term
    hold_ref[...] = acc
    for i in range(chunks):
        partial_ref[i] = hold_ref[pl.ds(i * chunk, chunk), :]


def settle_kernel(parts_ref, out_ref):
    total = parts_ref[0]
    for i in range(1, parts_ref.shape[0]):
        total = total + parts_ref[i]
    out_ref[...] = jnp.zeros_like(out_ref)
    out_ref[: parts_ref.shape[1]] = total.astype(jnp.bfloat16)


def spread_kernel(block_ref, out_ref):
    count = block_ref.shape[0]
    for i in range(out_ref.shape[0] // count):
        out_ref[i * count : (i + 1) * count] = block_ref[...]


def project_kernel(
    embed_own, embed_other, merged_own, merged_other, weights_ref, place_ref, query_ref, sent_ref
):
    core, x_id = place_ref[0], place_ref[1]
    chunks, _, tokens = embed_own.shape
    chunk = weights_ref.shape[1]
    width = 2 * chunks * chunk
    acc = jnp.zeros((weights_ref.shape[2], tokens), jnp.float32)
    for kind, pair in enumerate(((embed_own, embed_other), (merged_own, merged_other))):
        total = jnp.zeros((1, tokens), jnp.float32)
        for ref in pair:
            for i in range(chunks):
                part = ref[i, :chunk].astype(jnp.float32)
                total = total + jnp.sum(part * part, axis=0, keepdims=True)
        scale = lax.rsqrt(total / width + 1e-06)
        for ref, side in zip(pair, (core, 1 - core)):
            for i in range(chunks):
                if kind == 0:
                    at = i // 2 * 4 + 2 * side + i % 2
                else:
                    at = 2 * chunks + (2 * (i % 2) + side) * 4 + i // 2
                normed = (ref[i, :chunk].astype(jnp.float32) * scale).astype(jnp.bfloat16)
                acc = acc + lax.dot_general(weights_ref[at], normed, DIM0, preferred_element_type=jnp.float32)
    half = acc.shape[0] // 2
    query_ref[...] = acc[:half].astype(jnp.bfloat16)
    rows = acc[half:].T.astype(jnp.bfloat16)
    size = sent_ref.shape[1]
    quarter = rows[:size]
    for i in range(1, tokens // size):
        quarter = jnp.where(x_id == i, rows[i * size : (i + 1) * size], quarter)
    for i in range(sent_ref.shape[0]):
        sent_ref[i] = quarter


def attend_kernel(query_ref, sent_ref, all_ref, bias_ref, place_ref, out_ref):
    x_id = place_ref[1]
    own = sent_ref[0]
    groups, chunk, _ = all_ref.shape
    zeros = jnp.zeros((HD, BLK), jnp.bfloat16)
    lanes = 4 * BLK
    key_row = lax.broadcasted_iota(jnp.int32, (chunk, lanes), 0) + (x_id % 2) * chunk
    lane = lax.broadcasted_iota(jnp.int32, (chunk, lanes), 1)
    own_bias = jnp.where((lane // (2 * BLK) == x_id // 2) & (key_row <= lane % BLK), 0.0, -1e30)
    step = 16
    for source in range(query_ref.shape[0]):
        pieces = []
        for a in range(2):
            for g in range(2):
                piece = query_ref[source, g * HD : (g + 1) * HD, a * BLK : (a + 1) * BLK]
                pieces.append(jnp.concatenate([piece * jnp.bfloat16(0.125), zeros], axis=0))
        queries = jnp.concatenate(pieces, axis=1)
        scores = jnp.dot(own, queries, preferred_element_type=jnp.float32) + own_bias
        top = jnp.maximum(jnp.max(scores, axis=0, keepdims=True), -1e20)
        weights = jnp.exp(scores - top)
        total = jnp.sum(weights, axis=0, keepdims=True)
        accum = lax.dot_general(own, weights.astype(jnp.bfloat16), DIM0, preferred_element_type=jnp.float32)
        for first in range(0, groups, step):
            keys = all_ref[first : first + step].reshape(step * chunk, 2 * HD)
            bias = bias_ref[first : first + step, :]
            scores = jnp.dot(keys, queries, preferred_element_type=jnp.float32)
            scores = scores.reshape(step, chunk, lanes)
            highest = jnp.max(scores, axis=1) + bias
            new_top = jnp.maximum(top, jnp.max(highest, axis=0, keepdims=True))
            weights = jnp.exp(scores + (bias - new_top)[:, None, :])
            rescale = jnp.exp(top - new_top)
            weights = weights.reshape(step * chunk, lanes)
            total = total * rescale + jnp.sum(weights, axis=0, keepdims=True)
            mixed = lax.dot_general(
                keys, weights.astype(jnp.bfloat16), DIM0, preferred_element_type=jnp.float32
            )
            accum = accum * rescale + mixed
            top = new_top
        out_ref[source, :HD] = accum[HD:]
        row = lax.broadcasted_iota(jnp.int32, (8, lanes), 0)
        out_ref[source, HD:] = jnp.where(row == 0, top, total)


def combine_kernel(parts_ref, out_ref):
    count = parts_ref.shape[0]
    tops = [parts_ref[i, HD : HD + 1, :] for i in range(count)]
    top = tops[0]
    for i in range(1, count):
        top = jnp.maximum(top, tops[i])
    total = jnp.zeros_like(top)
    accum = jnp.zeros((HD, parts_ref.shape[2]), jnp.float32)
    for i in range(count):
        share = jnp.exp(tops[i] - top)
        total = total + parts_ref[i, HD + 1 : HD + 2, :] * share
        accum = accum + parts_ref[i, :HD, :] * share
    result = accum / total
    for a in range(2):
        left = result[:, 2 * a * BLK : (2 * a + 1) * BLK]
        right = result[:, (2 * a + 1) * BLK : (2 * a + 2) * BLK]
        out_ref[a * BLK : (a + 1) * BLK, :] = jnp.concatenate([left, right], axis=0).T.astype(jnp.bfloat16)


def body(hidden, merge_weight, query_weight, key_weight, value_weight, block_order):
    tokens, features = hidden.shape[1:]
    n_x, n_seg = lax.axis_size("x"), lax.axis_size(SEG)
    n_ctx = lax.axis_size(CTX)
    x_id, core, ctx_id = lax.axis_index("x"), lax.axis_index("core"), lax.axis_index(CTX)
    chunk = features // n_seg
    smem = pl.BlockSpec(memory_space=pltpu.SMEM)
    place = jnp.stack([core, x_id]).astype(jnp.int32)

    packed = pl.pallas_call(
        pack_kernel,
        out_shape=jax.ShapeDtypeStruct((query_weight.shape[0], 4 * HD), jnp.bfloat16),
        in_specs=[VMEM] * 3,
        out_specs=VMEM,
        name="pack",
    )(query_weight, key_weight.T, value_weight.T)
    weights = lax.all_gather(packed, "yh", axis=0)
    weights = lax.all_gather(weights, "z", axis=0)
    weights = weights.reshape(n_ctx, *weights.shape[2:])

    turned = hidden[0].T
    split = (features // 2 + 15) // 16 * 16
    low = lax.all_gather(turned[:split], SEG, axis=0)
    high = lax.all_gather(turned[split:], SEG, axis=0)

    padded = (chunk + 7) // 8 * 8
    partial, embed = pl.pallas_call(
        merge_kernel,
        out_shape=(
            jax.ShapeDtypeStruct((n_x, chunk, tokens), jnp.float32),
            jax.ShapeDtypeStruct((2 * n_x, padded, tokens), jnp.bfloat16),
        ),
        in_specs=[VMEM] * 3 + [smem],
        out_specs=(VMEM, VMEM),
        scratch_shapes=[pltpu.VMEM((features, tokens), jnp.float32)],
        compiler_params=pltpu.CompilerParams(vmem_limit_bytes=40 << 20),
        name="merge",
    )(low, high, merge_weight, place)
    parts = lax.all_to_all(partial, "x", 0, 0)
    merged = pl.pallas_call(
        settle_kernel,
        out_shape=jax.ShapeDtypeStruct((padded, tokens), jnp.bfloat16),
        in_specs=[VMEM],
        out_specs=VMEM,
        name="settle",
    )(parts)
    merged = lax.all_gather(merged, "yl", axis=0)
    merged = pl.pallas_call(
        spread_kernel,
        out_shape=jax.ShapeDtypeStruct((2 * n_x, padded, tokens), jnp.bfloat16),
        in_specs=[VMEM],
        out_specs=VMEM,
        name="spread",
    )(merged)

    def over_x(copies):
        own = lax.all_to_all(copies, "x", 0, 0, tiled=True)
        return own, lax.ppermute(own, "core", [(0, 1), (1, 0)])

    embed_own, embed_other = over_x(embed)
    merged_own, merged_other = over_x(merged)

    quarter = tokens // n_x
    query, sent = pl.pallas_call(
        project_kernel,
        out_shape=(
            jax.ShapeDtypeStruct((2 * HD, tokens), jnp.bfloat16),
            jax.ShapeDtypeStruct((n_ctx, quarter, 2 * HD), jnp.bfloat16),
        ),
        in_specs=[VMEM] * 5 + [smem],
        out_specs=(VMEM, VMEM),
        compiler_params=pltpu.CompilerParams(vmem_limit_bytes=40 << 20),
        name="project",
    )(embed_own, embed_other, merged_own, merged_other, weights, place)

    queries = lax.all_gather(query, "x", axis=0)
    taken = lax.all_to_all(sent, ("yh", "z"), 0, 0)

    n_z, n_yh = lax.axis_size("z"), lax.axis_size("yh")
    placed = block_order.reshape(n_z, n_yh, 2).transpose(2, 1, 0).reshape(2, n_ctx)
    placed = jnp.where(x_id < n_x // 2, placed[0], placed[1])
    mine = lax.dynamic_slice_in_dim(block_order, ctx_id * 2, 2, 0)
    bias = jnp.where(placed[:, None] < jnp.repeat(mine, 2 * BLK)[None, :], 0.0, -1e30).astype(jnp.float32)

    parts = pl.pallas_call(
        attend_kernel,
        out_shape=jax.ShapeDtypeStruct((n_x, HD + 8, 4 * BLK), jnp.float32),
        in_specs=[VMEM] * 4 + [smem],
        out_specs=VMEM,
        compiler_params=pltpu.CompilerParams(vmem_limit_bytes=40 << 20),
        name="attend",
    )(queries, sent, taken, bias, place)
    parts = lax.all_to_all(parts, "x", 0, 0)
    return pl.pallas_call(
        combine_kernel,
        out_shape=jax.ShapeDtypeStruct((tokens, 2 * HD), jnp.bfloat16),
        in_specs=[VMEM],
        out_specs=VMEM,
        name="combine",
    )(parts)


def solution(mesh):
    shape = mesh.shape
    grid = mesh.devices.reshape(2, shape["segment"] // 2, shape["ctx"] // 2, 2, shape["head"])
    fine = Mesh(grid, ("yl", "core", "z", "yh", "x"))
    return jax.shard_map(
        body,
        mesh=fine,
        in_specs=(
            P(SEG, CTX, "x"),
            P(None, "x", SEG),
            P(CTX, (*SEG, "x")),
            P(CTX, SEG),
            P(CTX, SEG),
            P(),
        ),
        out_specs=P(CTX, (*SEG, "x")),
        check_vma=False,
    )
```

time: 219 us -> 175 us (0.80)
  the two profiles are of different devices: /device:TPU:8 before, /device:TPU:32 now
where the time goes in v2:
time: 175 us; the launch traced here: 174 us
  blocking collectives  71.7 us (41%)
  waiting for transfers between devices  38.7 us (22%)
  starting transfers between devices  21.8 us (12%)
  Pallas kernels  21.7 us (12%)
  between operations  13.5 us (8%)
  local copies, waits for them, and re-layouts  6.18 us (4%)
    all_to_all x1, waiting for transfers between devices, body(): taken = lax.all_to_all(sent, ('yh', 'z'), 0, 0)  20 us
    all_to_all x1, blocking collectives, body(): parts = lax.all_to_all(partial, 'x', 0, 0)  16.6 us
    all_gather x1, blocking collectives, body(): queries = lax.all_gather(query, 'x', axis=0)  12.9 us
    all_to_all x1, blocking collectives, body(): parts = lax.all_to_all(parts, 'x', 0, 0)  11.5 us
    all_to_all x1, starting transfers between devices, body(): taken = lax.all_to_all(sent, ('yh', 'z'), 0, 0)  10.8 us
    all_to_all x2, waiting for transfers between devices, over_x(): own = lax.all_to_all(copies, 'x', 0, 0, tiled=True)  9.49 us
    pallas_call x1, Pallas kernels, body(): pl.pallas_call(attend_kernel, out_shape=jax.ShapeDtypeStruct((n_x, HD + 8...  8.82 us
    all_gather x1, blocking collectives, body(): low = lax.all_gather(turned[:split], SEG, axis=0)  8.53 us
  transfers between devices with their start and end apart: 6, of which 5 were waited for; matrix products, arithmetic and copies ran while one was open for 1% of the time, Pallas kernels for 4%

profile of v2, /device:TPU:32, one launch (start us, length us, event | category | flops | bytes accessed | tf_op | source)
XLA Modules:
  0.0 173.8 jit_solution(7730824957452555709)
XLA Ops:
  6.5 0.0 all-gather.9.cloned.1.call-start
  6.5 1.5 pack.1
  8.1 8.3 %all-gather.6 = bf16[2,180,256]{2,1,0:T(8,128)(2,1)} all-gather(bf16[1,180,256]{2,1,0:T(8,128)(2,1)} %bitcast.20), channel_id=5, replica_groups=mesh['yl'=2,'core'=2,'z'=16,'yh'=2,'x'=4] {'yh'}, dimensions={0}, use_global_device_ids=true | all-gather | bytes 276480 | tf_op jit(solution)/shard_map/all_gather | solution.py:169
  16.4 0.0 all-gather.9.cloned.1.call-update
  16.4 0.9 slice.18
  17.4 0.9 slice.19
  18.3 0.1 pad_add_fusion.place_ref
  18.4 7.4 %all-gather.1 = bf16[1408,256]{1,0:T(8,128)(2,1)S(1)} all-gather(bf16[352,256]{1,0:T(8,128)(2,1)S(1)} %slice.19), channel_id=3, replica_groups=mesh['yl'=2,'core'=2,'z'=16,'yh'=2,'x'=4] {'yl','core'}, dimensions={0}, use_global_device_ids=true | all-gather | bytes 901120 | tf_op jit(solution)/shard_map/all_gather | solution.py:176
  25.8 8.5 %all-gather = bf16[1472,256]{1,0:T(8,128)(2,1)S(1)} all-gather(bf16[368,256]{1,0:T(8,128)(2,1)S(1)} %slice.18), channel_id=2, replica_groups=mesh['yl'=2,'core'=2,'z'=16,'yh'=2,'x'=4] {'yl','core'}, dimensions={0}, use_global_device_ids=true | all-gather | bytes 942080 | tf_op jit(solution)/shard_map/all_gather | solution.py:175
  34.3 0.0 copy-start
  34.3 2.0 %copy-done = bf16[3,720,720]{2,1,0:T(8,128)(2,1)S(1)} copy-done((bf16[3,720,720]{2,1,0:T(8,128)(2,1)S(1)}, bf16[3,720,720]{2,1,0:T(8,128)(2,1)}, u32[]{:S(2)}) %copy-start) | copy-done | bytes 3110424
  36.3 2.7 %merge.1 = (f32[4,180,256]{2,1,0:T(8,128)S(1)}, bf16[8,184,256]{2,1,0:T(8,128)(2,1)}) custom-call(bf16[4,368,256]{2,1,0:T(8,128)(2,1)S(1)} %bitcast.16, bf16[4,352,256]{2,1,0:T(8,128)(2,1)S(1)} %bitcast.17, bf16[3,720,720]{2,1,0:T(8,128)(2,1)S(1)} %copy-done, s32[2]{0:T(128)S(1)} %pad_add_fusion.place_ref), custom_call_target="tpu_custom_call" | custom-call | tf_op jit(solution)/shard_map/merge/pallas_call | solution.py:179
  39.1 16.6 %all_to_all.25.parts_ref = f32[4,180,256]{2,1,0:T(8,128)} all-to-all(f32[4,180,256]{2,1,0:T(8,128)S(1)} %get-tuple-element.10), channel_id=1, replica_groups=mesh['yl'=2,'core'=2,'z'=16,'yh'=2,'x'=4] {'x'}, dimensions={0} | all-to-all | bytes 1474560 | tf_op jit(solution)/shard_map/all_to_all | solution.py:191
  55.7 3.5 %all-to-all-start = ((bf16[8,184,256]{2,1,0:T(8,128)(2,1)}), bf16[8,184,256]{2,1,0:T(8,128)(2,1)S(1)}, u32[]{:S(2)}, u32[]{:S(2)}) async-start(bf16[8,184,256]{2,1,0:T(8,128)(2,1)} %get-tuple-element.9), calls=%async_computation | async-start | bytes 1507328 | tf_op jit(solution)/shard_map/all_to_all | solution.py:209
  59.2 1.8 %settle.1 = bf16[184,256]{1,0:T(8,128)(2,1)} custom-call(f32[4,180,256]{2,1,0:T(8,128)} %all_to_all.25.parts_ref), custom_call_target="tpu_custom_call" | custom-call | tf_op jit(solution)/shard_map/settle/pallas_call | solution.py:192
  61.0 6.4 %all-gather.2 = bf16[368,256]{1,0:T(8,128)(2,1)} all-gather(bf16[184,256]{1,0:T(8,128)(2,1)} %settle.1), channel_id=4, replica_groups=mesh['yl'=2,'core'=2,'z'=16,'yh'=2,'x'=4] {'yl'}, dimensions={0}, use_global_device_ids=true | all-gather | bytes 282624 | tf_op jit(solution)/shard_map/all_gather | solution.py:199
  67.4 1.8 %spread.1 = bf16[8,184,256]{2,1,0:T(8,128)(2,1)} custom-call(bf16[2,184,256]{2,1,0:T(8,128)(2,1)} %bitcast.19), custom_call_target="tpu_custom_call" | custom-call | tf_op jit(solution)/shard_map/spread/pallas_call | solution.py:200
  69.2 1.3 all-to-all-done.embed_own
  70.5 0.0 copy-start.2
  70.5 3.6 %all-to-all-start.2 = ((bf16[8,184,256]{2,1,0:T(8,128)(2,1)}), bf16[8,184,256]{2,1,0:T(8,128)(2,1)S(1)}, u32[]{:S(2)}, u32[]{:S(2)}) async-start(bf16[8,184,256]{2,1,0:T(8,128)(2,1)} %spread.1), calls=%async_computation.2 | async-start | bytes 1507328 | tf_op jit(solution)/shard_map/all_to_all | solution.py:209
  74.1 1.9 %collective-permute-start = (bf16[8,184,256]{2,1,0:T(8,128)(2,1)S(1)}, bf16[8,184,256]{2,1,0:T(8,128)(2,1)S(1)}, u32[]{:S(2)}, u32[]{:S(2)}) collective-permute-start(bf16[8,184,256]{2,1,0:T(8,128)(2,1)S(1)} %all-to-all-done.embed_own), channel_id=1, source_target_pairs={{0,128},{128,0},{1,129},{129,1},{2,130},{130,2},{3,131},{131,3},{4... | collective-permute-start | bytes 2261000 | tf_op jit(solution)/shard_map/ppermute | solution.py:210
  76.1 8.2 %all-to-all-done.2.merged_own = bf16[8,184,256]{2,1,0:T(8,128)(2,1)S(1)} async-done(((bf16[8,184,256]{2,1,0:T(8,128)(2,1)}), bf16[8,184,256]{2,1,0:T(8,128)(2,1)S(1)}, u32[]{:S(2)}, u32[]{:S(2)}) %all-to-all-start.2) | async-done | bytes 753696 | tf_op jit(solution)/shard_map/all_to_all | solution.py:209
  84.3 1.9 %collective-permute-start.1 = (bf16[8,184,256]{2,1,0:T(8,128)(2,1)S(1)}, bf16[8,184,256]{2,1,0:T(8,128)(2,1)S(1)}, u32[]{:S(2)}, u32[]{:S(2)}) collective-permute-start(bf16[8,184,256]{2,1,0:T(8,128)(2,1)S(1)} %all-to-all-done.2.merged_own), channel_id=1, source_target_pairs={{0,128},{128,0},{1,129},{129,1},{2,130},{130,2},{3,131},{131,3},{4... | collective-permute-start | bytes 2261000 | tf_op jit(solution)/shard_map/ppermute | solution.py:210
  86.2 0.0 collective-permute-done.embed_other
  86.2 2.2 %collective-permute-done.1.merged_other = bf16[8,184,256]{2,1,0:T(8,128)(2,1)S(1)} collective-permute-done((bf16[8,184,256]{2,1,0:T(8,128)(2,1)S(1)}, bf16[8,184,256]{2,1,0:T(8,128)(2,1)S(1)}, u32[]{:S(2)}, u32[]{:S(2)}) %collective-permute-start.1) | collective-permute-done | bytes 753696 | tf_op jit(solution)/shard_map/ppermute | solution.py:210
  88.4 7.0 %all-gather.9.cloned.1.call-done.weights_ref = bf16[32,180,256]{2,1,0:T(8,128)(2,1)} async-done(((bf16[2,180,256]{2,1,0:T(8,128)(2,1)}), bf16[32,180,256]{2,1,0:T(8,128)(2,1)}) %all-gather.9.cloned.1.call-update) | async-done | bytes 2949136 | tf_op jit(solution)/shard_map/all_gather | solution.py:170
  95.4 0.0 copy-start.1
  95.4 1.9 %copy-done.1 = bf16[32,180,256]{2,1,0:T(8,128)(2,1)S(1)} copy-done((bf16[32,180,256]{2,1,0:T(8,128)(2,1)S(1)}, bf16[32,180,256]{2,1,0:T(8,128)(2,1)}, u32[]{:S(2)}) %copy-start.1) | copy-done | bytes 2949144
  97.2 3.2 %project.1 = (bf16[128,256]{1,0:T(8,128)(2,1)S(1)}, bf16[32,64,128]{2,1,0:T(8,128)(2,1)}) custom-call(bf16[8,184,256]{2,1,0:T(8,128)(2,1)S(1)} %all-to-all-done.embed_own, bf16[8,184,256]{2,1,0:T(8,128)(2,1)S(1)} %collective-permute-done.embed_other, bf16[8,184,256]{2,1,0:T(8,128)(2,1)S(1)} %all-to-all-done.2.merged_own, ...), custom_call_target="tpu_custom_call" | custom-call | tf_op jit(solution)/shard_map/project/pallas_call | solution.py:216
  100.4 10.8 %all-to-all-start.3 = ((bf16[32,64,128]{2,1,0:T(8,128)(2,1)}), bf16[32,64,128]{2,1,0:T(8,128)(2,1)S(1)}, u32[]{:S(2)}, u32[]{:S(2)}) async-start(bf16[32,64,128]{2,1,0:T(8,128)(2,1)} %get-tuple-element.12.sent_ref), calls=%async_computation.3 | async-start | bytes 1048576 | tf_op jit(solution)/shard_map/all_to_all | solution.py:229
  111.2 0.0 copy-done.2
  111.2 0.1 reshape.24
  111.3 0.1 dynamic_slice.3
  111.4 0.1 broadcast_bitcast_fusion
  111.5 0.1 slice_select_fusion
  111.6 0.1 copy.9
  111.7 0.1 select_n.24
  111.8 0.1 compare_select_fusion.bias_ref
  111.8 12.9 %all-gather.5 = bf16[512,256]{1,0:T(8,128)(2,1)S(1)} all-gather(bf16[128,256]{1,0:T(8,128)(2,1)S(1)} %get-tuple-element.11), channel_id=7, replica_groups=mesh['yl'=2,'core'=2,'z'=16,'yh'=2,'x'=4] {'x'}, dimensions={0}, use_global_device_ids=true | all-gather | bytes 327680 | tf_op jit(solution)/shard_map/all_gather | solution.py:228
  124.7 20.0 %all-to-all-done.3.all_ref = bf16[32,64,128]{2,1,0:T(8,128)(2,1)S(1)} async-done(((bf16[32,64,128]{2,1,0:T(8,128)(2,1)}), bf16[32,64,128]{2,1,0:T(8,128)(2,1)S(1)}, u32[]{:S(2)}, u32[]{:S(2)}) %all-to-all-start.3) | async-done | bytes 524320 | tf_op jit(solution)/shard_map/all_to_all | solution.py:229
  144.8 8.8 %attend.1 = f32[4,72,512]{2,1,0:T(8,128)S(1)} custom-call(bf16[4,128,256]{2,1,0:T(8,128)(2,1)S(1)} %bitcast.18, bf16[32,64,128]{2,1,0:T(8,128)(2,1)} %get-tuple-element.12.sent_ref, bf16[32,64,128]{2,1,0:T(8,128)(2,1)S(1)} %all-to-all-done.3.all_ref, f32[32,512]{1,0:T(8,128)S(1)} %compare_select_fusion.bias_ref, s32[2]{0:T(128)S(1)} %pad_add_fusion.place_ref), custom_call_target="tpu_custom_call" | custom-call | tf_op jit(solution)/shard_map/attend/pallas_call | solution.py:237
  153.6 11.5 %all_to_all.26.parts_ref = f32[4,72,512]{2,1,0:T(8,128)} all-to-all(f32[4,72,512]{2,1,0:T(8,128)S(1)} %attend.1), channel_id=1, replica_groups=mesh['yl'=2,'core'=2,'z'=16,'yh'=2,'x'=4] {'x'}, dimensions={0} | all-to-all | bytes 1179648 | tf_op jit(solution)/shard_map/all_to_all | solution.py:245
  165.1 1.8 %combine.1 = bf16[256,128]{1,0:T(8,128)(2,1)} custom-call(f32[4,72,512]{2,1,0:T(8,128)} %all_to_all.26.parts_ref), custom_call_target="tpu_custom_call" | custom-call | tf_op jit(solution)/shard_map/combine/pallas_call | solution.py:246
  (1 shorter events, 0.0 us)
Async XLA Ops:
  6.5 88.8 %all-gather.9.cloned.1.call-start = ((), (), s32[]{:S(2)}) async-start(), calls=%async_computation.5 | async-start | bytes 3203072 | tf_op jit(solution)/shard_map/all_gather | solution.py:170
  34.3 2.0 %copy-start = (bf16[3,720,720]{2,1,0:T(8,128)(2,1)S(1)}, bf16[3,720,720]{2,1,0:T(8,128)(2,1)}, u32[]{:S(2)}) copy-start(bf16[3,720,720]{2,1,0:T(8,128)(2,1)} %weight_ref.1) | copy-start | bytes 9331204
  55.7 14.8 %all-to-all-start = ((bf16[8,184,256]{2,1,0:T(8,128)(2,1)}), bf16[8,184,256]{2,1,0:T(8,128)(2,1)S(1)}, u32[]{:S(2)}, u32[]{:S(2)}) async-start(bf16[8,184,256]{2,1,0:T(8,128)(2,1)} %get-tuple-element.9), calls=%async_computation | async-start | bytes 1507328 | tf_op jit(solution)/shard_map/all_to_all | solution.py:209
  70.5 40.7 %copy-start.2 = (s32[64]{0:T(128)S(1)}, s32[64]{0:T(128)}, u32[]{:S(2)}) copy-start(s32[64]{0:T(128)} %param.11) | copy-start | bytes 772
  70.5 13.8 %all-to-all-start.2 = ((bf16[8,184,256]{2,1,0:T(8,128)(2,1)}), bf16[8,184,256]{2,1,0:T(8,128)(2,1)S(1)}, u32[]{:S(2)}, u32[]{:S(2)}) async-start(bf16[8,184,256]{2,1,0:T(8,128)(2,1)} %spread.1), calls=%async_computation.2 | async-start | bytes 1507328 | tf_op jit(solution)/shard_map/all_to_all | solution.py:209
  74.1 12.1 %collective-permute-start = (bf16[8,184,256]{2,1,0:T(8,128)(2,1)S(1)}, bf16[8,184,256]{2,1,0:T(8,128)(2,1)S(1)}, u32[]{:S(2)}, u32[]{:S(2)}) collective-permute-start(bf16[8,184,256]{2,1,0:T(8,128)(2,1)S(1)} %all-to-all-done.embed_own), channel_id=1, source_target_pairs={{0,128},{128,0},{1,129},{129,1},{2,130},{130,2},{3,131},{131,3},{4... | collective-permute-start | bytes 2261000 | tf_op jit(solution)/shard_map/ppermute | solution.py:210
  84.3 4.1 %collective-permute-start.1 = (bf16[8,184,256]{2,1,0:T(8,128)(2,1)S(1)}, bf16[8,184,256]{2,1,0:T(8,128)(2,1)S(1)}, u32[]{:S(2)}, u32[]{:S(2)}) collective-permute-start(bf16[8,184,256]{2,1,0:T(8,128)(2,1)S(1)} %all-to-all-done.2.merged_own), channel_id=1, source_target_pairs={{0,128},{128,0},{1,129},{129,1},{2,130},{130,2},{3,131},{131,3},{4... | collective-permute-start | bytes 2261000 | tf_op jit(solution)/shard_map/ppermute | solution.py:210
  95.4 1.9 %copy-start.1 = (bf16[32,180,256]{2,1,0:T(8,128)(2,1)S(1)}, bf16[32,180,256]{2,1,0:T(8,128)(2,1)}, u32[]{:S(2)}) copy-start(bf16[32,180,256]{2,1,0:T(8,128)(2,1)} %all-gather.9.cloned.1.call-done.weights_ref) | copy-start | bytes 8847364
  100.4 44.4 %all-to-all-start.3 = ((bf16[32,64,128]{2,1,0:T(8,128)(2,1)}), bf16[32,64,128]{2,1,0:T(8,128)(2,1)S(1)}, u32[]{:S(2)}, u32[]{:S(2)}) async-start(bf16[32,64,128]{2,1,0:T(8,128)(2,1)} %get-tuple-element.12.sent_ref), calls=%async_computation.3 | async-start | bytes 1048576 | tf_op jit(solution)/shard_map/all_to_all | solution.py:229
Sparse Core Ops, SparseCore 0:
  16.6 78.7 all-gather.8

commit v3 on v2

--- a/solution.py
+++ b/solution.py
@@ -54,16 +54,13 @@
         out_ref[i * count : (i + 1) * count] = block_ref[...]
 
 
-def project_kernel(
-    embed_own, embed_other, merged_own, merged_other, weights_ref, place_ref, query_ref, sent_ref
-):
-    core, x_id = place_ref[0], place_ref[1]
-    chunks, _, tokens = embed_own.shape
-    chunk = weights_ref.shape[1]
+def norm_kernel(embed_own, embed_other, merged_own, merged_other, place_ref, out_ref):
+    core = place_ref[0]
+    chunks = embed_own.shape[0]
+    chunk = out_ref.shape[1]
     width = 2 * chunks * chunk
-    acc = jnp.zeros((weights_ref.shape[2], tokens), jnp.float32)
     for kind, pair in enumerate(((embed_own, embed_other), (merged_own, merged_other))):
-        total = jnp.zeros((1, tokens), jnp.float32)
+        total = jnp.zeros((1, out_ref.shape[2]), jnp.float32)
         for ref in pair:
             for i in range(chunks):
                 part = ref[i, :chunk].astype(jnp.float32)
@@ -75,8 +72,31 @@
                     at = i // 2 * 4 + 2 * side + i % 2
                 else:
                     at = 2 * chunks + (2 * (i % 2) + side) * 4 + i // 2
-                normed = (ref[i, :chunk].astype(jnp.float32) * scale).astype(jnp.bfloat16)
-                acc = acc + lax.dot_general(weights_ref[at], normed, DIM0, preferred_element_type=jnp.float32)
+                out_ref[at] = (ref[i, :chunk].astype(jnp.float32) * scale).astype(jnp.bfloat16)
+
+
+def project_kernel(
+    rows_hbm, weights_hbm, place_ref, query_ref, sent_ref, own_ref, rows_ref, weights_ref, arrived
+):
+    x_id = place_ref[1]
+    pieces = arrived.shape[1]
+    count = weights_ref.shape[0] // pieces
+    copies = []
+    for p in range(pieces):
+        span = pl.ds(p * count, count)
+        both = ((rows_hbm, rows_ref), (weights_hbm, weights_ref))
+        copies.append(
+            [pltpu.make_async_copy(src.at[span], dst.at[span], arrived.at[k, p]) for k, (src, dst) in enumerate(both)]
+        )
+        for copy in copies[-1]:
+            copy.start()
+    tokens = rows_ref.shape[2]
+    acc = jnp.zeros((weights_ref.shape[2], tokens), jnp.float32)
+    for p in range(pieces):
+        for copy in copies[p]:
+            copy.wait()
+        for at in range(p * count, (p + 1) * count):
+            acc = acc + lax.dot_general(weights_ref[at], rows_ref[at], DIM0, preferred_element_type=jnp.float32)
     half = acc.shape[0] // 2
     query_ref[...] = acc[:half].astype(jnp.bfloat16)
     rows = acc[half:].T.astype(jnp.bfloat16)
@@ -86,49 +106,69 @@
         quarter = jnp.where(x_id == i, rows[i * size : (i + 1) * size], quarter)
     for i in range(sent_ref.shape[0]):
         sent_ref[i] = quarter
-
-
-def attend_kernel(query_ref, sent_ref, all_ref, bias_ref, place_ref, out_ref):
+    own_ref[...] = quarter
+
+
+def heads_of(query_ref, source):
+    zeros = jnp.zeros((HD, BLK), jnp.bfloat16)
+    pieces = []
+    for a in range(2):
+        for g in range(2):
+            piece = query_ref[source, g * HD : (g + 1) * HD, a * BLK : (a + 1) * BLK]
+            pieces.append(jnp.concatenate([piece * jnp.bfloat16(0.125), zeros], axis=0))
+    return jnp.concatenate(pieces, axis=1)
+
+
+def attend_keys(queries, keys_ref, bias_ref, state):
+    top, total, accum = state
+    groups, chunk, _ = keys_ref.shape
+    keys = keys_ref[...].reshape(groups * chunk, 2 * HD)
+    bias = bias_ref[...]
+    scores = jnp.dot(keys, queries, preferred_element_type=jnp.float32)
+    scores = scores.reshape(groups, chunk, queries.shape[1])
+    highest = jnp.max(scores, axis=1) + bias
+    new_top = jnp.maximum(top, jnp.max(highest, axis=0, keepdims=True))
+    weights = jnp.exp(scores + (bias - new_top)[:, None, :])
+    rescale = jnp.exp(top - new_top)
+    weights = weights.reshape(groups * chunk, queries.shape[1])
+    total = total * rescale + jnp.sum(weights, axis=0, keepdims=True)
+    mixed = lax.dot_general(keys, weights.astype(jnp.bfloat16), DIM0, preferred_element_type=jnp.float32)
+    return new_top, total, accum * rescale + mixed[HD:]
+
+
+def store_state(out_ref, source, state):
+    top, total, accum = state
+    out_ref[source, :HD] = accum
+    row = lax.broadcasted_iota(jnp.int32, (8, accum.shape[1]), 0)
+    out_ref[source, HD:] = jnp.where(row == 0, top, total)
+
+
+def first_kernel(query_ref, own_ref, keys_ref, bias_ref, place_ref, out_ref):
     x_id = place_ref[1]
-    own = sent_ref[0]
-    groups, chunk, _ = all_ref.shape
-    zeros = jnp.zeros((HD, BLK), jnp.bfloat16)
-    lanes = 4 * BLK
+    own = own_ref[...]
+    chunk = own.shape[0]
+    lanes = out_ref.shape[2]
     key_row = lax.broadcasted_iota(jnp.int32, (chunk, lanes), 0) + (x_id % 2) * chunk
     lane = lax.broadcasted_iota(jnp.int32, (chunk, lanes), 1)
     own_bias = jnp.where((lane // (2 * BLK) == x_id // 2) & (key_row <= lane % BLK), 0.0, -1e30)
-    step = 16
     for source in range(query_ref.shape[0]):
-        pieces = []
-        for a in range(2):
-            for g in range(2):
-                piece = query_ref[source, g * HD : (g + 1) * HD, a * BLK : (a + 1) * BLK]
-                pieces.append(jnp.concatenate([piece * jnp.bfloat16(0.125), zeros], axis=0))
-        queries = jnp.concatenate(pieces, axis=1)
+        queries = heads_of(query_ref, source)
         scores = jnp.dot(own, queries, preferred_element_type=jnp.float32) + own_bias
         top = jnp.maximum(jnp.max(scores, axis=0, keepdims=True), -1e20)
         weights = jnp.exp(scores - top)
         total = jnp.sum(weights, axis=0, keepdims=True)
         accum = lax.dot_general(own, weights.astype(jnp.bfloat16), DIM0, preferred_element_type=jnp.float32)
-        for first in range(0, groups, step):
-            keys = all_ref[first : first + step].reshape(step * chunk, 2 * HD)
-            bias = bias_ref[first : first + step, :]
-            scores = jnp.dot(keys, queries, preferred_element_type=jnp.float32)
-            scores = scores.reshape(step, chunk, lanes)
-            highest = jnp.max(scores, axis=1) + bias
-            new_top = jnp.maximum(top, jnp.max(highest, axis=0, keepdims=True))
-            weights = jnp.exp(scores + (bias - new_top)[:, None, :])
-            rescale = jnp.exp(top - new_top)
-            weights = weights.reshape(step * chunk, lanes)
-            total = total * rescale + jnp.sum(weights, axis=0, keepdims=True)
-            mixed = lax.dot_general(
-                keys, weights.astype(jnp.bfloat16), DIM0, preferred_element_type=jnp.float32
-            )
-            accum = accum * rescale + mixed
-            top = new_top
-        out_ref[source, :HD] = accum[HD:]
-        row = lax.broadcasted_iota(jnp.int32, (8, lanes), 0)
-        out_ref[source, HD:] = jnp.where(row == 0, top, total)
+        store_state(out_ref, source, attend_keys(queries, keys_ref, bias_ref, (top, total, accum[HD:])))
+
+
+def second_kernel(query_ref, keys_ref, bias_ref, state_ref, out_ref):
+    for source in range(query_ref.shape[0]):
+        state = (
+            state_ref[source, HD : HD + 1, :],
+            state_ref[source, HD + 1 : HD + 2, :],
+            state_ref[source, :HD, :],
+        )
+        store_state(out_ref, source, attend_keys(heads_of(query_ref, source), keys_ref, bias_ref, state))
 
 
 def combine_kernel(parts_ref, out_ref):
@@ -156,7 +196,7 @@
     n_ctx = lax.axis_size(CTX)
     x_id, core, ctx_id = lax.axis_index("x"), lax.axis_index("core"), lax.axis_index(CTX)
     chunk = features // n_seg
-    smem = pl.BlockSpec(memory_space=pltpu.SMEM)
+    smem, hbm = pl.BlockSpec(memory_space=pltpu.SMEM), pl.BlockSpec(memory_space=pltpu.HBM)
     place = jnp.stack([core, x_id]).astype(jnp.int32)
 
     packed = pl.pallas_call(
@@ -213,35 +253,68 @@
     merged_own, merged_other = over_x(merged)
 
     quarter = tokens // n_x
-    query, sent = pl.pallas_call(
+    params = pltpu.CompilerParams(vmem_limit_bytes=40 << 20)
+    rows = pl.pallas_call(
+        norm_kernel,
+        out_shape=jax.ShapeDtypeStruct((n_ctx, chunk, tokens), jnp.bfloat16),
+        in_specs=[VMEM] * 4 + [smem],
+        out_specs=VMEM,
+        compiler_params=params,
+        name="norm",
+    )(embed_own, embed_other, merged_own, merged_other, place)
+    n_z, n_yh = lax.axis_size("z"), lax.axis_size("yh")
+    query, sent, own = pl.pallas_call(
         project_kernel,
         out_shape=(
             jax.ShapeDtypeStruct((2 * HD, tokens), jnp.bfloat16),
-            jax.ShapeDtypeStruct((n_ctx, quarter, 2 * HD), jnp.bfloat16),
+            jax.ShapeDtypeStruct((n_z, quarter, 2 * HD), jnp.bfloat16),
+            jax.ShapeDtypeStruct((quarter, 2 * HD), jnp.bfloat16),
         ),
-        in_specs=[VMEM] * 5 + [smem],
-        out_specs=(VMEM, VMEM),
-        compiler_params=pltpu.CompilerParams(vmem_limit_bytes=40 << 20),
+        in_specs=[hbm, hbm, smem],
+        out_specs=(VMEM, VMEM, VMEM),
+        scratch_shapes=[
+            pltpu.VMEM(rows.shape, rows.dtype),
+            pltpu.VMEM(weights.shape, weights.dtype),
+            pltpu.SemaphoreType.DMA((2, 4)),
+        ],
+        compiler_params=pltpu.CompilerParams(vmem_limit_bytes=60 << 20),
         name="project",
-    )(embed_own, embed_other, merged_own, merged_other, weights, place)
-
+    )(rows, weights, place)
+
+    taken = lax.all_to_all(sent, "z", 0, 0)
     queries = lax.all_gather(query, "x", axis=0)
-    taken = lax.all_to_all(sent, ("yh", "z"), 0, 0)
-
-    n_z, n_yh = lax.axis_size("z"), lax.axis_size("yh")
-    placed = block_order.reshape(n_z, n_yh, 2).transpose(2, 1, 0).reshape(2, n_ctx)
-    placed = jnp.where(x_id < n_x // 2, placed[0], placed[1])
-    mine = lax.dynamic_slice_in_dim(block_order, ctx_id * 2, 2, 0)
-    bias = jnp.where(placed[:, None] < jnp.repeat(mine, 2 * BLK)[None, :], 0.0, -1e30).astype(jnp.float32)
-
+    other = lax.ppermute(taken, "yh", [(0, 1), (1, 0)])
+
+    placed = block_order.reshape(n_z, n_yh, 2)
+    placed = jnp.where(x_id < n_x // 2, placed[:, :, 0], placed[:, :, 1])
+    mine = jnp.repeat(lax.dynamic_slice_in_dim(block_order, ctx_id * 2, 2, 0), 2 * BLK)
+    yh = lax.axis_index("yh")
+    near = jnp.where(yh == 0, placed[:, 0], placed[:, 1])
+    far = jnp.where(yh == 0, placed[:, 1], placed[:, 0])
+    near = jnp.where(near[:, None] < mine[None, :], 0.0, -1e30).astype(jnp.float32)
+    far = jnp.where(far[:, None] < mine[None, :], 0.0, -1e30).astype(jnp.float32)
+
+    scores = 8 * BLK * 2 * n_z * quarter
+    state = jax.ShapeDtypeStruct((n_x, HD + 8, 4 * BLK), jnp.float32)
+    cost = pl.CostEstimate(flops=scores * 4 * HD, bytes_accessed=2 << 20, transcendentals=scores)
     parts = pl.pallas_call(
-        attend_kernel,
-        out_shape=jax.ShapeDtypeStruct((n_x, HD + 8, 4 * BLK), jnp.float32),
+        first_kernel,
+        out_shape=state,
         in_specs=[VMEM] * 4 + [smem],
         out_specs=VMEM,
-        compiler_params=pltpu.CompilerParams(vmem_limit_bytes=40 << 20),
-        name="attend",
-    )(queries, sent, taken, bias, place)
+        compiler_params=params,
+        cost_estimate=cost,
+        name="attend_first",
+    )(queries, own, taken, near, place)
+    parts = pl.pallas_call(
+        second_kernel,
+        out_shape=state,
+        in_specs=[VMEM] * 4,
+        out_specs=VMEM,
+        compiler_params=params,
+        cost_estimate=cost,
+        name="attend_second",
+    )(queries, other, far, parts)
     parts = lax.all_to_all(parts, "x", 0, 0)
     return pl.pallas_call(
         combine_kernel,

time: 175 us -> 178 us (1.017)
  waiting for transfers between devices: 38.7 us -> 33.8 us
  starting transfers between devices: 21.8 us -> 26.3 us
  Pallas kernels: 21.7 us -> 25 us
    ppermute x0 -> x1, starting transfers between devices: none -> 4.38 us  [body(): other = lax.ppermute(taken, 'yh', [(0, 1), (1, 0)])]
    all_gather x1, waiting for transfers between devices: 6.95 us -> 4.16 us  [body(): weights = lax.all_gather(weights, 'z', axis=0)]
    pallas_call x1, Pallas kernels: 3.16 us -> 5.55 us  [body(): pl.pallas_call(project_kernel, out_shape=(jax.ShapeDtypeStruct((2 * HD, t...]
    all_to_all x1, waiting for transfers between devices: 20 us -> 17.9 us  [body(): taken = lax.all_to_all(sent, 'z', 0, 0)]
    pallas_call x1 -> x3, Pallas kernels: 8.82 us -> 9.74 us  [the longest x1 4.92 us: body(): pl.pallas_call(first_kernel, out_shape=state, in_specs=[VMEM] * 4 + [smem...]
    unnamed x8 -> x14, local copies, waits for them, and re-layouts: 3.93 us -> 4.44 us
  transfers between devices with their start and end apart: 6 -> 7, of which waited for: 5 -> 5; matrix products, arithmetic and copies ran while one was open for 1% -> 1% of each run, Pallas kernels for 4% -> 7%
where the time goes in v3:
time: 178 us; the launch traced here: 177 us
  blocking collectives  71.6 us (40%)
  waiting for transfers between devices  33.8 us (19%)
  starting transfers between devices  26.3 us (15%)
  Pallas kernels  25 us (14%)
  between operations  13.5 us (8%)
  local copies, waits for them, and re-layouts  6.6 us (4%)
    all_to_all x1, waiting for transfers between devices, body(): taken = lax.all_to_all(sent, 'z', 0, 0)  17.9 us
    all_to_all x1, blocking collectives, body(): parts = lax.all_to_all(partial, 'x', 0, 0)  16.6 us
    all_gather x1, blocking collectives, body(): queries = lax.all_gather(query, 'x', axis=0)  12.8 us
    all_to_all x1, blocking collectives, body(): parts = lax.all_to_all(parts, 'x', 0, 0)  11.5 us
    all_to_all x1, starting transfers between devices, body(): taken = lax.all_to_all(sent, 'z', 0, 0)  11.1 us
    all_to_all x2, waiting for transfers between devices, over_x(): own = lax.all_to_all(copies, 'x', 0, 0, tiled=True)  9.5 us
    all_gather x1, blocking collectives, body(): low = lax.all_gather(turned[:split], SEG, axis=0)  8.53 us
    all_gather x1, blocking collectives, body(): weights = lax.all_gather(packed, 'yh', axis=0)  8.33 us
  transfers between devices with their start and end apart: 7, of which 5 were waited for; matrix products, arithmetic and copies ran while one was open for 1% of the time, Pallas kernels for 7%

profile of v3, /device:TPU:32, one launch (start us, length us, event | category | flops | bytes accessed | tf_op | source)
XLA Modules:
  0.0 177.1 jit_solution(17455635069861657346)
XLA Ops:
  6.5 0.0 all-gather.9.cloned.1.call-start
  6.5 1.6 pack.1
  8.1 8.3 %all-gather.6 = bf16[2,180,256]{2,1,0:T(8,128)(2,1)} all-gather(bf16[1,180,256]{2,1,0:T(8,128)(2,1)} %bitcast.25), channel_id=5, replica_groups=mesh['yl'=2,'core'=2,'z'=16,'yh'=2,'x'=4] {'yh'}, dimensions={0}, use_global_device_ids=true | all-gather | bytes 276480 | tf_op jit(solution)/shard_map/all_gather | solution.py:209
  16.4 0.0 all-gather.9.cloned.1.call-update
  16.5 0.9 slice.26
  17.4 0.9 slice.27
  18.3 0.1 pad_add_fusion.place_ref
  18.4 0.0 copy-start.2
  18.4 7.4 %all-gather.1 = bf16[1408,256]{1,0:T(8,128)(2,1)S(1)} all-gather(bf16[352,256]{1,0:T(8,128)(2,1)S(1)} %slice.27), channel_id=3, replica_groups=mesh['yl'=2,'core'=2,'z'=16,'yh'=2,'x'=4] {'yl','core'}, dimensions={0}, use_global_device_ids=true | all-gather | bytes 901120 | tf_op jit(solution)/shard_map/all_gather | solution.py:216
  25.8 8.5 %all-gather = bf16[1472,256]{1,0:T(8,128)(2,1)S(1)} all-gather(bf16[368,256]{1,0:T(8,128)(2,1)S(1)} %slice.26), channel_id=2, replica_groups=mesh['yl'=2,'core'=2,'z'=16,'yh'=2,'x'=4] {'yl','core'}, dimensions={0}, use_global_device_ids=true | all-gather | bytes 942080 | tf_op jit(solution)/shard_map/all_gather | solution.py:215
  34.4 2.0 %copy-done.1 = bf16[3,720,720]{2,1,0:T(8,128)(2,1)S(1)} copy-done((bf16[3,720,720]{2,1,0:T(8,128)(2,1)S(1)}, bf16[3,720,720]{2,1,0:T(8,128)(2,1)}, u32[]{:S(2)}) %copy-start.1) | copy-done | bytes 3110424
  36.4 2.7 %merge.1 = (f32[4,180,256]{2,1,0:T(8,128)S(1)}, bf16[8,184,256]{2,1,0:T(8,128)(2,1)}) custom-call(bf16[4,368,256]{2,1,0:T(8,128)(2,1)S(1)} %bitcast.20, bf16[4,352,256]{2,1,0:T(8,128)(2,1)S(1)} %bitcast.21, bf16[3,720,720]{2,1,0:T(8,128)(2,1)S(1)} %copy-done.1, s32[2]{0:T(128)S(1)} %pad_add_fusion.place_ref), custom_call_target="tpu_custom_call" | custom-call | tf_op jit(solution)/shard_map/merge/pallas_call | solution.py:219
  39.1 16.6 %all_to_all.25.parts_ref = f32[4,180,256]{2,1,0:T(8,128)} all-to-all(f32[4,180,256]{2,1,0:T(8,128)S(1)} %get-tuple-element.11), channel_id=1, replica_groups=mesh['yl'=2,'core'=2,'z'=16,'yh'=2,'x'=4] {'x'}, dimensions={0} | all-to-all | bytes 1474560 | tf_op jit(solution)/shard_map/all_to_all | solution.py:231
  55.7 3.5 %all-to-all-start = ((bf16[8,184,256]{2,1,0:T(8,128)(2,1)}), bf16[8,184,256]{2,1,0:T(8,128)(2,1)S(1)}, u32[]{:S(2)}, u32[]{:S(2)}) async-start(bf16[8,184,256]{2,1,0:T(8,128)(2,1)} %get-tuple-element.10), calls=%async_computation | async-start | bytes 1507328 | tf_op jit(solution)/shard_map/all_to_all | solution.py:249
  59.2 1.8 %settle.1 = bf16[184,256]{1,0:T(8,128)(2,1)} custom-call(f32[4,180,256]{2,1,0:T(8,128)} %all_to_all.25.parts_ref), custom_call_target="tpu_custom_call" | custom-call | tf_op jit(solution)/shard_map/settle/pallas_call | solution.py:232
  61.0 6.4 %all-gather.2 = bf16[368,256]{1,0:T(8,128)(2,1)} all-gather(bf16[184,256]{1,0:T(8,128)(2,1)} %settle.1), channel_id=4, replica_groups=mesh['yl'=2,'core'=2,'z'=16,'yh'=2,'x'=4] {'yl'}, dimensions={0}, use_global_device_ids=true | all-gather | bytes 282624 | tf_op jit(solution)/shard_map/all_gather | solution.py:239
  67.4 1.9 %spread.1 = bf16[8,184,256]{2,1,0:T(8,128)(2,1)} custom-call(bf16[2,184,256]{2,1,0:T(8,128)(2,1)} %bitcast.24), custom_call_target="tpu_custom_call" | custom-call | tf_op jit(solution)/shard_map/spread/pallas_call | solution.py:240
  69.2 1.3 all-to-all-done.embed_own
  70.5 3.5 %all-to-all-start.2 = ((bf16[8,184,256]{2,1,0:T(8,128)(2,1)}), bf16[8,184,256]{2,1,0:T(8,128)(2,1)S(1)}, u32[]{:S(2)}, u32[]{:S(2)}) async-start(bf16[8,184,256]{2,1,0:T(8,128)(2,1)} %spread.1), calls=%async_computation.2 | async-start | bytes 1507328 | tf_op jit(solution)/shard_map/all_to_all | solution.py:249
  74.0 1.9 %collective-permute-start = (bf16[8,184,256]{2,1,0:T(8,128)(2,1)S(1)}, bf16[8,184,256]{2,1,0:T(8,128)(2,1)S(1)}, u32[]{:S(2)}, u32[]{:S(2)}) collective-permute-start(bf16[8,184,256]{2,1,0:T(8,128)(2,1)S(1)} %all-to-all-done.embed_own), channel_id=1, source_target_pairs={{0,128},{128,0},{1,129},{129,1},{2,130},{130,2},{3,131},{131,3},{4... | collective-permute-start | bytes 2261000 | tf_op jit(solution)/shard_map/ppermute | solution.py:250
  75.9 8.2 %all-to-all-done.2.merged_own = bf16[8,184,256]{2,1,0:T(8,128)(2,1)S(1)} async-done(((bf16[8,184,256]{2,1,0:T(8,128)(2,1)}), bf16[8,184,256]{2,1,0:T(8,128)(2,1)S(1)}, u32[]{:S(2)}, u32[]{:S(2)}) %all-to-all-start.2) | async-done | bytes 753696 | tf_op jit(solution)/shard_map/all_to_all | solution.py:249
  84.2 1.9 %collective-permute-start.1 = (bf16[8,184,256]{2,1,0:T(8,128)(2,1)S(1)}, bf16[8,184,256]{2,1,0:T(8,128)(2,1)S(1)}, u32[]{:S(2)}, u32[]{:S(2)}) collective-permute-start(bf16[8,184,256]{2,1,0:T(8,128)(2,1)S(1)} %all-to-all-done.2.merged_own), channel_id=1, source_target_pairs={{0,128},{128,0},{1,129},{129,1},{2,130},{130,2},{3,131},{131,3},{4... | collective-permute-start | bytes 2261000 | tf_op jit(solution)/shard_map/ppermute | solution.py:250
  86.1 0.0 collective-permute-done.embed_other
  86.1 2.2 %collective-permute-done.1.merged_other = bf16[8,184,256]{2,1,0:T(8,128)(2,1)S(1)} collective-permute-done((bf16[8,184,256]{2,1,0:T(8,128)(2,1)S(1)}, bf16[8,184,256]{2,1,0:T(8,128)(2,1)S(1)}, u32[]{:S(2)}, u32[]{:S(2)}) %collective-permute-start.1) | collective-permute-done | bytes 753696 | tf_op jit(solution)/shard_map/ppermute | solution.py:250
  88.3 0.0 copy-done.2
  88.3 1.3 norm.1.rows_hbm
  89.6 0.0 copy-start
  89.6 1.6 copy-done
  91.2 4.2 %all-gather.9.cloned.1.call-done.weights_hbm = bf16[32,180,256]{2,1,0:T(8,128)(2,1)} async-done(((bf16[2,180,256]{2,1,0:T(8,128)(2,1)}), bf16[32,180,256]{2,1,0:T(8,128)(2,1)}) %all-gather.9.cloned.1.call-update) | async-done | bytes 2949136 | tf_op jit(solution)/shard_map/all_gather | solution.py:210
  95.4 5.5 %project.1 = (bf16[128,256]{1,0:T(8,128)(2,1)}, bf16[16,64,128]{2,1,0:T(8,128)(2,1)}, bf16[64,128]{1,0:T(8,128)(2,1)}) custom-call(bf16[32,180,256]{2,1,0:T(8,128)(2,1)} %copy-done, bf16[32,180,256]{2,1,0:T(8,128)(2,1)} %all-gather.9.cloned.1.call-done.weights_hbm, s32[2]{0:T(128)} %copy-done.2), custom_call_target="tpu_custom_call" | custom-call | tf_op jit(solution)/shard_map/project/pallas_call | solution.py:266
  100.9 11.1 %all-to-all-start.3 = ((bf16[16,64,128]{2,1,0:T(8,128)(2,1)}), bf16[16,64,128]{2,1,0:T(8,128)(2,1)S(1)}, u32[]{:S(2)}, u32[]{:S(2)}) async-start(bf16[16,64,128]{2,1,0:T(8,128)(2,1)} %get-tuple-element.13), calls=%async_computation.3 | async-start | bytes 524288 | tf_op jit(solution)/shard_map/all_to_all | solution.py:284
  112.0 0.0 copy-done.5
  112.0 0.1 reshape.10
  112.1 0.1 dynamic_slice.3
  112.2 0.1 broadcast_bitcast_fusion
  112.3 0.1 slice_select_fusion
  112.4 0.1 copy.9
  112.5 17.9 %all-to-all-done.3.keys_ref = bf16[16,64,128]{2,1,0:T(8,128)(2,1)S(1)} async-done(((bf16[16,64,128]{2,1,0:T(8,128)(2,1)}), bf16[16,64,128]{2,1,0:T(8,128)(2,1)S(1)}, u32[]{:S(2)}, u32[]{:S(2)}) %all-to-all-start.3) | async-done | bytes 262176 | tf_op jit(solution)/shard_map/all_to_all | solution.py:284
  130.4 4.4 %collective-permute-start.2 = (bf16[16,64,128]{2,1,0:T(8,128)(2,1)S(1)}, bf16[16,64,128]{2,1,0:T(8,128)(2,1)S(1)}, u32[]{:S(2)}, u32[]{:S(2)}) collective-permute-start(bf16[16,64,128]{2,1,0:T(8,128)(2,1)S(1)} %all-to-all-done.3.keys_ref), channel_id=1, source_target_pairs={{0,4},{4,0},{1,5},{5,1},{2,6},{6,2},{3,7},{7,3},{8,12},{12,8},{9,1... | collective-permute-start | bytes 786440 | tf_op jit(solution)/shard_map/ppermute | solution.py:286
  134.8 0.1 compare_select_fusion
  134.8 12.8 %all-gather.5 = bf16[512,256]{1,0:T(8,128)(2,1)S(1)} all-gather(bf16[128,256]{1,0:T(8,128)(2,1)} %get-tuple-element.12), channel_id=7, replica_groups=mesh['yl'=2,'core'=2,'z'=16,'yh'=2,'x'=4] {'x'}, dimensions={0}, use_global_device_ids=true | all-gather | bytes 327680 | tf_op jit(solution)/shard_map/all_gather | solution.py:285
  147.6 0.0 copy-done.3
  147.6 0.7 copy-done.4
  148.3 4.9 %attend_first.1.state_ref = f32[4,72,512]{2,1,0:T(8,128)S(1)} custom-call(bf16[4,128,256]{2,1,0:T(8,128)(2,1)S(1)} %bitcast.22, bf16[64,128]{1,0:T(8,128)(2,1)S(1)} %copy-done.4, bf16[16,64,128]{2,1,0:T(8,128)(2,1)S(1)} %all-to-all-done.3.keys_ref, f32[16,512]{1,0:T(8,128)S(1)} %get-tuple-element.15.bias_ref, s32[2]{0:T(128)S(1)} %copy-done.3), custom_call_target="tpu_custom_call" | custom-call | flops 536870912 | bytes 2097152 | tf_op jit(solution)/shard_map/attend_first/pallas_call | solution.py:300
  153.3 0.0 collective-permute-done.2.keys_ref
  153.3 3.6 %attend_second.1 = f32[4,72,512]{2,1,0:T(8,128)S(1)} custom-call(bf16[4,128,256]{2,1,0:T(8,128)(2,1)S(1)} %bitcast.23, bf16[16,64,128]{2,1,0:T(8,128)(2,1)S(1)} %collective-permute-done.2.keys_ref, f32[16,512]{1,0:T(8,128)S(1)} %get-tuple-element.16.bias_ref, f32[4,72,512]{2,1,0:T(8,128)S(1)} %attend_first.1.state_ref), custom_call_target="tpu_custom_call" | custom-call | flops 536870912 | bytes 2097152 | tf_op jit(solution)/shard_map/attend_second/pallas_call | solution.py:309
  156.8 11.5 %all_to_all.26.parts_ref = f32[4,72,512]{2,1,0:T(8,128)} all-to-all(f32[4,72,512]{2,1,0:T(8,128)S(1)} %attend_second.1), channel_id=1, replica_groups=mesh['yl'=2,'core'=2,'z'=16,'yh'=2,'x'=4] {'x'}, dimensions={0} | all-to-all | bytes 1179648 | tf_op jit(solution)/shard_map/all_to_all | solution.py:318
  168.4 1.8 %combine.1 = bf16[256,128]{1,0:T(8,128)(2,1)} custom-call(f32[4,72,512]{2,1,0:T(8,128)} %all_to_all.26.parts_ref), custom_call_target="tpu_custom_call" | custom-call | tf_op jit(solution)/shard_map/combine/pallas_call | solution.py:319
  (6 shorter events, 0.0 us)
Async XLA Ops:
  6.5 88.8 %all-gather.9.cloned.1.call-start = ((), (), s32[]{:S(2)}) async-start(), calls=%async_computation.5 | async-start | bytes 3203072 | tf_op jit(solution)/shard_map/all_gather | solution.py:210
  18.4 69.9 %copy-start.2 = (s32[2]{0:T(128)}, s32[2]{0:T(128)S(1)}, u32[]{:S(2)}) copy-start(s32[2]{0:T(128)S(1)} %pad_add_fusion.place_ref) | copy-start | bytes 28
  34.4 2.0 %copy-start.1 = (bf16[3,720,720]{2,1,0:T(8,128)(2,1)S(1)}, bf16[3,720,720]{2,1,0:T(8,128)(2,1)}, u32[]{:S(2)}) copy-start(bf16[3,720,720]{2,1,0:T(8,128)(2,1)} %weight_ref.1) | copy-start | bytes 9331204
  55.7 14.8 %all-to-all-start = ((bf16[8,184,256]{2,1,0:T(8,128)(2,1)}), bf16[8,184,256]{2,1,0:T(8,128)(2,1)S(1)}, u32[]{:S(2)}, u32[]{:S(2)}) async-start(bf16[8,184,256]{2,1,0:T(8,128)(2,1)} %get-tuple-element.10), calls=%async_computation | async-start | bytes 1507328 | tf_op jit(solution)/shard_map/all_to_all | solution.py:249
  70.5 13.7 %all-to-all-start.2 = ((bf16[8,184,256]{2,1,0:T(8,128)(2,1)}), bf16[8,184,256]{2,1,0:T(8,128)(2,1)S(1)}, u32[]{:S(2)}, u32[]{:S(2)}) async-start(bf16[8,184,256]{2,1,0:T(8,128)(2,1)} %spread.1), calls=%async_computation.2 | async-start | bytes 1507328 | tf_op jit(solution)/shard_map/all_to_all | solution.py:249
  74.0 12.1 %collective-permute-start = (bf16[8,184,256]{2,1,0:T(8,128)(2,1)S(1)}, bf16[8,184,256]{2,1,0:T(8,128)(2,1)S(1)}, u32[]{:S(2)}, u32[]{:S(2)}) collective-permute-start(bf16[8,184,256]{2,1,0:T(8,128)(2,1)S(1)} %all-to-all-done.embed_own), channel_id=1, source_target_pairs={{0,128},{128,0},{1,129},{129,1},{2,130},{130,2},{3,131},{131,3},{4... | collective-permute-start | bytes 2261000 | tf_op jit(solution)/shard_map/ppermute | solution.py:250
  84.2 4.1 %collective-permute-start.1 = (bf16[8,184,256]{2,1,0:T(8,128)(2,1)S(1)}, bf16[8,184,256]{2,1,0:T(8,128)(2,1)S(1)}, u32[]{:S(2)}, u32[]{:S(2)}) collective-permute-start(bf16[8,184,256]{2,1,0:T(8,128)(2,1)S(1)} %all-to-all-done.2.merged_own), channel_id=1, source_target_pairs={{0,128},{128,0},{1,129},{129,1},{2,130},{130,2},{3,131},{131,3},{4... | collective-permute-start | bytes 2261000 | tf_op jit(solution)/shard_map/ppermute | solution.py:250
  89.6 1.6 copy-start
  91.2 20.8 %copy-start.5 = (s32[64]{0:T(128)S(1)}, s32[64]{0:T(128)}, u32[]{:S(2)}) copy-start(s32[64]{0:T(128)} %param.11) | copy-start | bytes 772
  91.2 56.4 %copy-start.3 = (s32[2]{0:T(128)S(1)}, s32[2]{0:T(128)}, u32[]{:S(2)}) copy-start(s32[2]{0:T(128)} %copy-done.2) | copy-start | bytes 28
  100.9 29.4 %all-to-all-start.3 = ((bf16[16,64,128]{2,1,0:T(8,128)(2,1)}), bf16[16,64,128]{2,1,0:T(8,128)(2,1)S(1)}, u32[]{:S(2)}, u32[]{:S(2)}) async-start(bf16[16,64,128]{2,1,0:T(8,128)(2,1)} %get-tuple-element.13), calls=%async_computation.3 | async-start | bytes 524288 | tf_op jit(solution)/shard_map/all_to_all | solution.py:284
  130.4 22.9 %collective-permute-start.2 = (bf16[16,64,128]{2,1,0:T(8,128)(2,1)S(1)}, bf16[16,64,128]{2,1,0:T(8,128)(2,1)S(1)}, u32[]{:S(2)}, u32[]{:S(2)}) collective-permute-start(bf16[16,64,128]{2,1,0:T(8,128)(2,1)S(1)} %all-to-all-done.3.keys_ref), channel_id=1, source_target_pairs={{0,4},{4,0},{1,5},{5,1},{2,6},{6,2},{3,7},{7,3},{8,12},{12,8},{9,1... | collective-permute-start | bytes 786440 | tf_op jit(solution)/shard_map/ppermute | solution.py:286
  147.6 0.7 copy-start.4
Sparse Core Ops, SparseCore 0:
  16.6 78.7 all-gather.8

commit v4 on v3

--- a/solution.py
+++ b/solution.py
@@ -75,38 +75,37 @@
                 out_ref[at] = (ref[i, :chunk].astype(jnp.float32) * scale).astype(jnp.bfloat16)
 
 
-def project_kernel(
-    rows_hbm, weights_hbm, place_ref, query_ref, sent_ref, own_ref, rows_ref, weights_ref, arrived
-):
-    x_id = place_ref[1]
-    pieces = arrived.shape[1]
-    count = weights_ref.shape[0] // pieces
+def project_columns(rows_ref, weights_hbm, first, weights_ref, arrived):
+    pieces = arrived.shape[0]
+    count, columns = weights_ref.shape[0] // pieces, weights_ref.shape[2]
     copies = []
     for p in range(pieces):
         span = pl.ds(p * count, count)
-        both = ((rows_hbm, rows_ref), (weights_hbm, weights_ref))
-        copies.append(
-            [pltpu.make_async_copy(src.at[span], dst.at[span], arrived.at[k, p]) for k, (src, dst) in enumerate(both)]
-        )
-        for copy in copies[-1]:
-            copy.start()
-    tokens = rows_ref.shape[2]
-    acc = jnp.zeros((weights_ref.shape[2], tokens), jnp.float32)
+        source = weights_hbm.at[span, :, pl.ds(first, columns)]
+        copies.append(pltpu.make_async_copy(source, weights_ref.at[span], arrived.at[p]))
+        copies[-1].start()
+    acc = jnp.zeros((columns, rows_ref.shape[2]), jnp.float32)
     for p in range(pieces):
-        for copy in copies[p]:
-            copy.wait()
+        copies[p].wait()
         for at in range(p * count, (p + 1) * count):
             acc = acc + lax.dot_general(weights_ref[at], rows_ref[at], DIM0, preferred_element_type=jnp.float32)
-    half = acc.shape[0] // 2
-    query_ref[...] = acc[:half].astype(jnp.bfloat16)
-    rows = acc[half:].T.astype(jnp.bfloat16)
-    size = sent_ref.shape[1]
+    return acc
+
+
+def project_kv_kernel(rows_ref, weights_hbm, place_ref, sent_ref, own_ref, weights_ref, arrived):
+    x_id = place_ref[1]
+    rows = project_columns(rows_ref, weights_hbm, 2 * HD, weights_ref, arrived).T.astype(jnp.bfloat16)
+    size = own_ref.shape[0]
     quarter = rows[:size]
-    for i in range(1, tokens // size):
+    for i in range(1, rows.shape[0] // size):
         quarter = jnp.where(x_id == i, rows[i * size : (i + 1) * size], quarter)
     for i in range(sent_ref.shape[0]):
         sent_ref[i] = quarter
     own_ref[...] = quarter
+
+
+def project_q_kernel(rows_ref, weights_hbm, after_ref, query_ref, weights_ref, arrived):
+    query_ref[...] = project_columns(rows_ref, weights_hbm, 0, weights_ref, arrived).astype(jnp.bfloat16)
 
 
 def heads_of(query_ref, source):
@@ -143,7 +142,7 @@
     out_ref[source, HD:] = jnp.where(row == 0, top, total)
 
 
-def first_kernel(query_ref, own_ref, keys_ref, bias_ref, place_ref, out_ref):
+def own_kernel(query_ref, own_ref, place_ref, out_ref):
     x_id = place_ref[1]
     own = own_ref[...]
     chunk = own.shape[0]
@@ -158,10 +157,10 @@
         weights = jnp.exp(scores - top)
         total = jnp.sum(weights, axis=0, keepdims=True)
         accum = lax.dot_general(own, weights.astype(jnp.bfloat16), DIM0, preferred_element_type=jnp.float32)
-        store_state(out_ref, source, attend_keys(queries, keys_ref, bias_ref, (top, total, accum[HD:])))
-
-
-def second_kernel(query_ref, keys_ref, bias_ref, state_ref, out_ref):
+        store_state(out_ref, source, (top, total, accum[HD:]))
+
+
+def more_kernel(query_ref, keys_ref, bias_ref, state_ref, out_ref):
     for source in range(query_ref.shape[0]):
         state = (
             state_ref[source, HD : HD + 1, :],
@@ -263,26 +262,41 @@
         name="norm",
     )(embed_own, embed_other, merged_own, merged_other, place)
     n_z, n_yh = lax.axis_size("z"), lax.axis_size("yh")
-    query, sent, own = pl.pallas_call(
-        project_kernel,
+    tight = pltpu.CompilerParams(vmem_limit_bytes=50 << 20)
+    scratch = [pltpu.VMEM((n_ctx, chunk, 2 * HD), jnp.bfloat16), pltpu.SemaphoreType.DMA((4,))]
+    sent, own = pl.pallas_call(
+        project_kv_kernel,
         out_shape=(
-            jax.ShapeDtypeStruct((2 * HD, tokens), jnp.bfloat16),
             jax.ShapeDtypeStruct((n_z, quarter, 2 * HD), jnp.bfloat16),
             jax.ShapeDtypeStruct((quarter, 2 * HD), jnp.bfloat16),
         ),
-        in_specs=[hbm, hbm, smem],
-        out_specs=(VMEM, VMEM, VMEM),
-        scratch_shapes=[
-            pltpu.VMEM(rows.shape, rows.dtype),
-            pltpu.VMEM(weights.shape, weights.dtype),
-            pltpu.SemaphoreType.DMA((2, 4)),
-        ],
-        compiler_params=pltpu.CompilerParams(vmem_limit_bytes=60 << 20),
-        name="project",
+        in_specs=[VMEM, hbm, smem],
+        out_specs=(VMEM, VMEM),
+        scratch_shapes=scratch,
+        compiler_params=tight,
+        name="project_kv",
     )(rows, weights, place)
-
     taken = lax.all_to_all(sent, "z", 0, 0)
+    query = pl.pallas_call(
+        project_q_kernel,
+        out_shape=jax.ShapeDtypeStruct((2 * HD, tokens), jnp.bfloat16),
+        in_specs=[VMEM, hbm, VMEM],
+        out_specs=VMEM,
+        scratch_shapes=scratch,
+        compiler_params=tight,
+        name="project_q",
+    )(rows, weights, own)
     queries = lax.all_gather(query, "x", axis=0)
+    state = jax.ShapeDtypeStruct((n_x, HD + 8, 4 * BLK), jnp.float32)
+    parts = pl.pallas_call(
+        own_kernel,
+        out_shape=state,
+        in_specs=[VMEM] * 2 + [smem],
+        out_specs=VMEM,
+        compiler_params=params,
+        name="attend_own",
+    )(queries, own, place)
+    taken, queries, parts = lax.optimization_barrier((taken, queries, parts))
     other = lax.ppermute(taken, "yh", [(0, 1), (1, 0)])
 
     placed = block_order.reshape(n_z, n_yh, 2)
@@ -295,26 +309,17 @@
     far = jnp.where(far[:, None] < mine[None, :], 0.0, -1e30).astype(jnp.float32)
 
     scores = 8 * BLK * 2 * n_z * quarter
-    state = jax.ShapeDtypeStruct((n_x, HD + 8, 4 * BLK), jnp.float32)
     cost = pl.CostEstimate(flops=scores * 4 * HD, bytes_accessed=2 << 20, transcendentals=scores)
-    parts = pl.pallas_call(
-        first_kernel,
-        out_shape=state,
-        in_specs=[VMEM] * 4 + [smem],
-        out_specs=VMEM,
-        compiler_params=params,
-        cost_estimate=cost,
-        name="attend_first",
-    )(queries, own, taken, near, place)
-    parts = pl.pallas_call(
-        second_kernel,
-        out_shape=state,
-        in_specs=[VMEM] * 4,
-        out_specs=VMEM,
-        compiler_params=params,
-        cost_estimate=cost,
-        name="attend_second",
-    )(queries, other, far, parts)
+    for keys, bias in ((taken, near), (other, far)):
+        parts = pl.pallas_call(
+            more_kernel,
+            out_shape=state,
+            in_specs=[VMEM] * 4,
+            out_specs=VMEM,
+            compiler_params=params,
+            cost_estimate=cost,
+            name="attend_more",
+        )(queries, keys, bias, parts)
     parts = lax.all_to_all(parts, "x", 0, 0)
     return pl.pallas_call(
         combine_kernel,

time: 178 us -> 166 us (0.933)
  waiting for transfers between devices: 33.8 us -> 16.3 us
  local copies, waits for them, and re-layouts: 6.6 us -> 9.39 us
  starting transfers between devices: 26.3 us -> 28.1 us
    all_to_all x1, waiting for transfers between devices: 17.9 us -> 1.43 us  [body(): taken = lax.all_to_all(sent, 'z', 0, 0)]
    unnamed x14 -> x18, local copies, waits for them, and re-layouts: 4.44 us -> 7.23 us
    ppermute x1, waiting for transfers between devices: 0.01 us -> 2.57 us  [body(): other = lax.ppermute(taken, 'yh', [(0, 1), (1, 0)])]
    pallas_call x3 -> x5, Pallas kernels: 14 us -> 15.2 us  [the longest x2 7.15 us: body(): pl.pallas_call(more_kernel, out_shape=state, in_specs=[VMEM] * 4, out_spe...]
  transfers between devices with their start and end apart: 7 -> 7, of which waited for: 5 -> 6; matrix products, arithmetic and copies ran while one was open for 1% -> 1% of each run, Pallas kernels for 7% -> 9%
where the time goes in v4:
time: 166 us; the launch traced here: 165 us
  blocking collectives  71.6 us (43%)
  starting transfers between devices  28.1 us (17%)
  Pallas kernels  26.2 us (16%)
  waiting for transfers between devices  16.3 us (10%)
  between operations  13.5 us (8%)
  local copies, waits for them, and re-layouts  9.39 us (6%)
    all_to_all x1, blocking collectives, body(): parts = lax.all_to_all(partial, 'x', 0, 0)  16.6 us
    all_to_all x1, starting transfers between devices, body(): taken = lax.all_to_all(sent, 'z', 0, 0)  12.7 us
    all_gather x1, blocking collectives, body(): queries = lax.all_gather(query, 'x', axis=0)  12.3 us
    all_to_all x1, blocking collectives, body(): parts = lax.all_to_all(parts, 'x', 0, 0)  12 us
    all_to_all x2, waiting for transfers between devices, over_x(): own = lax.all_to_all(copies, 'x', 0, 0, tiled=True)  9.49 us
    all_gather x1, blocking collectives, body(): low = lax.all_gather(turned[:split], SEG, axis=0)  8.53 us
    all_gather x1, blocking collectives, body(): weights = lax.all_gather(packed, 'yh', axis=0)  8.33 us
    all_gather x1, blocking collectives, body(): high = lax.all_gather(turned[split:], SEG, axis=0)  7.41 us
  transfers between devices with their start and end apart: 7, of which 6 were waited for; matrix products, arithmetic and copies ran while one was open for 1% of the time, Pallas kernels for 9%

profile of v4, /device:TPU:32, one launch (start us, length us, event | category | flops | bytes accessed | tf_op | source)
XLA Modules:
  0.0 165.4 jit_solution(8868088536903407294)
XLA Ops:
  6.5 1.5 pack.1
  8.1 8.3 %all-gather.6 = bf16[2,180,256]{2,1,0:T(8,128)(2,1)} all-gather(bf16[1,180,256]{2,1,0:T(8,128)(2,1)} %bitcast.26), channel_id=5, replica_groups=mesh['yl'=2,'core'=2,'z'=16,'yh'=2,'x'=4] {'yh'}, dimensions={0}, use_global_device_ids=true | all-gather | bytes 276480 | tf_op jit(solution)/shard_map/all_gather | solution.py:208
  16.4 0.0 all-gather.9.cloned.1.call-update
  16.4 0.9 slice.26
  17.4 0.9 slice.27
  18.3 0.1 pad_add_fusion.place_ref
  18.4 7.4 %all-gather.1 = bf16[1408,256]{1,0:T(8,128)(2,1)S(1)} all-gather(bf16[352,256]{1,0:T(8,128)(2,1)S(1)} %slice.27), channel_id=3, replica_groups=mesh['yl'=2,'core'=2,'z'=16,'yh'=2,'x'=4] {'yl','core'}, dimensions={0}, use_global_device_ids=true | all-gather | bytes 901120 | tf_op jit(solution)/shard_map/all_gather | solution.py:215
  25.8 8.5 %all-gather = bf16[1472,256]{1,0:T(8,128)(2,1)S(1)} all-gather(bf16[368,256]{1,0:T(8,128)(2,1)S(1)} %slice.26), channel_id=2, replica_groups=mesh['yl'=2,'core'=2,'z'=16,'yh'=2,'x'=4] {'yl','core'}, dimensions={0}, use_global_device_ids=true | all-gather | bytes 942080 | tf_op jit(solution)/shard_map/all_gather | solution.py:214
  34.4 2.0 %copy-done = bf16[3,720,720]{2,1,0:T(8,128)(2,1)S(1)} copy-done((bf16[3,720,720]{2,1,0:T(8,128)(2,1)S(1)}, bf16[3,720,720]{2,1,0:T(8,128)(2,1)}, u32[]{:S(2)}) %copy-start) | copy-done | bytes 3110424
  36.4 2.7 %merge.1 = (f32[4,180,256]{2,1,0:T(8,128)S(1)}, bf16[8,184,256]{2,1,0:T(8,128)(2,1)}) custom-call(bf16[4,368,256]{2,1,0:T(8,128)(2,1)S(1)} %bitcast.20, bf16[4,352,256]{2,1,0:T(8,128)(2,1)S(1)} %bitcast.21, bf16[3,720,720]{2,1,0:T(8,128)(2,1)S(1)} %copy-done, s32[2]{0:T(128)S(1)} %pad_add_fusion.place_ref), custom_call_target="tpu_custom_call" | custom-call | tf_op jit(solution)/shard_map/merge/pallas_call | solution.py:218
  39.1 16.6 %all_to_all.25.parts_ref = f32[4,180,256]{2,1,0:T(8,128)} all-to-all(f32[4,180,256]{2,1,0:T(8,128)S(1)} %get-tuple-element.13), channel_id=1, replica_groups=mesh['yl'=2,'core'=2,'z'=16,'yh'=2,'x'=4] {'x'}, dimensions={0} | all-to-all | bytes 1474560 | tf_op jit(solution)/shard_map/all_to_all | solution.py:230
  55.7 3.5 %all-to-all-start = ((bf16[8,184,256]{2,1,0:T(8,128)(2,1)}), bf16[8,184,256]{2,1,0:T(8,128)(2,1)S(1)}, u32[]{:S(2)}, u32[]{:S(2)}) async-start(bf16[8,184,256]{2,1,0:T(8,128)(2,1)} %get-tuple-element.12), calls=%async_computation | async-start | bytes 1507328 | tf_op jit(solution)/shard_map/all_to_all | solution.py:248
  59.2 1.8 %settle.1 = bf16[184,256]{1,0:T(8,128)(2,1)} custom-call(f32[4,180,256]{2,1,0:T(8,128)} %all_to_all.25.parts_ref), custom_call_target="tpu_custom_call" | custom-call | tf_op jit(solution)/shard_map/settle/pallas_call | solution.py:231
  61.0 6.4 %all-gather.2 = bf16[368,256]{1,0:T(8,128)(2,1)} all-gather(bf16[184,256]{1,0:T(8,128)(2,1)} %settle.1), channel_id=4, replica_groups=mesh['yl'=2,'core'=2,'z'=16,'yh'=2,'x'=4] {'yl'}, dimensions={0}, use_global_device_ids=true | all-gather | bytes 282624 | tf_op jit(solution)/shard_map/all_gather | solution.py:238
  67.4 1.8 %spread.1 = bf16[8,184,256]{2,1,0:T(8,128)(2,1)} custom-call(bf16[2,184,256]{2,1,0:T(8,128)(2,1)} %bitcast.25), custom_call_target="tpu_custom_call" | custom-call | tf_op jit(solution)/shard_map/spread/pallas_call | solution.py:239
  69.2 1.3 all-to-all-done.embed_own
  70.5 3.5 %all-to-all-start.2 = ((bf16[8,184,256]{2,1,0:T(8,128)(2,1)}), bf16[8,184,256]{2,1,0:T(8,128)(2,1)S(1)}, u32[]{:S(2)}, u32[]{:S(2)}) async-start(bf16[8,184,256]{2,1,0:T(8,128)(2,1)} %spread.1), calls=%async_computation.2 | async-start | bytes 1507328 | tf_op jit(solution)/shard_map/all_to_all | solution.py:248
  74.0 1.9 %collective-permute-start = (bf16[8,184,256]{2,1,0:T(8,128)(2,1)S(1)}, bf16[8,184,256]{2,1,0:T(8,128)(2,1)S(1)}, u32[]{:S(2)}, u32[]{:S(2)}) collective-permute-start(bf16[8,184,256]{2,1,0:T(8,128)(2,1)S(1)} %all-to-all-done.embed_own), channel_id=1, source_target_pairs={{0,128},{128,0},{1,129},{129,1},{2,130},{130,2},{3,131},{131,3},{4... | collective-permute-start | bytes 2261000 | tf_op jit(solution)/shard_map/ppermute | solution.py:249
  75.9 8.2 %all-to-all-done.2.merged_own = bf16[8,184,256]{2,1,0:T(8,128)(2,1)S(1)} async-done(((bf16[8,184,256]{2,1,0:T(8,128)(2,1)}), bf16[8,184,256]{2,1,0:T(8,128)(2,1)S(1)}, u32[]{:S(2)}, u32[]{:S(2)}) %all-to-all-start.2) | async-done | bytes 753696 | tf_op jit(solution)/shard_map/all_to_all | solution.py:248
  84.2 1.9 %collective-permute-start.1 = (bf16[8,184,256]{2,1,0:T(8,128)(2,1)S(1)}, bf16[8,184,256]{2,1,0:T(8,128)(2,1)S(1)}, u32[]{:S(2)}, u32[]{:S(2)}) collective-permute-start(bf16[8,184,256]{2,1,0:T(8,128)(2,1)S(1)} %all-to-all-done.2.merged_own), channel_id=1, source_target_pairs={{0,128},{128,0},{1,129},{129,1},{2,130},{130,2},{3,131},{131,3},{4... | collective-permute-start | bytes 2261000 | tf_op jit(solution)/shard_map/ppermute | solution.py:249
  86.1 0.9 copy-done.3
  87.0 0.0 collective-permute-done.embed_other
  87.0 0.9 copy-done.5
  87.9 0.4 collective-permute-done.1.merged_other
  88.3 1.1 copy-done.2
  89.4 1.1 copy-done.4
  90.5 1.1 copy-done.6
  91.7 1.3 norm.1.rows_ref
  92.9 0.0 copy-start.7
  92.9 2.4 %all-gather.9.cloned.1.call-done.weights_hbm = bf16[32,180,256]{2,1,0:T(8,128)(2,1)} async-done(((bf16[2,180,256]{2,1,0:T(8,128)(2,1)}), bf16[32,180,256]{2,1,0:T(8,128)(2,1)}) %all-gather.9.cloned.1.call-update) | async-done | bytes 2949136 | tf_op jit(solution)/shard_map/all_gather | solution.py:209
  95.4 3.9 %project_kv.1 = (bf16[16,64,128]{2,1,0:T(8,128)(2,1)}, bf16[64,128]{1,0:T(8,128)(2,1)S(1)}) custom-call(bf16[32,180,256]{2,1,0:T(8,128)(2,1)S(1)} %norm.1.rows_ref, bf16[32,180,256]{2,1,0:T(8,128)(2,1)} %all-gather.9.cloned.1.call-done.weights_hbm, s32[2]{0:T(128)S(1)} %pad_add_fusion.place_ref), custom_call_target="tpu_custom_call" | custom-call | tf_op jit(solution)/shard_map/project_kv/pallas_call | solution.py:267
  99.3 12.7 %all-to-all-start.3 = ((bf16[16,64,128]{2,1,0:T(8,128)(2,1)}), bf16[16,64,128]{2,1,0:T(8,128)(2,1)S(1)}, u32[]{:S(2)}, u32[]{:S(2)}) async-start(bf16[16,64,128]{2,1,0:T(8,128)(2,1)} %get-tuple-element.14), calls=%async_computation.3 | async-start | bytes 524288 | tf_op jit(solution)/shard_map/all_to_all | solution.py:279
  112.0 0.1 reshape.10
  112.2 0.1 dynamic_slice.3
  112.2 0.1 broadcast_bitcast_fusion
  112.3 0.1 slice_select_fusion
  112.4 0.1 copy.9
  112.5 2.6 %project_q.1 = bf16[128,256]{1,0:T(8,128)(2,1)S(1)} custom-call(bf16[32,180,256]{2,1,0:T(8,128)(2,1)S(1)} %norm.1.rows_ref, bf16[32,180,256]{2,1,0:T(8,128)(2,1)} %all-gather.9.cloned.1.call-done.weights_hbm, bf16[64,128]{1,0:T(8,128)(2,1)S(1)} %get-tuple-element.15.after_ref.own_ref), custom_call_target="tpu_custom_call" | custom-call | tf_op jit(solution)/shard_map/project_q/pallas_call | solution.py:280
  115.1 12.3 %all-gather.5 = bf16[512,256]{1,0:T(8,128)(2,1)S(1)} all-gather(bf16[128,256]{1,0:T(8,128)(2,1)S(1)} %project_q.1), channel_id=7, replica_groups=mesh['yl'=2,'core'=2,'z'=16,'yh'=2,'x'=4] {'x'}, dimensions={0}, use_global_device_ids=true | all-gather | bytes 327680 | tf_op jit(solution)/shard_map/all_gather | solution.py:289
  127.4 1.5 attend_own.1.state_ref
  129.0 1.4 all-to-all-done.3.keys_ref
  130.4 4.6 %collective-permute-start.2 = (bf16[16,64,128]{2,1,0:T(8,128)(2,1)S(1)}, bf16[16,64,128]{2,1,0:T(8,128)(2,1)S(1)}, u32[]{:S(2)}, u32[]{:S(2)}) collective-permute-start(bf16[16,64,128]{2,1,0:T(8,128)(2,1)S(1)} %all-to-all-done.3.keys_ref), channel_id=1, source_target_pairs={{0,4},{4,0},{1,5},{5,1},{2,6},{6,2},{3,7},{7,3},{8,12},{12,8},{9,1... | collective-permute-start | bytes 786440 | tf_op jit(solution)/shard_map/ppermute | solution.py:300
  135.0 0.1 compare_select_fusion
  135.0 3.6 %attend_more.2.state_ref = f32[4,72,512]{2,1,0:T(8,128)S(1)} custom-call(bf16[4,128,256]{2,1,0:T(8,128)(2,1)S(1)} %bitcast.23, bf16[16,64,128]{2,1,0:T(8,128)(2,1)S(1)} %all-to-all-done.3.keys_ref, f32[16,512]{1,0:T(8,128)S(1)} %get-tuple-element.19.bias_ref, f32[4,72,512]{2,1,0:T(8,128)S(1)} %attend_own.1.state_ref), custom_call_target="tpu_custom_call" | custom-call | flops 536870912 | bytes 2097152 | tf_op jit(solution)/shard_map/attend_more/pallas_call | solution.py:314
  138.6 2.6 %collective-permute-done.2.keys_ref = bf16[16,64,128]{2,1,0:T(8,128)(2,1)S(1)} collective-permute-done((bf16[16,64,128]{2,1,0:T(8,128)(2,1)S(1)}, bf16[16,64,128]{2,1,0:T(8,128)(2,1)S(1)}, u32[]{:S(2)}, u32[]{:S(2)}) %collective-permute-start.2) | collective-permute-done | bytes 262176 | tf_op jit(solution)/shard_map/ppermute | solution.py:300
  141.2 3.6 %attend_more.3 = f32[4,72,512]{2,1,0:T(8,128)S(1)} custom-call(bf16[4,128,256]{2,1,0:T(8,128)(2,1)S(1)} %bitcast.24, bf16[16,64,128]{2,1,0:T(8,128)(2,1)S(1)} %collective-permute-done.2.keys_ref, f32[16,512]{1,0:T(8,128)S(1)} %get-tuple-element.20.bias_ref, f32[4,72,512]{2,1,0:T(8,128)S(1)} %attend_more.2.state_ref), custom_call_target="tpu_custom_call" | custom-call | flops 536870912 | bytes 2097152 | tf_op jit(solution)/shard_map/attend_more/pallas_call | solution.py:314
  144.8 12.0 %all_to_all.26.parts_ref = f32[4,72,512]{2,1,0:T(8,128)} all-to-all(f32[4,72,512]{2,1,0:T(8,128)S(1)} %attend_more.3), channel_id=1, replica_groups=mesh['yl'=2,'core'=2,'z'=16,'yh'=2,'x'=4] {'x'}, dimensions={0} | all-to-all | bytes 1179648 | tf_op jit(solution)/shard_map/all_to_all | solution.py:323
  156.7 1.8 %combine.1 = bf16[256,128]{1,0:T(8,128)(2,1)} custom-call(f32[4,72,512]{2,1,0:T(8,128)} %all_to_all.26.parts_ref), custom_call_target="tpu_custom_call" | custom-call | tf_op jit(solution)/shard_map/combine/pallas_call | solution.py:324
  (12 shorter events, 0.0 us)
Async XLA Ops:
  6.5 88.8 %all-gather.9.cloned.1.call-start = ((), (), s32[]{:S(2)}) async-start(), calls=%async_computation.5 | async-start | bytes 3203072 | tf_op jit(solution)/shard_map/all_gather | solution.py:209
  34.4 2.0 %copy-start = (bf16[3,720,720]{2,1,0:T(8,128)(2,1)S(1)}, bf16[3,720,720]{2,1,0:T(8,128)(2,1)}, u32[]{:S(2)}) copy-start(bf16[3,720,720]{2,1,0:T(8,128)(2,1)} %weight_ref.1) | copy-start | bytes 9331204
  55.7 14.8 %all-to-all-start = ((bf16[8,184,256]{2,1,0:T(8,128)(2,1)}), bf16[8,184,256]{2,1,0:T(8,128)(2,1)S(1)}, u32[]{:S(2)}, u32[]{:S(2)}) async-start(bf16[8,184,256]{2,1,0:T(8,128)(2,1)} %get-tuple-element.12), calls=%async_computation | async-start | bytes 1507328 | tf_op jit(solution)/shard_map/all_to_all | solution.py:248
  70.5 16.5 %copy-start.1 = (bf16[8,184,256]{2,1,0:T(8,128)(2,1)}, bf16[8,184,256]{2,1,0:T(8,128)(2,1)S(1)}, u32[]{:S(2)}) copy-start(bf16[8,184,256]{2,1,0:T(8,128)(2,1)S(1)} %all-to-all-done.embed_own) | copy-start | bytes 2260996
  70.5 13.7 %all-to-all-start.2 = ((bf16[8,184,256]{2,1,0:T(8,128)(2,1)}), bf16[8,184,256]{2,1,0:T(8,128)(2,1)S(1)}, u32[]{:S(2)}, u32[]{:S(2)}) async-start(bf16[8,184,256]{2,1,0:T(8,128)(2,1)} %spread.1), calls=%async_computation.2 | async-start | bytes 1507328 | tf_op jit(solution)/shard_map/all_to_all | solution.py:248
  74.0 13.0 %collective-permute-start = (bf16[8,184,256]{2,1,0:T(8,128)(2,1)S(1)}, bf16[8,184,256]{2,1,0:T(8,128)(2,1)S(1)}, u32[]{:S(2)}, u32[]{:S(2)}) collective-permute-start(bf16[8,184,256]{2,1,0:T(8,128)(2,1)S(1)} %all-to-all-done.embed_own), channel_id=1, source_target_pairs={{0,128},{128,0},{1,129},{129,1},{2,130},{130,2},{3,131},{131,3},{4... | collective-permute-start | bytes 2261000 | tf_op jit(solution)/shard_map/ppermute | solution.py:249
  84.2 4.1 %collective-permute-start.1 = (bf16[8,184,256]{2,1,0:T(8,128)(2,1)S(1)}, bf16[8,184,256]{2,1,0:T(8,128)(2,1)S(1)}, u32[]{:S(2)}, u32[]{:S(2)}) collective-permute-start(bf16[8,184,256]{2,1,0:T(8,128)(2,1)S(1)} %all-to-all-done.2.merged_own), channel_id=1, source_target_pairs={{0,128},{128,0},{1,129},{129,1},{2,130},{130,2},{3,131},{131,3},{4... | collective-permute-start | bytes 2261000 | tf_op jit(solution)/shard_map/ppermute | solution.py:249
  86.1 0.9 copy-start.3
  87.0 0.9 copy-start.5
  88.3 1.1 copy-start.2
  89.4 1.1 copy-start.4
  90.5 1.1 copy-start.6
  92.9 19.1 %copy-start.7 = (s32[64]{0:T(128)S(1)}, s32[64]{0:T(128)}, u32[]{:S(2)}) copy-start(s32[64]{0:T(128)} %param.11) | copy-start | bytes 772
  99.3 31.1 %all-to-all-start.3 = ((bf16[16,64,128]{2,1,0:T(8,128)(2,1)}), bf16[16,64,128]{2,1,0:T(8,128)(2,1)S(1)}, u32[]{:S(2)}, u32[]{:S(2)}) async-start(bf16[16,64,128]{2,1,0:T(8,128)(2,1)} %get-tuple-element.14), calls=%async_computation.3 | async-start | bytes 524288 | tf_op jit(solution)/shard_map/all_to_all | solution.py:279
  130.4 10.8 %collective-permute-start.2 = (bf16[16,64,128]{2,1,0:T(8,128)(2,1)S(1)}, bf16[16,64,128]{2,1,0:T(8,128)(2,1)S(1)}, u32[]{:S(2)}, u32[]{:S(2)}) collective-permute-start(bf16[16,64,128]{2,1,0:T(8,128)(2,1)S(1)} %all-to-all-done.3.keys_ref), channel_id=1, source_target_pairs={{0,4},{4,0},{1,5},{5,1},{2,6},{6,2},{3,7},{7,3},{8,12},{12,8},{9,1... | collective-permute-start | bytes 786440 | tf_op jit(solution)/shard_map/ppermute | solution.py:300
Sparse Core Ops, SparseCore 0:
  16.6 78.7 all-gather.8

commit v5 on v4

--- a/solution.py
+++ b/solution.py
@@ -15,8 +15,10 @@
 
 def pack_kernel(query_ref, key_ref, value_ref, out_ref):
     turned = jnp.concatenate([key_ref[...], value_ref[...]], axis=0).astype(jnp.float32)
-    out_ref[:, : query_ref.shape[1]] = query_ref[...]
-    out_ref[:, query_ref.shape[1] :] = turned.T.astype(jnp.bfloat16)
+    chunk = query_ref.shape[0]
+    out_ref[...] = jnp.zeros_like(out_ref)
+    out_ref[:chunk, : query_ref.shape[1]] = query_ref[...]
+    out_ref[:chunk, query_ref.shape[1] :] = turned.T.astype(jnp.bfloat16)
 
 
 def merge_kernel(low_ref, high_ref, weight_ref, place_ref, partial_ref, embed_ref, hold_ref):
@@ -54,13 +56,23 @@
         out_ref[i * count : (i + 1) * count] = block_ref[...]
 
 
-def norm_kernel(embed_own, embed_other, merged_own, merged_other, place_ref, out_ref):
-    core = place_ref[0]
+def project_kernel(
+    embed_own, embed_other, merged_own, merged_other, weights_hbm, place_ref,
+    query_ref, sent_ref, own_ref, rows_ref, weights_ref, arrived,
+):
+    core, x_id = place_ref[0], place_ref[1]
+    pieces = arrived.shape[0]
+    count = weights_ref.shape[0] // pieces
+    copies = []
+    for p in range(pieces):
+        span = pl.ds(p * count, count)
+        copies.append(pltpu.make_async_copy(weights_hbm.at[span], weights_ref.at[span], arrived.at[p]))
+        copies[-1].start()
     chunks = embed_own.shape[0]
-    chunk = out_ref.shape[1]
+    _, chunk, tokens = rows_ref.shape
     width = 2 * chunks * chunk
     for kind, pair in enumerate(((embed_own, embed_other), (merged_own, merged_other))):
-        total = jnp.zeros((1, out_ref.shape[2]), jnp.float32)
+        total = jnp.zeros((1, tokens), jnp.float32)
         for ref in pair:
             for i in range(chunks):
                 part = ref[i, :chunk].astype(jnp.float32)
@@ -72,40 +84,24 @@
                     at = i // 2 * 4 + 2 * side + i % 2
                 else:
                     at = 2 * chunks + (2 * (i % 2) + side) * 4 + i // 2
-                out_ref[at] = (ref[i, :chunk].astype(jnp.float32) * scale).astype(jnp.bfloat16)
-
-
-def project_columns(rows_ref, weights_hbm, first, weights_ref, arrived):
-    pieces = arrived.shape[0]
-    count, columns = weights_ref.shape[0] // pieces, weights_ref.shape[2]
-    copies = []
-    for p in range(pieces):
-        span = pl.ds(p * count, count)
-        source = weights_hbm.at[span, :, pl.ds(first, columns)]
-        copies.append(pltpu.make_async_copy(source, weights_ref.at[span], arrived.at[p]))
-        copies[-1].start()
-    acc = jnp.zeros((columns, rows_ref.shape[2]), jnp.float32)
+                rows_ref[at] = (ref[i, :chunk].astype(jnp.float32) * scale).astype(jnp.bfloat16)
+    acc = jnp.zeros((weights_ref.shape[2], tokens), jnp.float32)
     for p in range(pieces):
         copies[p].wait()
         for at in range(p * count, (p + 1) * count):
-            acc = acc + lax.dot_general(weights_ref[at], rows_ref[at], DIM0, preferred_element_type=jnp.float32)
-    return acc
-
-
-def project_kv_kernel(rows_ref, weights_hbm, place_ref, sent_ref, own_ref, weights_ref, arrived):
-    x_id = place_ref[1]
-    rows = project_columns(rows_ref, weights_hbm, 2 * HD, weights_ref, arrived).T.astype(jnp.bfloat16)
+            acc = acc + lax.dot_general(
+                weights_ref[at, :chunk], rows_ref[at], DIM0, preferred_element_type=jnp.float32
+            )
+    half = acc.shape[0] // 2
+    query_ref[...] = acc[:half].astype(jnp.bfloat16)
+    rows = acc[half:].T.astype(jnp.bfloat16)
     size = own_ref.shape[0]
     quarter = rows[:size]
-    for i in range(1, rows.shape[0] // size):
+    for i in range(1, tokens // size):
         quarter = jnp.where(x_id == i, rows[i * size : (i + 1) * size], quarter)
     for i in range(sent_ref.shape[0]):
         sent_ref[i] = quarter
     own_ref[...] = quarter
-
-
-def project_q_kernel(rows_ref, weights_hbm, after_ref, query_ref, weights_ref, arrived):
-    query_ref[...] = project_columns(rows_ref, weights_hbm, 0, weights_ref, arrived).astype(jnp.bfloat16)
 
 
 def heads_of(query_ref, source):
@@ -160,19 +156,43 @@
         store_state(out_ref, source, (top, total, accum[HD:]))
 
 
+def load_state(state_ref, source):
+    rows = (slice(HD, HD + 1), slice(HD + 1, HD + 2), slice(0, HD))
+    return tuple(state_ref[source, r, :] for r in rows)
+
+
 def more_kernel(query_ref, keys_ref, bias_ref, state_ref, out_ref):
     for source in range(query_ref.shape[0]):
-        state = (
-            state_ref[source, HD : HD + 1, :],
-            state_ref[source, HD + 1 : HD + 2, :],
-            state_ref[source, :HD, :],
+        state = load_state(state_ref, source)
+        store_state(out_ref, source, attend_keys(heads_of(query_ref, source), keys_ref, bias_ref, state))
+
+
+def thirds(value):
+    high = value.astype(jnp.bfloat16).astype(jnp.float32)
+    middle = (value - high).astype(jnp.bfloat16).astype(jnp.float32)
+    return high, middle, value - high - middle
+
+
+def last_kernel(query_ref, keys_ref, bias_ref, state_ref, out_ref):
+    for source in range(query_ref.shape[0]):
+        top, total, accum = attend_keys(
+            heads_of(query_ref, source), keys_ref, bias_ref, load_state(state_ref, source)
         )
-        store_state(out_ref, source, attend_keys(heads_of(query_ref, source), keys_ref, bias_ref, state))
+        out_ref[source, :HD] = accum.astype(jnp.bfloat16)
+        row = lax.broadcasted_iota(jnp.int32, (out_ref.shape[1] - HD, accum.shape[1]), 0)
+        rest = jnp.zeros(row.shape, jnp.float32)
+        for at, term in enumerate((*thirds(top), *thirds(total))):
+            rest = jnp.where(row == at, term, rest)
+        out_ref[source, HD:] = rest.astype(jnp.bfloat16)
 
 
 def combine_kernel(parts_ref, out_ref):
     count = parts_ref.shape[0]
-    tops = [parts_ref[i, HD : HD + 1, :] for i in range(count)]
+    tops, totals = [], []
+    for i in range(count):
+        rest = parts_ref[i, HD:, :].astype(jnp.float32)
+        tops.append(rest[0:1] + rest[1:2] + rest[2:3])
+        totals.append(rest[3:4] + rest[4:5] + rest[5:6])
     top = tops[0]
     for i in range(1, count):
         top = jnp.maximum(top, tops[i])
@@ -180,8 +200,8 @@
     accum = jnp.zeros((HD, parts_ref.shape[2]), jnp.float32)
     for i in range(count):
         share = jnp.exp(tops[i] - top)
-        total = total + parts_ref[i, HD + 1 : HD + 2, :] * share
-        accum = accum + parts_ref[i, :HD, :] * share
+        total = total + totals[i] * share
+        accum = accum + parts_ref[i, :HD, :].astype(jnp.float32) * share
     result = accum / total
     for a in range(2):
         left = result[:, 2 * a * BLK : (2 * a + 1) * BLK]
@@ -198,9 +218,10 @@
     smem, hbm = pl.BlockSpec(memory_space=pltpu.SMEM), pl.BlockSpec(memory_space=pltpu.HBM)
     place = jnp.stack([core, x_id]).astype(jnp.int32)
 
+    padded = (chunk + 7) // 8 * 8
     packed = pl.pallas_call(
         pack_kernel,
-        out_shape=jax.ShapeDtypeStruct((query_weight.shape[0], 4 * HD), jnp.bfloat16),
+        out_shape=jax.ShapeDtypeStruct((padded, 4 * HD), jnp.bfloat16),
         in_specs=[VMEM] * 3,
         out_specs=VMEM,
         name="pack",
@@ -214,7 +235,6 @@
     low = lax.all_gather(turned[:split], SEG, axis=0)
     high = lax.all_gather(turned[split:], SEG, axis=0)
 
-    padded = (chunk + 7) // 8 * 8
     partial, embed = pl.pallas_call(
         merge_kernel,
         out_shape=(
@@ -253,39 +273,25 @@
 
     quarter = tokens // n_x
     params = pltpu.CompilerParams(vmem_limit_bytes=40 << 20)
-    rows = pl.pallas_call(
-        norm_kernel,
-        out_shape=jax.ShapeDtypeStruct((n_ctx, chunk, tokens), jnp.bfloat16),
-        in_specs=[VMEM] * 4 + [smem],
-        out_specs=VMEM,
-        compiler_params=params,
-        name="norm",
-    )(embed_own, embed_other, merged_own, merged_other, place)
     n_z, n_yh = lax.axis_size("z"), lax.axis_size("yh")
-    tight = pltpu.CompilerParams(vmem_limit_bytes=50 << 20)
-    scratch = [pltpu.VMEM((n_ctx, chunk, 2 * HD), jnp.bfloat16), pltpu.SemaphoreType.DMA((4,))]
-    sent, own = pl.pallas_call(
-        project_kv_kernel,
+    query, sent, own = pl.pallas_call(
+        project_kernel,
         out_shape=(
+            jax.ShapeDtypeStruct((2 * HD, tokens), jnp.bfloat16),
             jax.ShapeDtypeStruct((n_z, quarter, 2 * HD), jnp.bfloat16),
             jax.ShapeDtypeStruct((quarter, 2 * HD), jnp.bfloat16),
         ),
-        in_specs=[VMEM, hbm, smem],
-        out_specs=(VMEM, VMEM),
-        scratch_shapes=scratch,
-        compiler_params=tight,
-        name="project_kv",
-    )(rows, weights, place)
+        in_specs=[VMEM] * 4 + [hbm, smem],
+        out_specs=(VMEM, VMEM, VMEM),
+        scratch_shapes=[
+            pltpu.VMEM((n_ctx, chunk, tokens), jnp.bfloat16),
+            pltpu.VMEM(weights.shape, weights.dtype),
+            pltpu.SemaphoreType.DMA((4,)),
+        ],
+        compiler_params=pltpu.CompilerParams(vmem_limit_bytes=48 << 20),
+        name="project",
+    )(embed_own, embed_other, merged_own, merged_other, weights, place)
     taken = lax.all_to_all(sent, "z", 0, 0)
-    query = pl.pallas_call(
-        project_q_kernel,
-        out_shape=jax.ShapeDtypeStruct((2 * HD, tokens), jnp.bfloat16),
-        in_specs=[VMEM, hbm, VMEM],
-        out_specs=VMEM,
-        scratch_shapes=scratch,
-        compiler_params=tight,
-        name="project_q",
-    )(rows, weights, own)
     queries = lax.all_gather(query, "x", axis=0)
     state = jax.ShapeDtypeStruct((n_x, HD + 8, 4 * BLK), jnp.float32)
     parts = pl.pallas_call(
@@ -310,10 +316,11 @@
 
     scores = 8 * BLK * 2 * n_z * quarter
     cost = pl.CostEstimate(flops=scores * 4 * HD, bytes_accessed=2 << 20, transcendentals=scores)
-    for keys, bias in ((taken, near), (other, far)):
+    sums = jax.ShapeDtypeStruct((n_x, HD + 16, 4 * BLK), jnp.bfloat16)
+    for kernel, keys, bias, shape in ((more_kernel, taken, near, state), (last_kernel, other, far, sums)):
         parts = pl.pallas_call(
-            more_kernel,
-            out_shape=state,
+            kernel,
+            out_shape=shape,
             in_specs=[VMEM] * 4,
             out_specs=VMEM,
             compiler_params=params,

time: 166 us -> 161 us (0.970)
  waiting for transfers between devices: 16.3 us -> 24.8 us
  local copies, waits for them, and re-layouts: 9.39 us -> 4.25 us
  starting transfers between devices: 28.1 us -> 23.2 us
  Pallas kernels: 26.2 us -> 23.6 us
    unnamed x18 -> x6, local copies, waits for them, and re-layouts: 7.23 us -> 2.09 us
    all_gather x1, waiting for transfers between devices: 2.43 us -> 7.07 us  [body(): weights = lax.all_gather(weights, 'z', axis=0)]
    all_to_all x1, starting transfers between devices: 12.7 us -> 8.13 us  [body(): taken = lax.all_to_all(sent, 'z', 0, 0)]
    pallas_call x6 -> x4, Pallas kernels: 16.5 us -> 13.9 us  [the longest x2 7.15 us: body(): pl.pallas_call(kernel, out_shape=shape, in_specs=[VMEM] * 4, out_specs=VM...]
    all_to_all x1, blocking collectives: 12 us -> 10.1 us  [body(): parts = lax.all_to_all(parts, 'x', 0, 0)]
    all_to_all x1, waiting for transfers between devices: 1.43 us -> 3.22 us  [body(): taken = lax.all_to_all(sent, 'z', 0, 0)]
    ppermute x2, waiting for transfers between devices: 0.42 us -> 2.2 us  [over_x(): return (own, lax.ppermute(own, 'core', [(0, 1), (1, 0)]))]
  transfers between devices with their start and end apart: 7 -> 7, of which waited for: 6 -> 6; matrix products, arithmetic and copies ran while one was open for 1% -> 2% of each run, Pallas kernels for 9% -> 7%
where the time goes in v5:
time: 161 us; the launch traced here: 160 us
  blocking collectives  70.6 us (44%)
  waiting for transfers between devices  24.8 us (15%)
  Pallas kernels  23.6 us (15%)
  starting transfers between devices  23.2 us (14%)
  between operations  13.5 us (8%)
  local copies, waits for them, and re-layouts  4.25 us (3%)
    all_to_all x1, blocking collectives, body(): parts = lax.all_to_all(partial, 'x', 0, 0)  16.6 us
    all_gather x1, blocking collectives, body(): queries = lax.all_gather(query, 'x', axis=0)  13.1 us
    all_to_all x1, blocking collectives, body(): parts = lax.all_to_all(parts, 'x', 0, 0)  10.1 us
    all_to_all x2, waiting for transfers between devices, over_x(): own = lax.all_to_all(copies, 'x', 0, 0, tiled=True)  9.44 us
    all_gather x1, blocking collectives, body(): low = lax.all_gather(turned[:split], SEG, axis=0)  8.53 us
    all_gather x1, blocking collectives, body(): weights = lax.all_gather(packed, 'yh', axis=0)  8.38 us
    all_to_all x1, starting transfers between devices, body(): taken = lax.all_to_all(sent, 'z', 0, 0)  8.13 us
    all_gather x1, blocking collectives, body(): high = lax.all_gather(turned[split:], SEG, axis=0)  7.41 us
  transfers between devices with their start and end apart: 7, of which 6 were waited for; matrix products, arithmetic and copies ran while one was open for 2% of the time, Pallas kernels for 7%

profile of v5, /device:TPU:32, one launch (start us, length us, event | category | flops | bytes accessed | tf_op | source)
XLA Modules:
  0.0 160.2 jit_solution(4411636605107741972)
XLA Ops:
  6.5 0.0 all-gather.8.cloned.1.call-start
  6.5 1.6 pack.1
  8.1 8.4 %all-gather.3 = bf16[368,256]{1,0:T(8,128)(2,1)} all-gather(bf16[184,256]{1,0:T(8,128)(2,1)} %pack.1), channel_id=5, replica_groups=mesh['yl'=2,'core'=2,'z'=16,'yh'=2,'x'=4] {'yh'}, dimensions={0}, use_global_device_ids=true | all-gather | bytes 282624 | tf_op jit(solution)/shard_map/all_gather | solution.py:229
  16.5 0.0 all-gather.8.cloned.1.call-update
  16.5 0.9 slice.26
  17.5 0.9 slice.27
  18.4 0.1 pad_add_fusion.place_ref
  18.5 7.4 %all-gather.1 = bf16[1408,256]{1,0:T(8,128)(2,1)S(1)} all-gather(bf16[352,256]{1,0:T(8,128)(2,1)S(1)} %slice.27), channel_id=3, replica_groups=mesh['yl'=2,'core'=2,'z'=16,'yh'=2,'x'=4] {'yl','core'}, dimensions={0}, use_global_device_ids=true | all-gather | bytes 901120 | tf_op jit(solution)/shard_map/all_gather | solution.py:236
  25.9 8.5 %all-gather = bf16[1472,256]{1,0:T(8,128)(2,1)S(1)} all-gather(bf16[368,256]{1,0:T(8,128)(2,1)S(1)} %slice.26), channel_id=2, replica_groups=mesh['yl'=2,'core'=2,'z'=16,'yh'=2,'x'=4] {'yl','core'}, dimensions={0}, use_global_device_ids=true | all-gather | bytes 942080 | tf_op jit(solution)/shard_map/all_gather | solution.py:235
  34.4 0.0 copy-start
  34.4 2.0 %copy-done = bf16[3,720,720]{2,1,0:T(8,128)(2,1)S(1)} copy-done((bf16[3,720,720]{2,1,0:T(8,128)(2,1)S(1)}, bf16[3,720,720]{2,1,0:T(8,128)(2,1)}, u32[]{:S(2)}) %copy-start) | copy-done | bytes 3110424
  36.4 2.7 %merge.1 = (f32[4,180,256]{2,1,0:T(8,128)S(1)}, bf16[8,184,256]{2,1,0:T(8,128)(2,1)}) custom-call(bf16[4,368,256]{2,1,0:T(8,128)(2,1)S(1)} %bitcast.20, bf16[4,352,256]{2,1,0:T(8,128)(2,1)S(1)} %bitcast.21, bf16[3,720,720]{2,1,0:T(8,128)(2,1)S(1)} %copy-done, s32[2]{0:T(128)S(1)} %pad_add_fusion.place_ref), custom_call_target="tpu_custom_call" | custom-call | tf_op jit(solution)/shard_map/merge/pallas_call | solution.py:238
  39.1 16.6 %all_to_all.25.parts_ref = f32[4,180,256]{2,1,0:T(8,128)} all-to-all(f32[4,180,256]{2,1,0:T(8,128)S(1)} %get-tuple-element.14), channel_id=1, replica_groups=mesh['yl'=2,'core'=2,'z'=16,'yh'=2,'x'=4] {'x'}, dimensions={0} | all-to-all | bytes 1474560 | tf_op jit(solution)/shard_map/all_to_all | solution.py:250
  55.8 3.5 %all-to-all-start = ((bf16[8,184,256]{2,1,0:T(8,128)(2,1)}), bf16[8,184,256]{2,1,0:T(8,128)(2,1)S(1)}, u32[]{:S(2)}, u32[]{:S(2)}) async-start(bf16[8,184,256]{2,1,0:T(8,128)(2,1)} %get-tuple-element.13), calls=%async_computation | async-start | bytes 1507328 | tf_op jit(solution)/shard_map/all_to_all | solution.py:268
  59.3 1.8 %settle.1 = bf16[184,256]{1,0:T(8,128)(2,1)} custom-call(f32[4,180,256]{2,1,0:T(8,128)} %all_to_all.25.parts_ref), custom_call_target="tpu_custom_call" | custom-call | tf_op jit(solution)/shard_map/settle/pallas_call | solution.py:251
  61.1 6.4 %all-gather.2 = bf16[368,256]{1,0:T(8,128)(2,1)} all-gather(bf16[184,256]{1,0:T(8,128)(2,1)} %settle.1), channel_id=4, replica_groups=mesh['yl'=2,'core'=2,'z'=16,'yh'=2,'x'=4] {'yl'}, dimensions={0}, use_global_device_ids=true | all-gather | bytes 282624 | tf_op jit(solution)/shard_map/all_gather | solution.py:258
  67.4 1.9 %spread.1 = bf16[8,184,256]{2,1,0:T(8,128)(2,1)} custom-call(bf16[2,184,256]{2,1,0:T(8,128)(2,1)} %bitcast.25), custom_call_target="tpu_custom_call" | custom-call | tf_op jit(solution)/shard_map/spread/pallas_call | solution.py:259
  69.3 1.3 all-to-all-done.embed_own
  70.6 3.5 %all-to-all-start.2 = ((bf16[8,184,256]{2,1,0:T(8,128)(2,1)}), bf16[8,184,256]{2,1,0:T(8,128)(2,1)S(1)}, u32[]{:S(2)}, u32[]{:S(2)}) async-start(bf16[8,184,256]{2,1,0:T(8,128)(2,1)} %spread.1), calls=%async_computation.2 | async-start | bytes 1507328 | tf_op jit(solution)/shard_map/all_to_all | solution.py:268
  74.1 0.0 copy-start.1
  74.1 1.9 %collective-permute-start = (bf16[8,184,256]{2,1,0:T(8,128)(2,1)S(1)}, bf16[8,184,256]{2,1,0:T(8,128)(2,1)S(1)}, u32[]{:S(2)}, u32[]{:S(2)}) collective-permute-start(bf16[8,184,256]{2,1,0:T(8,128)(2,1)S(1)} %all-to-all-done.embed_own), channel_id=1, source_target_pairs={{0,128},{128,0},{1,129},{129,1},{2,130},{130,2},{3,131},{131,3},{4... | collective-permute-start | bytes 2261000 | tf_op jit(solution)/shard_map/ppermute | solution.py:269
  76.0 8.2 %all-to-all-done.2.merged_own = bf16[8,184,256]{2,1,0:T(8,128)(2,1)S(1)} async-done(((bf16[8,184,256]{2,1,0:T(8,128)(2,1)}), bf16[8,184,256]{2,1,0:T(8,128)(2,1)S(1)}, u32[]{:S(2)}, u32[]{:S(2)}) %all-to-all-start.2) | async-done | bytes 753696 | tf_op jit(solution)/shard_map/all_to_all | solution.py:268
  84.2 1.9 %collective-permute-start.1 = (bf16[8,184,256]{2,1,0:T(8,128)(2,1)S(1)}, bf16[8,184,256]{2,1,0:T(8,128)(2,1)S(1)}, u32[]{:S(2)}, u32[]{:S(2)}) collective-permute-start(bf16[8,184,256]{2,1,0:T(8,128)(2,1)S(1)} %all-to-all-done.2.merged_own), channel_id=1, source_target_pairs={{0,128},{128,0},{1,129},{129,1},{2,130},{130,2},{3,131},{131,3},{4... | collective-permute-start | bytes 2261000 | tf_op jit(solution)/shard_map/ppermute | solution.py:269
  86.1 0.0 collective-permute-done.embed_other
  86.1 2.2 %collective-permute-done.1.merged_other = bf16[8,184,256]{2,1,0:T(8,128)(2,1)S(1)} collective-permute-done((bf16[8,184,256]{2,1,0:T(8,128)(2,1)S(1)}, bf16[8,184,256]{2,1,0:T(8,128)(2,1)S(1)}, u32[]{:S(2)}, u32[]{:S(2)}) %collective-permute-start.1) | collective-permute-done | bytes 753696 | tf_op jit(solution)/shard_map/ppermute | solution.py:269
  88.3 7.1 %all-gather.8.cloned.1.call-done.weights_hbm = bf16[32,184,256]{2,1,0:T(8,128)(2,1)} async-done(((bf16[2,184,256]{2,1,0:T(8,128)(2,1)}), bf16[32,184,256]{2,1,0:T(8,128)(2,1)}) %all-gather.8.cloned.1.call-update) | async-done | bytes 3014672 | tf_op jit(solution)/shard_map/all_gather | solution.py:230
  95.4 5.2 %project.1 = (bf16[128,256]{1,0:T(8,128)(2,1)S(1)}, bf16[16,64,128]{2,1,0:T(8,128)(2,1)}, bf16[64,128]{1,0:T(8,128)(2,1)S(1)}) custom-call(bf16[8,184,256]{2,1,0:T(8,128)(2,1)S(1)} %all-to-all-done.embed_own, bf16[8,184,256]{2,1,0:T(8,128)(2,1)S(1)} %collective-permute-done.embed_other, bf16[8,184,256]{2,1,0:T(8,128)(2,1)S(1)} %all-to-all-done.2.merged_own, ...), custom_call_target="tpu_custom_call" | custom-call | tf_op jit(solution)/shard_map/project/pallas_call | solution.py:277
  100.6 8.1 %all-to-all-start.3 = ((bf16[16,64,128]{2,1,0:T(8,128)(2,1)}), bf16[16,64,128]{2,1,0:T(8,128)(2,1)S(1)}, u32[]{:S(2)}, u32[]{:S(2)}) async-start(bf16[16,64,128]{2,1,0:T(8,128)(2,1)} %get-tuple-element.15), calls=%async_computation.3 | async-start | bytes 524288 | tf_op jit(solution)/shard_map/all_to_all | solution.py:294
  108.7 0.0 copy-done.1
  108.7 0.1 reshape.10
  108.8 0.1 dynamic_slice.3
  108.9 0.1 broadcast_bitcast_fusion
  109.0 0.1 slice_select_fusion
  109.1 0.1 copy.9
  109.2 13.1 %all-gather.5 = bf16[512,256]{1,0:T(8,128)(2,1)S(1)} all-gather(bf16[128,256]{1,0:T(8,128)(2,1)S(1)} %get-tuple-element.16), channel_id=7, replica_groups=mesh['yl'=2,'core'=2,'z'=16,'yh'=2,'x'=4] {'x'}, dimensions={0}, use_global_device_ids=true | all-gather | bytes 327680 | tf_op jit(solution)/shard_map/all_gather | solution.py:295
  122.3 1.5 attend_own.1.state_ref
  123.8 3.2 %all-to-all-done.3.keys_ref = bf16[16,64,128]{2,1,0:T(8,128)(2,1)S(1)} async-done(((bf16[16,64,128]{2,1,0:T(8,128)(2,1)}), bf16[16,64,128]{2,1,0:T(8,128)(2,1)S(1)}, u32[]{:S(2)}, u32[]{:S(2)}) %all-to-all-start.3) | async-done | bytes 262176 | tf_op jit(solution)/shard_map/all_to_all | solution.py:294
  127.1 4.2 %collective-permute-start.2 = (bf16[16,64,128]{2,1,0:T(8,128)(2,1)S(1)}, bf16[16,64,128]{2,1,0:T(8,128)(2,1)S(1)}, u32[]{:S(2)}, u32[]{:S(2)}) collective-permute-start(bf16[16,64,128]{2,1,0:T(8,128)(2,1)S(1)} %all-to-all-done.3.keys_ref), channel_id=1, source_target_pairs={{0,4},{4,0},{1,5},{5,1},{2,6},{6,2},{3,7},{7,3},{8,12},{12,8},{9,1... | collective-permute-start | bytes 786440 | tf_op jit(solution)/shard_map/ppermute | solution.py:306
  131.3 0.1 compare_select_fusion
  131.4 3.6 %attend_more.2.state_ref = f32[4,72,512]{2,1,0:T(8,128)S(1)} custom-call(bf16[4,128,256]{2,1,0:T(8,128)(2,1)S(1)} %bitcast.23, bf16[16,64,128]{2,1,0:T(8,128)(2,1)S(1)} %all-to-all-done.3.keys_ref, f32[16,512]{1,0:T(8,128)S(1)} %get-tuple-element.21.bias_ref, f32[4,72,512]{2,1,0:T(8,128)S(1)} %attend_own.1.state_ref), custom_call_target="tpu_custom_call" | custom-call | flops 536870912 | bytes 2097152 | tf_op jit(solution)/shard_map/attend_more/pallas_call | solution.py:321
  134.9 2.9 %collective-permute-done.2.keys_ref = bf16[16,64,128]{2,1,0:T(8,128)(2,1)S(1)} collective-permute-done((bf16[16,64,128]{2,1,0:T(8,128)(2,1)S(1)}, bf16[16,64,128]{2,1,0:T(8,128)(2,1)S(1)}, u32[]{:S(2)}, u32[]{:S(2)}) %collective-permute-start.2) | collective-permute-done | bytes 262176 | tf_op jit(solution)/shard_map/ppermute | solution.py:306
  137.8 3.6 %attend_more.3 = bf16[4,80,512]{2,1,0:T(8,128)(2,1)S(1)} custom-call(bf16[4,128,256]{2,1,0:T(8,128)(2,1)S(1)} %bitcast.24, bf16[16,64,128]{2,1,0:T(8,128)(2,1)S(1)} %collective-permute-done.2.keys_ref, f32[16,512]{1,0:T(8,128)S(1)} %get-tuple-element.22.bias_ref, f32[4,72,512]{2,1,0:T(8,128)S(1)} %attend_more.2.state_ref), custom_call_target="tpu_custom_call" | custom-call | flops 536870912 | bytes 2097152 | tf_op jit(solution)/shard_map/attend_more/pallas_call | solution.py:321
  141.4 10.1 %all_to_all.26.parts_ref = bf16[4,80,512]{2,1,0:T(8,128)(2,1)} all-to-all(bf16[4,80,512]{2,1,0:T(8,128)(2,1)S(1)} %attend_more.3), channel_id=1, replica_groups=mesh['yl'=2,'core'=2,'z'=16,'yh'=2,'x'=4] {'x'}, dimensions={0} | all-to-all | bytes 655360 | tf_op jit(solution)/shard_map/all_to_all | solution.py:330
  151.5 1.8 %combine.1 = bf16[256,128]{1,0:T(8,128)(2,1)} custom-call(bf16[4,80,512]{2,1,0:T(8,128)(2,1)} %all_to_all.26.parts_ref), custom_call_target="tpu_custom_call" | custom-call | tf_op jit(solution)/shard_map/combine/pallas_call | solution.py:331
  (2 shorter events, 0.0 us)
Async XLA Ops:
  6.5 88.8 %all-gather.8.cloned.1.call-start = ((), (), s32[]{:S(2)}) async-start(), calls=%async_computation.5 | async-start | bytes 3203072 | tf_op jit(solution)/shard_map/all_gather | solution.py:230
  34.4 2.0 %copy-start = (bf16[3,720,720]{2,1,0:T(8,128)(2,1)S(1)}, bf16[3,720,720]{2,1,0:T(8,128)(2,1)}, u32[]{:S(2)}) copy-start(bf16[3,720,720]{2,1,0:T(8,128)(2,1)} %weight_ref.1) | copy-start | bytes 9331204
  55.8 14.8 %all-to-all-start = ((bf16[8,184,256]{2,1,0:T(8,128)(2,1)}), bf16[8,184,256]{2,1,0:T(8,128)(2,1)S(1)}, u32[]{:S(2)}, u32[]{:S(2)}) async-start(bf16[8,184,256]{2,1,0:T(8,128)(2,1)} %get-tuple-element.13), calls=%async_computation | async-start | bytes 1507328 | tf_op jit(solution)/shard_map/all_to_all | solution.py:268
  70.6 13.6 %all-to-all-start.2 = ((bf16[8,184,256]{2,1,0:T(8,128)(2,1)}), bf16[8,184,256]{2,1,0:T(8,128)(2,1)S(1)}, u32[]{:S(2)}, u32[]{:S(2)}) async-start(bf16[8,184,256]{2,1,0:T(8,128)(2,1)} %spread.1), calls=%async_computation.2 | async-start | bytes 1507328 | tf_op jit(solution)/shard_map/all_to_all | solution.py:268
  74.1 34.7 %copy-start.1 = (s32[64]{0:T(128)S(1)}, s32[64]{0:T(128)}, u32[]{:S(2)}) copy-start(s32[64]{0:T(128)} %param.11) | copy-start | bytes 772
  74.1 12.0 %collective-permute-start = (bf16[8,184,256]{2,1,0:T(8,128)(2,1)S(1)}, bf16[8,184,256]{2,1,0:T(8,128)(2,1)S(1)}, u32[]{:S(2)}, u32[]{:S(2)}) collective-permute-start(bf16[8,184,256]{2,1,0:T(8,128)(2,1)S(1)} %all-to-all-done.embed_own), channel_id=1, source_target_pairs={{0,128},{128,0},{1,129},{129,1},{2,130},{130,2},{3,131},{131,3},{4... | collective-permute-start | bytes 2261000 | tf_op jit(solution)/shard_map/ppermute | solution.py:269
  84.2 4.1 %collective-permute-start.1 = (bf16[8,184,256]{2,1,0:T(8,128)(2,1)S(1)}, bf16[8,184,256]{2,1,0:T(8,128)(2,1)S(1)}, u32[]{:S(2)}, u32[]{:S(2)}) collective-permute-start(bf16[8,184,256]{2,1,0:T(8,128)(2,1)S(1)} %all-to-all-done.2.merged_own), channel_id=1, source_target_pairs={{0,128},{128,0},{1,129},{129,1},{2,130},{130,2},{3,131},{131,3},{4... | collective-permute-start | bytes 2261000 | tf_op jit(solution)/shard_map/ppermute | solution.py:269
  100.6 26.5 %all-to-all-start.3 = ((bf16[16,64,128]{2,1,0:T(8,128)(2,1)}), bf16[16,64,128]{2,1,0:T(8,128)(2,1)S(1)}, u32[]{:S(2)}, u32[]{:S(2)}) async-start(bf16[16,64,128]{2,1,0:T(8,128)(2,1)} %get-tuple-element.15), calls=%async_computation.3 | async-start | bytes 524288 | tf_op jit(solution)/shard_map/all_to_all | solution.py:294
  127.1 10.8 %collective-permute-start.2 = (bf16[16,64,128]{2,1,0:T(8,128)(2,1)S(1)}, bf16[16,64,128]{2,1,0:T(8,128)(2,1)S(1)}, u32[]{:S(2)}, u32[]{:S(2)}) collective-permute-start(bf16[16,64,128]{2,1,0:T(8,128)(2,1)S(1)} %all-to-all-done.3.keys_ref), channel_id=1, source_target_pairs={{0,4},{4,0},{1,5},{5,1},{2,6},{6,2},{3,7},{7,3},{8,12},{12,8},{9,1... | collective-permute-start | bytes 786440 | tf_op jit(solution)/shard_map/ppermute | solution.py:306
Sparse Core Ops, SparseCore 0:
  16.6 78.6 all-gather.7

commit v6 on v5

--- a/solution.py
+++ b/solution.py
@@ -61,13 +61,8 @@
     query_ref, sent_ref, own_ref, rows_ref, weights_ref, arrived,
 ):
     core, x_id = place_ref[0], place_ref[1]
-    pieces = arrived.shape[0]
-    count = weights_ref.shape[0] // pieces
-    copies = []
-    for p in range(pieces):
-        span = pl.ds(p * count, count)
-        copies.append(pltpu.make_async_copy(weights_hbm.at[span], weights_ref.at[span], arrived.at[p]))
-        copies[-1].start()
+    copy = pltpu.make_async_copy(weights_hbm, weights_ref, arrived)
+    copy.start()
     chunks = embed_own.shape[0]
     _, chunk, tokens = rows_ref.shape
     width = 2 * chunks * chunk
@@ -86,12 +81,11 @@
                     at = 2 * chunks + (2 * (i % 2) + side) * 4 + i // 2
                 rows_ref[at] = (ref[i, :chunk].astype(jnp.float32) * scale).astype(jnp.bfloat16)
     acc = jnp.zeros((weights_ref.shape[2], tokens), jnp.float32)
-    for p in range(pieces):
-        copies[p].wait()
-        for at in range(p * count, (p + 1) * count):
-            acc = acc + lax.dot_general(
-                weights_ref[at, :chunk], rows_ref[at], DIM0, preferred_element_type=jnp.float32
-            )
+    copy.wait()
+    for at in range(weights_ref.shape[0]):
+        acc = acc + lax.dot_general(
+            weights_ref[at, :chunk], rows_ref[at], DIM0, preferred_element_type=jnp.float32
+        )
     half = acc.shape[0] // 2
     query_ref[...] = acc[:half].astype(jnp.bfloat16)
     rows = acc[half:].T.astype(jnp.bfloat16)
@@ -286,7 +280,7 @@
         scratch_shapes=[
             pltpu.VMEM((n_ctx, chunk, tokens), jnp.bfloat16),
             pltpu.VMEM(weights.shape, weights.dtype),
-            pltpu.SemaphoreType.DMA((4,)),
+            pltpu.SemaphoreType.DMA,
         ],
         compiler_params=pltpu.CompilerParams(vmem_limit_bytes=48 << 20),
         name="project",

time: 161 us -> 160 us (level)
  no operation moved by 1% of the time
where the time goes in v6:
time: 160 us; the launch traced here: 159 us
  blocking collectives  70.6 us (44%)
  waiting for transfers between devices  24.8 us (16%)
  starting transfers between devices  23.2 us (14%)
  Pallas kernels  22.9 us (14%)
  between operations  13.5 us (8%)
  local copies, waits for them, and re-layouts  4.25 us (3%)
    all_to_all x1, blocking collectives, body(): parts = lax.all_to_all(partial, 'x', 0, 0)  16.6 us
    all_gather x1, blocking collectives, body(): queries = lax.all_gather(query, 'x', axis=0)  13.1 us
    all_to_all x1, blocking collectives, body(): parts = lax.all_to_all(parts, 'x', 0, 0)  10.1 us
    all_to_all x2, waiting for transfers between devices, over_x(): own = lax.all_to_all(copies, 'x', 0, 0, tiled=True)  9.44 us
    all_gather x1, blocking collectives, body(): low = lax.all_gather(turned[:split], SEG, axis=0)  8.53 us
    all_gather x1, blocking collectives, body(): weights = lax.all_gather(packed, 'yh', axis=0)  8.38 us
    all_to_all x1, starting transfers between devices, body(): taken = lax.all_to_all(sent, 'z', 0, 0)  8.13 us
    all_gather x1, blocking collectives, body(): high = lax.all_gather(turned[split:], SEG, axis=0)  7.41 us
  transfers between devices with their start and end apart: 7, of which 6 were waited for; matrix products, arithmetic and copies ran while one was open for 2% of the time, Pallas kernels for 7%

profile of v6, /device:TPU:32, one launch (start us, length us, event | category | flops | bytes accessed | tf_op | source)
XLA Modules:
  0.0 159.5 jit_solution(8510055327290317836)
XLA Ops:
  6.5 0.0 all-gather.8.cloned.1.call-start
  6.5 1.6 pack.1
  8.1 8.4 %all-gather.3 = bf16[368,256]{1,0:T(8,128)(2,1)} all-gather(bf16[184,256]{1,0:T(8,128)(2,1)} %pack.1), channel_id=5, replica_groups=mesh['yl'=2,'core'=2,'z'=16,'yh'=2,'x'=4] {'yh'}, dimensions={0}, use_global_device_ids=true | all-gather | bytes 282624 | tf_op jit(solution)/shard_map/all_gather | solution.py:223
  16.5 0.0 all-gather.8.cloned.1.call-update
  16.5 0.9 slice.26
  17.5 0.9 slice.27
  18.4 0.1 pad_add_fusion.place_ref
  18.5 7.4 %all-gather.1 = bf16[1408,256]{1,0:T(8,128)(2,1)S(1)} all-gather(bf16[352,256]{1,0:T(8,128)(2,1)S(1)} %slice.27), channel_id=3, replica_groups=mesh['yl'=2,'core'=2,'z'=16,'yh'=2,'x'=4] {'yl','core'}, dimensions={0}, use_global_device_ids=true | all-gather | bytes 901120 | tf_op jit(solution)/shard_map/all_gather | solution.py:230
  25.9 8.5 %all-gather = bf16[1472,256]{1,0:T(8,128)(2,1)S(1)} all-gather(bf16[368,256]{1,0:T(8,128)(2,1)S(1)} %slice.26), channel_id=2, replica_groups=mesh['yl'=2,'core'=2,'z'=16,'yh'=2,'x'=4] {'yl','core'}, dimensions={0}, use_global_device_ids=true | all-gather | bytes 942080 | tf_op jit(solution)/shard_map/all_gather | solution.py:229
  34.4 0.0 copy-start
  34.4 2.0 %copy-done = bf16[3,720,720]{2,1,0:T(8,128)(2,1)S(1)} copy-done((bf16[3,720,720]{2,1,0:T(8,128)(2,1)S(1)}, bf16[3,720,720]{2,1,0:T(8,128)(2,1)}, u32[]{:S(2)}) %copy-start) | copy-done | bytes 3110424
  36.4 2.7 %merge.1 = (f32[4,180,256]{2,1,0:T(8,128)S(1)}, bf16[8,184,256]{2,1,0:T(8,128)(2,1)}) custom-call(bf16[4,368,256]{2,1,0:T(8,128)(2,1)S(1)} %bitcast.20, bf16[4,352,256]{2,1,0:T(8,128)(2,1)S(1)} %bitcast.21, bf16[3,720,720]{2,1,0:T(8,128)(2,1)S(1)} %copy-done, s32[2]{0:T(128)S(1)} %pad_add_fusion.place_ref), custom_call_target="tpu_custom_call" | custom-call | tf_op jit(solution)/shard_map/merge/pallas_call | solution.py:232
  39.1 16.6 %all_to_all.25.parts_ref = f32[4,180,256]{2,1,0:T(8,128)} all-to-all(f32[4,180,256]{2,1,0:T(8,128)S(1)} %get-tuple-element.14), channel_id=1, replica_groups=mesh['yl'=2,'core'=2,'z'=16,'yh'=2,'x'=4] {'x'}, dimensions={0} | all-to-all | bytes 1474560 | tf_op jit(solution)/shard_map/all_to_all | solution.py:244
  55.8 3.5 %all-to-all-start = ((bf16[8,184,256]{2,1,0:T(8,128)(2,1)}), bf16[8,184,256]{2,1,0:T(8,128)(2,1)S(1)}, u32[]{:S(2)}, u32[]{:S(2)}) async-start(bf16[8,184,256]{2,1,0:T(8,128)(2,1)} %get-tuple-element.13), calls=%async_computation | async-start | bytes 1507328 | tf_op jit(solution)/shard_map/all_to_all | solution.py:262
  59.3 1.8 %settle.1 = bf16[184,256]{1,0:T(8,128)(2,1)} custom-call(f32[4,180,256]{2,1,0:T(8,128)} %all_to_all.25.parts_ref), custom_call_target="tpu_custom_call" | custom-call | tf_op jit(solution)/shard_map/settle/pallas_call | solution.py:245
  61.1 6.4 %all-gather.2 = bf16[368,256]{1,0:T(8,128)(2,1)} all-gather(bf16[184,256]{1,0:T(8,128)(2,1)} %settle.1), channel_id=4, replica_groups=mesh['yl'=2,'core'=2,'z'=16,'yh'=2,'x'=4] {'yl'}, dimensions={0}, use_global_device_ids=true | all-gather | bytes 282624 | tf_op jit(solution)/shard_map/all_gather | solution.py:252
  67.4 1.9 %spread.1 = bf16[8,184,256]{2,1,0:T(8,128)(2,1)} custom-call(bf16[2,184,256]{2,1,0:T(8,128)(2,1)} %bitcast.25), custom_call_target="tpu_custom_call" | custom-call | tf_op jit(solution)/shard_map/spread/pallas_call | solution.py:253
  69.3 1.3 all-to-all-done.embed_own
  70.6 3.5 %all-to-all-start.2 = ((bf16[8,184,256]{2,1,0:T(8,128)(2,1)}), bf16[8,184,256]{2,1,0:T(8,128)(2,1)S(1)}, u32[]{:S(2)}, u32[]{:S(2)}) async-start(bf16[8,184,256]{2,1,0:T(8,128)(2,1)} %spread.1), calls=%async_computation.2 | async-start | bytes 1507328 | tf_op jit(solution)/shard_map/all_to_all | solution.py:262
  74.1 0.0 copy-start.1
  74.1 1.9 %collective-permute-start = (bf16[8,184,256]{2,1,0:T(8,128)(2,1)S(1)}, bf16[8,184,256]{2,1,0:T(8,128)(2,1)S(1)}, u32[]{:S(2)}, u32[]{:S(2)}) collective-permute-start(bf16[8,184,256]{2,1,0:T(8,128)(2,1)S(1)} %all-to-all-done.embed_own), channel_id=1, source_target_pairs={{0,128},{128,0},{1,129},{129,1},{2,130},{130,2},{3,131},{131,3},{4... | collective-permute-start | bytes 2261000 | tf_op jit(solution)/shard_map/ppermute | solution.py:263
  76.0 8.2 %all-to-all-done.2.merged_own = bf16[8,184,256]{2,1,0:T(8,128)(2,1)S(1)} async-done(((bf16[8,184,256]{2,1,0:T(8,128)(2,1)}), bf16[8,184,256]{2,1,0:T(8,128)(2,1)S(1)}, u32[]{:S(2)}, u32[]{:S(2)}) %all-to-all-start.2) | async-done | bytes 753696 | tf_op jit(solution)/shard_map/all_to_all | solution.py:262
  84.2 1.9 %collective-permute-start.1 = (bf16[8,184,256]{2,1,0:T(8,128)(2,1)S(1)}, bf16[8,184,256]{2,1,0:T(8,128)(2,1)S(1)}, u32[]{:S(2)}, u32[]{:S(2)}) collective-permute-start(bf16[8,184,256]{2,1,0:T(8,128)(2,1)S(1)} %all-to-all-done.2.merged_own), channel_id=1, source_target_pairs={{0,128},{128,0},{1,129},{129,1},{2,130},{130,2},{3,131},{131,3},{4... | collective-permute-start | bytes 2261000 | tf_op jit(solution)/shard_map/ppermute | solution.py:263
  86.1 0.0 collective-permute-done.embed_other
  86.1 2.2 %collective-permute-done.1.merged_other = bf16[8,184,256]{2,1,0:T(8,128)(2,1)S(1)} collective-permute-done((bf16[8,184,256]{2,1,0:T(8,128)(2,1)S(1)}, bf16[8,184,256]{2,1,0:T(8,128)(2,1)S(1)}, u32[]{:S(2)}, u32[]{:S(2)}) %collective-permute-start.1) | collective-permute-done | bytes 753696 | tf_op jit(solution)/shard_map/ppermute | solution.py:263
  88.3 7.1 %all-gather.8.cloned.1.call-done.weights_hbm = bf16[32,184,256]{2,1,0:T(8,128)(2,1)} async-done(((bf16[2,184,256]{2,1,0:T(8,128)(2,1)}), bf16[32,184,256]{2,1,0:T(8,128)(2,1)}) %all-gather.8.cloned.1.call-update) | async-done | bytes 3014672 | tf_op jit(solution)/shard_map/all_gather | solution.py:224
  95.4 4.5 %project.1 = (bf16[128,256]{1,0:T(8,128)(2,1)S(1)}, bf16[16,64,128]{2,1,0:T(8,128)(2,1)}, bf16[64,128]{1,0:T(8,128)(2,1)S(1)}) custom-call(bf16[8,184,256]{2,1,0:T(8,128)(2,1)S(1)} %all-to-all-done.embed_own, bf16[8,184,256]{2,1,0:T(8,128)(2,1)S(1)} %collective-permute-done.embed_other, bf16[8,184,256]{2,1,0:T(8,128)(2,1)S(1)} %all-to-all-done.2.merged_own, ...), custom_call_target="tpu_custom_call" | custom-call | tf_op jit(solution)/shard_map/project/pallas_call | solution.py:271
  99.9 8.1 %all-to-all-start.3 = ((bf16[16,64,128]{2,1,0:T(8,128)(2,1)}), bf16[16,64,128]{2,1,0:T(8,128)(2,1)S(1)}, u32[]{:S(2)}, u32[]{:S(2)}) async-start(bf16[16,64,128]{2,1,0:T(8,128)(2,1)} %get-tuple-element.15), calls=%async_computation.3 | async-start | bytes 524288 | tf_op jit(solution)/shard_map/all_to_all | solution.py:288
  108.0 0.0 copy-done.1
  108.1 0.1 reshape.10
  108.2 0.1 dynamic_slice.3
  108.3 0.1 broadcast_bitcast_fusion
  108.3 0.1 slice_select_fusion
  108.4 0.1 copy.9
  108.5 13.1 %all-gather.5 = bf16[512,256]{1,0:T(8,128)(2,1)S(1)} all-gather(bf16[128,256]{1,0:T(8,128)(2,1)S(1)} %get-tuple-element.16), channel_id=7, replica_groups=mesh['yl'=2,'core'=2,'z'=16,'yh'=2,'x'=4] {'x'}, dimensions={0}, use_global_device_ids=true | all-gather | bytes 327680 | tf_op jit(solution)/shard_map/all_gather | solution.py:289
  121.6 1.5 attend_own.1.state_ref
  123.2 3.2 %all-to-all-done.3.keys_ref = bf16[16,64,128]{2,1,0:T(8,128)(2,1)S(1)} async-done(((bf16[16,64,128]{2,1,0:T(8,128)(2,1)}), bf16[16,64,128]{2,1,0:T(8,128)(2,1)S(1)}, u32[]{:S(2)}, u32[]{:S(2)}) %all-to-all-start.3) | async-done | bytes 262176 | tf_op jit(solution)/shard_map/all_to_all | solution.py:288
  126.4 4.2 %collective-permute-start.2 = (bf16[16,64,128]{2,1,0:T(8,128)(2,1)S(1)}, bf16[16,64,128]{2,1,0:T(8,128)(2,1)S(1)}, u32[]{:S(2)}, u32[]{:S(2)}) collective-permute-start(bf16[16,64,128]{2,1,0:T(8,128)(2,1)S(1)} %all-to-all-done.3.keys_ref), channel_id=1, source_target_pairs={{0,4},{4,0},{1,5},{5,1},{2,6},{6,2},{3,7},{7,3},{8,12},{12,8},{9,1... | collective-permute-start | bytes 786440 | tf_op jit(solution)/shard_map/ppermute | solution.py:300
  130.6 0.1 compare_select_fusion
  130.7 3.6 %attend_more.2.state_ref = f32[4,72,512]{2,1,0:T(8,128)S(1)} custom-call(bf16[4,128,256]{2,1,0:T(8,128)(2,1)S(1)} %bitcast.23, bf16[16,64,128]{2,1,0:T(8,128)(2,1)S(1)} %all-to-all-done.3.keys_ref, f32[16,512]{1,0:T(8,128)S(1)} %get-tuple-element.21.bias_ref, f32[4,72,512]{2,1,0:T(8,128)S(1)} %attend_own.1.state_ref), custom_call_target="tpu_custom_call" | custom-call | flops 536870912 | bytes 2097152 | tf_op jit(solution)/shard_map/attend_more/pallas_call | solution.py:315
  134.3 2.9 %collective-permute-done.2.keys_ref = bf16[16,64,128]{2,1,0:T(8,128)(2,1)S(1)} collective-permute-done((bf16[16,64,128]{2,1,0:T(8,128)(2,1)S(1)}, bf16[16,64,128]{2,1,0:T(8,128)(2,1)S(1)}, u32[]{:S(2)}, u32[]{:S(2)}) %collective-permute-start.2) | collective-permute-done | bytes 262176 | tf_op jit(solution)/shard_map/ppermute | solution.py:300
  137.2 3.6 %attend_more.3 = bf16[4,80,512]{2,1,0:T(8,128)(2,1)S(1)} custom-call(bf16[4,128,256]{2,1,0:T(8,128)(2,1)S(1)} %bitcast.24, bf16[16,64,128]{2,1,0:T(8,128)(2,1)S(1)} %collective-permute-done.2.keys_ref, f32[16,512]{1,0:T(8,128)S(1)} %get-tuple-element.22.bias_ref, f32[4,72,512]{2,1,0:T(8,128)S(1)} %attend_more.2.state_ref), custom_call_target="tpu_custom_call" | custom-call | flops 536870912 | bytes 2097152 | tf_op jit(solution)/shard_map/attend_more/pallas_call | solution.py:315
  140.8 10.1 %all_to_all.26.parts_ref = bf16[4,80,512]{2,1,0:T(8,128)(2,1)} all-to-all(bf16[4,80,512]{2,1,0:T(8,128)(2,1)S(1)} %attend_more.3), channel_id=1, replica_groups=mesh['yl'=2,'core'=2,'z'=16,'yh'=2,'x'=4] {'x'}, dimensions={0} | all-to-all | bytes 655360 | tf_op jit(solution)/shard_map/all_to_all | solution.py:324
  150.9 1.8 %combine.1 = bf16[256,128]{1,0:T(8,128)(2,1)} custom-call(bf16[4,80,512]{2,1,0:T(8,128)(2,1)} %all_to_all.26.parts_ref), custom_call_target="tpu_custom_call" | custom-call | tf_op jit(solution)/shard_map/combine/pallas_call | solution.py:325
  (2 shorter events, 0.0 us)
Async XLA Ops:
  6.5 88.8 %all-gather.8.cloned.1.call-start = ((), (), s32[]{:S(2)}) async-start(), calls=%async_computation.5 | async-start | bytes 3203072 | tf_op jit(solution)/shard_map/all_gather | solution.py:224
  34.4 2.0 %copy-start = (bf16[3,720,720]{2,1,0:T(8,128)(2,1)S(1)}, bf16[3,720,720]{2,1,0:T(8,128)(2,1)}, u32[]{:S(2)}) copy-start(bf16[3,720,720]{2,1,0:T(8,128)(2,1)} %weight_ref.1) | copy-start | bytes 9331204
  55.8 14.8 %all-to-all-start = ((bf16[8,184,256]{2,1,0:T(8,128)(2,1)}), bf16[8,184,256]{2,1,0:T(8,128)(2,1)S(1)}, u32[]{:S(2)}, u32[]{:S(2)}) async-start(bf16[8,184,256]{2,1,0:T(8,128)(2,1)} %get-tuple-element.13), calls=%async_computation | async-start | bytes 1507328 | tf_op jit(solution)/shard_map/all_to_all | solution.py:262
  70.6 13.6 %all-to-all-start.2 = ((bf16[8,184,256]{2,1,0:T(8,128)(2,1)}), bf16[8,184,256]{2,1,0:T(8,128)(2,1)S(1)}, u32[]{:S(2)}, u32[]{:S(2)}) async-start(bf16[8,184,256]{2,1,0:T(8,128)(2,1)} %spread.1), calls=%async_computation.2 | async-start | bytes 1507328 | tf_op jit(solution)/shard_map/all_to_all | solution.py:262
  74.1 34.0 %copy-start.1 = (s32[64]{0:T(128)S(1)}, s32[64]{0:T(128)}, u32[]{:S(2)}) copy-start(s32[64]{0:T(128)} %param.11) | copy-start | bytes 772
  74.1 12.0 %collective-permute-start = (bf16[8,184,256]{2,1,0:T(8,128)(2,1)S(1)}, bf16[8,184,256]{2,1,0:T(8,128)(2,1)S(1)}, u32[]{:S(2)}, u32[]{:S(2)}) collective-permute-start(bf16[8,184,256]{2,1,0:T(8,128)(2,1)S(1)} %all-to-all-done.embed_own), channel_id=1, source_target_pairs={{0,128},{128,0},{1,129},{129,1},{2,130},{130,2},{3,131},{131,3},{4... | collective-permute-start | bytes 2261000 | tf_op jit(solution)/shard_map/ppermute | solution.py:263
  84.2 4.1 %collective-permute-start.1 = (bf16[8,184,256]{2,1,0:T(8,128)(2,1)S(1)}, bf16[8,184,256]{2,1,0:T(8,128)(2,1)S(1)}, u32[]{:S(2)}, u32[]{:S(2)}) collective-permute-start(bf16[8,184,256]{2,1,0:T(8,128)(2,1)S(1)} %all-to-all-done.2.merged_own), channel_id=1, source_target_pairs={{0,128},{128,0},{1,129},{129,1},{2,130},{130,2},{3,131},{131,3},{4... | collective-permute-start | bytes 2261000 | tf_op jit(solution)/shard_map/ppermute | solution.py:263
  99.9 26.5 %all-to-all-start.3 = ((bf16[16,64,128]{2,1,0:T(8,128)(2,1)}), bf16[16,64,128]{2,1,0:T(8,128)(2,1)S(1)}, u32[]{:S(2)}, u32[]{:S(2)}) async-start(bf16[16,64,128]{2,1,0:T(8,128)(2,1)} %get-tuple-element.15), calls=%async_computation.3 | async-start | bytes 524288 | tf_op jit(solution)/shard_map/all_to_all | solution.py:288
  126.4 10.8 %collective-permute-start.2 = (bf16[16,64,128]{2,1,0:T(8,128)(2,1)S(1)}, bf16[16,64,128]{2,1,0:T(8,128)(2,1)S(1)}, u32[]{:S(2)}, u32[]{:S(2)}) collective-permute-start(bf16[16,64,128]{2,1,0:T(8,128)(2,1)S(1)} %all-to-all-done.3.keys_ref), channel_id=1, source_target_pairs={{0,4},{4,0},{1,5},{5,1},{2,6},{6,2},{3,7},{7,3},{8,12},{12,8},{9,1... | collective-permute-start | bytes 786440 | tf_op jit(solution)/shard_map/ppermute | solution.py:300
Sparse Core Ops, SparseCore 0:
  16.6 78.6 all-gather.7

commit v7 on v6

--- a/solution.py
+++ b/solution.py
@@ -16,12 +16,23 @@
 def pack_kernel(query_ref, key_ref, value_ref, out_ref):
     turned = jnp.concatenate([key_ref[...], value_ref[...]], axis=0).astype(jnp.float32)
     chunk = query_ref.shape[0]
-    out_ref[...] = jnp.zeros_like(out_ref)
+    whole = chunk // 16 * 16
+    out_ref[whole:] = jnp.zeros((out_ref.shape[0] - whole, out_ref.shape[1]), out_ref.dtype)
     out_ref[:chunk, : query_ref.shape[1]] = query_ref[...]
     out_ref[:chunk, query_ref.shape[1] :] = turned.T.astype(jnp.bfloat16)
 
 
-def merge_kernel(low_ref, high_ref, weight_ref, place_ref, partial_ref, embed_ref, hold_ref):
+def split_kernel(rows_ref, low_ref, high_ref):
+    split = low_ref.shape[0]
+    low_ref[...] = rows_ref[:split]
+    high_ref[...] = rows_ref[split:]
+
+
+def merge_kernel(low_ref, high_ref, weight_hbm, place_ref, partial_ref, embed_ref, hold_ref, weight_ref, arrived):
+    copies = []
+    for k in range(3):
+        copies.append(pltpu.make_async_copy(weight_hbm.at[k], weight_ref.at[k], arrived.at[k]))
+        copies[-1].start()
     split, total = low_ref.shape[1], weight_ref.shape[1]
     chunks, chunk, _ = partial_ref.shape
     hold_ref[:split] = low_ref[3].astype(jnp.float32)
@@ -34,6 +45,7 @@
             embed_ref[2 * i + half, :chunk] = block
     acc = None
     for k in range(3):
+        copies[k].wait()
         for ref, rows in ((low_ref, slice(0, split)), (high_ref, slice(split, total))):
             term = lax.dot_general(weight_ref[k, rows, :], ref[k], DIM0, preferred_element_type=jnp.float32)
             acc = term if acc is None else acc + term
@@ -226,8 +238,15 @@
 
     turned = hidden[0].T
     split = (features // 2 + 15) // 16 * 16
-    low = lax.all_gather(turned[:split], SEG, axis=0)
-    high = lax.all_gather(turned[split:], SEG, axis=0)
+    low, high = pl.pallas_call(
+        split_kernel,
+        out_shape=tuple(jax.ShapeDtypeStruct((n, tokens), turned.dtype) for n in (split, features - split)),
+        in_specs=[VMEM],
+        out_specs=(VMEM, VMEM),
+        name="split",
+    )(turned)
+    low = lax.all_gather(low, SEG, axis=0)
+    high = lax.all_gather(high, SEG, axis=0)
 
     partial, embed = pl.pallas_call(
         merge_kernel,
@@ -235,10 +254,14 @@
             jax.ShapeDtypeStruct((n_x, chunk, tokens), jnp.float32),
             jax.ShapeDtypeStruct((2 * n_x, padded, tokens), jnp.bfloat16),
         ),
-        in_specs=[VMEM] * 3 + [smem],
+        in_specs=[VMEM, VMEM, hbm, smem],
         out_specs=(VMEM, VMEM),
-        scratch_shapes=[pltpu.VMEM((features, tokens), jnp.float32)],
-        compiler_params=pltpu.CompilerParams(vmem_limit_bytes=40 << 20),
+        scratch_shapes=[
+            pltpu.VMEM((features, tokens), jnp.float32),
+            pltpu.VMEM(merge_weight.shape, merge_weight.dtype),
+            pltpu.SemaphoreType.DMA((3,)),
+        ],
+        compiler_params=pltpu.CompilerParams(vmem_limit_bytes=50 << 20),
         name="merge",
     )(low, high, merge_weight, place)
     parts = lax.all_to_all(partial, "x", 0, 0)

time: 160 us -> 160 us (level)
  local copies, waits for them, and re-layouts: 4.25 us -> 0.37 us
  Pallas kernels: 22.9 us -> 26.1 us
    unnamed x6 -> x4, local copies, waits for them, and re-layouts: 2.09 us -> 0.08 us
    slice x2 -> x0, local copies, waits for them, and re-layouts: 1.88 us -> none  [the longest x1 0.94 us: body(): low = lax.all_gather(turned[:split], SEG, axis=0)]
    pallas_call x0 -> x1, Pallas kernels: none -> 1.76 us  [body(): pl.pallas_call(split_kernel, out_shape=tuple((jax.ShapeDtypeStruct((n, to...]
  transfers between devices with their start and end apart: 7 -> 7, of which waited for: 6 -> 6; matrix products, arithmetic and copies ran while one was open for 2% -> 0% of each run, Pallas kernels for 7% -> 9%
where the time goes in v7:
time: 160 us; the launch traced here: 159 us
  blocking collectives  71 us (44%)
  Pallas kernels  26.1 us (16%)
  waiting for transfers between devices  24.6 us (15%)
  starting transfers between devices  23.5 us (15%)
  between operations  13.5 us (8%)
    all_to_all x1, blocking collectives, body(): parts = lax.all_to_all(partial, 'x', 0, 0)  16.6 us
    all_gather x1, blocking collectives, body(): queries = lax.all_gather(query, 'x', axis=0)  13.2 us
    all_to_all x1, blocking collectives, body(): parts = lax.all_to_all(parts, 'x', 0, 0)  10.1 us
    all_to_all x2, waiting for transfers between devices, over_x(): own = lax.all_to_all(copies, 'x', 0, 0, tiled=True)  9.31 us
    all_gather x1, blocking collectives, body(): low = lax.all_gather(low, SEG, axis=0)  8.74 us
    all_gather x1, blocking collectives, body(): weights = lax.all_gather(packed, 'yh', axis=0)  8.38 us
    all_to_all x1, starting transfers between devices, body(): taken = lax.all_to_all(sent, 'z', 0, 0)  7.94 us
    all_gather x1, blocking collectives, body(): high = lax.all_gather(high, SEG, axis=0)  7.62 us
  transfers between devices with their start and end apart: 7, of which 6 were waited for; matrix products, arithmetic and copies ran while one was open for 0% of the time, Pallas kernels for 9%

profile of v7, /device:TPU:32, one launch (start us, length us, event | category | flops | bytes accessed | tf_op | source)
XLA Modules:
  0.0 159.3 jit_solution(17426589222003586828)
XLA Ops:
  6.5 0.0 all-gather.8.cloned.1.call-start
  6.5 1.6 pack.1
  8.1 8.4 %all-gather.3 = bf16[368,256]{1,0:T(8,128)(2,1)} all-gather(bf16[184,256]{1,0:T(8,128)(2,1)} %pack.1), channel_id=5, replica_groups=mesh['yl'=2,'core'=2,'z'=16,'yh'=2,'x'=4] {'yh'}, dimensions={0}, use_global_device_ids=true | all-gather | bytes 282624 | tf_op jit(solution)/shard_map/all_gather | solution.py:235
  16.5 0.0 all-gather.8.cloned.1.call-update
  16.5 1.8 %split.1 = (bf16[368,256]{1,0:T(8,128)(2,1)}, bf16[352,256]{1,0:T(8,128)(2,1)}) custom-call(bf16[720,256]{1,0:T(8,128)(2,1)} %bitcast.27), custom_call_target="tpu_custom_call" | custom-call | tf_op jit(solution)/shard_map/split/pallas_call | solution.py:241
  18.3 0.1 pad_add_fusion.place_ref
  18.4 7.6 %all-gather.1 = bf16[1408,256]{1,0:T(8,128)(2,1)S(1)} all-gather(bf16[352,256]{1,0:T(8,128)(2,1)} %get-tuple-element.16), channel_id=3, replica_groups=mesh['yl'=2,'core'=2,'z'=16,'yh'=2,'x'=4] {'yl','core'}, dimensions={0}, use_global_device_ids=true | all-gather | bytes 901120 | tf_op jit(solution)/shard_map/all_gather | solution.py:249
  26.0 8.7 %all-gather = bf16[1472,256]{1,0:T(8,128)(2,1)S(1)} all-gather(bf16[368,256]{1,0:T(8,128)(2,1)} %get-tuple-element.15), channel_id=2, replica_groups=mesh['yl'=2,'core'=2,'z'=16,'yh'=2,'x'=4] {'yl','core'}, dimensions={0}, use_global_device_ids=true | all-gather | bytes 942080 | tf_op jit(solution)/shard_map/all_gather | solution.py:248
  34.7 4.2 %merge.1 = (f32[4,180,256]{2,1,0:T(8,128)S(1)}, bf16[8,184,256]{2,1,0:T(8,128)(2,1)}) custom-call(bf16[4,368,256]{2,1,0:T(8,128)(2,1)S(1)} %bitcast.20, bf16[4,352,256]{2,1,0:T(8,128)(2,1)S(1)} %bitcast.21, bf16[3,720,720]{2,1,0:T(8,128)(2,1)} %weight_hbm.1, s32[2]{0:T(128)S(1)} %pad_add_fusion.place_ref), custom_call_target="tpu_custom_call" | custom-call | tf_op jit(solution)/shard_map/merge/pallas_call | solution.py:251
  38.9 16.6 %all_to_all.25.parts_ref = f32[4,180,256]{2,1,0:T(8,128)} all-to-all(f32[4,180,256]{2,1,0:T(8,128)S(1)} %get-tuple-element.18), channel_id=1, replica_groups=mesh['yl'=2,'core'=2,'z'=16,'yh'=2,'x'=4] {'x'}, dimensions={0} | all-to-all | bytes 1474560 | tf_op jit(solution)/shard_map/all_to_all | solution.py:267
  55.5 3.5 %all-to-all-start = ((bf16[8,184,256]{2,1,0:T(8,128)(2,1)}), bf16[8,184,256]{2,1,0:T(8,128)(2,1)S(1)}, u32[]{:S(2)}, u32[]{:S(2)}) async-start(bf16[8,184,256]{2,1,0:T(8,128)(2,1)} %get-tuple-element.17), calls=%async_computation | async-start | bytes 1507328 | tf_op jit(solution)/shard_map/all_to_all | solution.py:285
  59.0 1.8 %settle.1 = bf16[184,256]{1,0:T(8,128)(2,1)} custom-call(f32[4,180,256]{2,1,0:T(8,128)} %all_to_all.25.parts_ref), custom_call_target="tpu_custom_call" | custom-call | tf_op jit(solution)/shard_map/settle/pallas_call | solution.py:268
  60.8 6.4 %all-gather.2 = bf16[368,256]{1,0:T(8,128)(2,1)} all-gather(bf16[184,256]{1,0:T(8,128)(2,1)} %settle.1), channel_id=4, replica_groups=mesh['yl'=2,'core'=2,'z'=16,'yh'=2,'x'=4] {'yl'}, dimensions={0}, use_global_device_ids=true | all-gather | bytes 282624 | tf_op jit(solution)/shard_map/all_gather | solution.py:275
  67.2 1.8 %spread.1 = bf16[8,184,256]{2,1,0:T(8,128)(2,1)} custom-call(bf16[2,184,256]{2,1,0:T(8,128)(2,1)} %bitcast.25), custom_call_target="tpu_custom_call" | custom-call | tf_op jit(solution)/shard_map/spread/pallas_call | solution.py:276
  69.0 1.2 all-to-all-done.embed_own
  70.3 3.5 %all-to-all-start.2 = ((bf16[8,184,256]{2,1,0:T(8,128)(2,1)}), bf16[8,184,256]{2,1,0:T(8,128)(2,1)S(1)}, u32[]{:S(2)}, u32[]{:S(2)}) async-start(bf16[8,184,256]{2,1,0:T(8,128)(2,1)} %spread.1), calls=%async_computation.2 | async-start | bytes 1507328 | tf_op jit(solution)/shard_map/all_to_all | solution.py:285
  73.8 0.0 copy-start
  73.8 2.0 %collective-permute-start = (bf16[8,184,256]{2,1,0:T(8,128)(2,1)S(1)}, bf16[8,184,256]{2,1,0:T(8,128)(2,1)S(1)}, u32[]{:S(2)}, u32[]{:S(2)}) collective-permute-start(bf16[8,184,256]{2,1,0:T(8,128)(2,1)S(1)} %all-to-all-done.embed_own), channel_id=1, source_target_pairs={{0,128},{128,0},{1,129},{129,1},{2,130},{130,2},{3,131},{131,3},{4... | collective-permute-start | bytes 2261000 | tf_op jit(solution)/shard_map/ppermute | solution.py:286
  75.8 8.1 %all-to-all-done.2.merged_own = bf16[8,184,256]{2,1,0:T(8,128)(2,1)S(1)} async-done(((bf16[8,184,256]{2,1,0:T(8,128)(2,1)}), bf16[8,184,256]{2,1,0:T(8,128)(2,1)S(1)}, u32[]{:S(2)}, u32[]{:S(2)}) %all-to-all-start.2) | async-done | bytes 753696 | tf_op jit(solution)/shard_map/all_to_all | solution.py:285
  83.9 1.9 %collective-permute-start.1 = (bf16[8,184,256]{2,1,0:T(8,128)(2,1)S(1)}, bf16[8,184,256]{2,1,0:T(8,128)(2,1)S(1)}, u32[]{:S(2)}, u32[]{:S(2)}) collective-permute-start(bf16[8,184,256]{2,1,0:T(8,128)(2,1)S(1)} %all-to-all-done.2.merged_own), channel_id=1, source_target_pairs={{0,128},{128,0},{1,129},{129,1},{2,130},{130,2},{3,131},{131,3},{4... | collective-permute-start | bytes 2261000 | tf_op jit(solution)/shard_map/ppermute | solution.py:286
  85.8 0.0 collective-permute-done.embed_other
  85.9 2.2 %collective-permute-done.1.merged_other = bf16[8,184,256]{2,1,0:T(8,128)(2,1)S(1)} collective-permute-done((bf16[8,184,256]{2,1,0:T(8,128)(2,1)S(1)}, bf16[8,184,256]{2,1,0:T(8,128)(2,1)S(1)}, u32[]{:S(2)}, u32[]{:S(2)}) %collective-permute-start.1) | collective-permute-done | bytes 753696 | tf_op jit(solution)/shard_map/ppermute | solution.py:286
  88.0 7.3 %all-gather.8.cloned.1.call-done.weights_hbm = bf16[32,184,256]{2,1,0:T(8,128)(2,1)} async-done(((bf16[2,184,256]{2,1,0:T(8,128)(2,1)}), bf16[32,184,256]{2,1,0:T(8,128)(2,1)}) %all-gather.8.cloned.1.call-update) | async-done | bytes 3014672 | tf_op jit(solution)/shard_map/all_gather | solution.py:236
  95.4 4.5 %project.1 = (bf16[128,256]{1,0:T(8,128)(2,1)S(1)}, bf16[16,64,128]{2,1,0:T(8,128)(2,1)}, bf16[64,128]{1,0:T(8,128)(2,1)S(1)}) custom-call(bf16[8,184,256]{2,1,0:T(8,128)(2,1)S(1)} %all-to-all-done.embed_own, bf16[8,184,256]{2,1,0:T(8,128)(2,1)S(1)} %collective-permute-done.embed_other, bf16[8,184,256]{2,1,0:T(8,128)(2,1)S(1)} %all-to-all-done.2.merged_own, ...), custom_call_target="tpu_custom_call" | custom-call | tf_op jit(solution)/shard_map/project/pallas_call | solution.py:294
  99.9 7.9 %all-to-all-start.3 = ((bf16[16,64,128]{2,1,0:T(8,128)(2,1)}), bf16[16,64,128]{2,1,0:T(8,128)(2,1)S(1)}, u32[]{:S(2)}, u32[]{:S(2)}) async-start(bf16[16,64,128]{2,1,0:T(8,128)(2,1)} %get-tuple-element.19), calls=%async_computation.3 | async-start | bytes 524288 | tf_op jit(solution)/shard_map/all_to_all | solution.py:311
  107.9 0.0 copy-done
  107.9 0.1 reshape.10
  108.0 0.1 dynamic_slice.3
  108.1 0.1 broadcast_bitcast_fusion
  108.1 0.1 slice_select_fusion
  108.2 0.1 copy.9
  108.3 13.2 %all-gather.5 = bf16[512,256]{1,0:T(8,128)(2,1)S(1)} all-gather(bf16[128,256]{1,0:T(8,128)(2,1)S(1)} %get-tuple-element.20), channel_id=7, replica_groups=mesh['yl'=2,'core'=2,'z'=16,'yh'=2,'x'=4] {'x'}, dimensions={0}, use_global_device_ids=true | all-gather | bytes 327680 | tf_op jit(solution)/shard_map/all_gather | solution.py:312
  121.5 1.5 attend_own.1.state_ref
  123.0 3.2 %all-to-all-done.3.keys_ref = bf16[16,64,128]{2,1,0:T(8,128)(2,1)S(1)} async-done(((bf16[16,64,128]{2,1,0:T(8,128)(2,1)}), bf16[16,64,128]{2,1,0:T(8,128)(2,1)S(1)}, u32[]{:S(2)}, u32[]{:S(2)}) %all-to-all-start.3) | async-done | bytes 262176 | tf_op jit(solution)/shard_map/all_to_all | solution.py:311
  126.2 4.6 %collective-permute-start.2 = (bf16[16,64,128]{2,1,0:T(8,128)(2,1)S(1)}, bf16[16,64,128]{2,1,0:T(8,128)(2,1)S(1)}, u32[]{:S(2)}, u32[]{:S(2)}) collective-permute-start(bf16[16,64,128]{2,1,0:T(8,128)(2,1)S(1)} %all-to-all-done.3.keys_ref), channel_id=1, source_target_pairs={{0,4},{4,0},{1,5},{5,1},{2,6},{6,2},{3,7},{7,3},{8,12},{12,8},{9,1... | collective-permute-start | bytes 786440 | tf_op jit(solution)/shard_map/ppermute | solution.py:323
  130.8 0.1 compare_select_fusion
  130.9 3.6 %attend_more.2.state_ref = f32[4,72,512]{2,1,0:T(8,128)S(1)} custom-call(bf16[4,128,256]{2,1,0:T(8,128)(2,1)S(1)} %bitcast.23, bf16[16,64,128]{2,1,0:T(8,128)(2,1)S(1)} %all-to-all-done.3.keys_ref, f32[16,512]{1,0:T(8,128)S(1)} %get-tuple-element.25.bias_ref, f32[4,72,512]{2,1,0:T(8,128)S(1)} %attend_own.1.state_ref), custom_call_target="tpu_custom_call" | custom-call | flops 536870912 | bytes 2097152 | tf_op jit(solution)/shard_map/attend_more/pallas_call | solution.py:338
  134.5 2.5 %collective-permute-done.2.keys_ref = bf16[16,64,128]{2,1,0:T(8,128)(2,1)S(1)} collective-permute-done((bf16[16,64,128]{2,1,0:T(8,128)(2,1)S(1)}, bf16[16,64,128]{2,1,0:T(8,128)(2,1)S(1)}, u32[]{:S(2)}, u32[]{:S(2)}) %collective-permute-start.2) | collective-permute-done | bytes 262176 | tf_op jit(solution)/shard_map/ppermute | solution.py:323
  137.0 3.6 %attend_more.3 = bf16[4,80,512]{2,1,0:T(8,128)(2,1)S(1)} custom-call(bf16[4,128,256]{2,1,0:T(8,128)(2,1)S(1)} %bitcast.24, bf16[16,64,128]{2,1,0:T(8,128)(2,1)S(1)} %collective-permute-done.2.keys_ref, f32[16,512]{1,0:T(8,128)S(1)} %get-tuple-element.26.bias_ref, f32[4,72,512]{2,1,0:T(8,128)S(1)} %attend_more.2.state_ref), custom_call_target="tpu_custom_call" | custom-call | flops 536870912 | bytes 2097152 | tf_op jit(solution)/shard_map/attend_more/pallas_call | solution.py:338
  140.6 10.1 %all_to_all.26.parts_ref = bf16[4,80,512]{2,1,0:T(8,128)(2,1)} all-to-all(bf16[4,80,512]{2,1,0:T(8,128)(2,1)S(1)} %attend_more.3), channel_id=1, replica_groups=mesh['yl'=2,'core'=2,'z'=16,'yh'=2,'x'=4] {'x'}, dimensions={0} | all-to-all | bytes 655360 | tf_op jit(solution)/shard_map/all_to_all | solution.py:347
  150.7 1.8 %combine.1 = bf16[256,128]{1,0:T(8,128)(2,1)} custom-call(bf16[4,80,512]{2,1,0:T(8,128)(2,1)} %all_to_all.26.parts_ref), custom_call_target="tpu_custom_call" | custom-call | tf_op jit(solution)/shard_map/combine/pallas_call | solution.py:348
  (2 shorter events, 0.0 us)
Async XLA Ops:
  6.5 88.8 %all-gather.8.cloned.1.call-start = ((), (), s32[]{:S(2)}) async-start(), calls=%async_computation.5 | async-start | bytes 3203072 | tf_op jit(solution)/shard_map/all_gather | solution.py:236
  55.5 14.8 %all-to-all-start = ((bf16[8,184,256]{2,1,0:T(8,128)(2,1)}), bf16[8,184,256]{2,1,0:T(8,128)(2,1)S(1)}, u32[]{:S(2)}, u32[]{:S(2)}) async-start(bf16[8,184,256]{2,1,0:T(8,128)(2,1)} %get-tuple-element.17), calls=%async_computation | async-start | bytes 1507328 | tf_op jit(solution)/shard_map/all_to_all | solution.py:285
  70.3 13.7 %all-to-all-start.2 = ((bf16[8,184,256]{2,1,0:T(8,128)(2,1)}), bf16[8,184,256]{2,1,0:T(8,128)(2,1)S(1)}, u32[]{:S(2)}, u32[]{:S(2)}) async-start(bf16[8,184,256]{2,1,0:T(8,128)(2,1)} %spread.1), calls=%async_computation.2 | async-start | bytes 1507328 | tf_op jit(solution)/shard_map/all_to_all | solution.py:285
  73.8 34.1 %copy-start = (s32[64]{0:T(128)S(1)}, s32[64]{0:T(128)}, u32[]{:S(2)}) copy-start(s32[64]{0:T(128)} %param.11) | copy-start | bytes 772
  73.8 12.1 %collective-permute-start = (bf16[8,184,256]{2,1,0:T(8,128)(2,1)S(1)}, bf16[8,184,256]{2,1,0:T(8,128)(2,1)S(1)}, u32[]{:S(2)}, u32[]{:S(2)}) collective-permute-start(bf16[8,184,256]{2,1,0:T(8,128)(2,1)S(1)} %all-to-all-done.embed_own), channel_id=1, source_target_pairs={{0,128},{128,0},{1,129},{129,1},{2,130},{130,2},{3,131},{131,3},{4... | collective-permute-start | bytes 2261000 | tf_op jit(solution)/shard_map/ppermute | solution.py:286
  83.9 4.1 %collective-permute-start.1 = (bf16[8,184,256]{2,1,0:T(8,128)(2,1)S(1)}, bf16[8,184,256]{2,1,0:T(8,128)(2,1)S(1)}, u32[]{:S(2)}, u32[]{:S(2)}) collective-permute-start(bf16[8,184,256]{2,1,0:T(8,128)(2,1)S(1)} %all-to-all-done.2.merged_own), channel_id=1, source_target_pairs={{0,128},{128,0},{1,129},{129,1},{2,130},{130,2},{3,131},{131,3},{4... | collective-permute-start | bytes 2261000 | tf_op jit(solution)/shard_map/ppermute | solution.py:286
  99.9 26.3 %all-to-all-start.3 = ((bf16[16,64,128]{2,1,0:T(8,128)(2,1)}), bf16[16,64,128]{2,1,0:T(8,128)(2,1)S(1)}, u32[]{:S(2)}, u32[]{:S(2)}) async-start(bf16[16,64,128]{2,1,0:T(8,128)(2,1)} %get-tuple-element.19), calls=%async_computation.3 | async-start | bytes 524288 | tf_op jit(solution)/shard_map/all_to_all | solution.py:311
  126.2 10.8 %collective-permute-start.2 = (bf16[16,64,128]{2,1,0:T(8,128)(2,1)S(1)}, bf16[16,64,128]{2,1,0:T(8,128)(2,1)S(1)}, u32[]{:S(2)}, u32[]{:S(2)}) collective-permute-start(bf16[16,64,128]{2,1,0:T(8,128)(2,1)S(1)} %all-to-all-done.3.keys_ref), channel_id=1, source_target_pairs={{0,4},{4,0},{1,5},{5,1},{2,6},{6,2},{3,7},{7,3},{8,12},{12,8},{9,1... | collective-permute-start | bytes 786440 | tf_op jit(solution)/shard_map/ppermute | solution.py:323
Sparse Core Ops, SparseCore 0:
  16.6 78.6 all-gather.7

commit v8 on v7

--- a/solution.py
+++ b/solution.py
@@ -144,7 +144,7 @@
     out_ref[source, HD:] = jnp.where(row == 0, top, total)
 
 
-def own_kernel(query_ref, own_ref, place_ref, out_ref):
+def own_kernel(query_ref, own_ref, place_ref, out_ref, ready_ref):
     x_id = place_ref[1]
     own = own_ref[...]
     chunk = own.shape[0]
@@ -154,6 +154,7 @@
     own_bias = jnp.where((lane // (2 * BLK) == x_id // 2) & (key_row <= lane % BLK), 0.0, -1e30)
     for source in range(query_ref.shape[0]):
         queries = heads_of(query_ref, source)
+        ready_ref[source] = queries
         scores = jnp.dot(own, queries, preferred_element_type=jnp.float32) + own_bias
         top = jnp.maximum(jnp.max(scores, axis=0, keepdims=True), -1e20)
         weights = jnp.exp(scores - top)
@@ -167,10 +168,10 @@
     return tuple(state_ref[source, r, :] for r in rows)
 
 
-def more_kernel(query_ref, keys_ref, bias_ref, state_ref, out_ref):
-    for source in range(query_ref.shape[0]):
+def more_kernel(ready_ref, keys_ref, bias_ref, state_ref, out_ref):
+    for source in range(ready_ref.shape[0]):
         state = load_state(state_ref, source)
-        store_state(out_ref, source, attend_keys(heads_of(query_ref, source), keys_ref, bias_ref, state))
+        store_state(out_ref, source, attend_keys(ready_ref[source], keys_ref, bias_ref, state))
 
 
 def thirds(value):
@@ -179,11 +180,10 @@
     return high, middle, value - high - middle
 
 
-def last_kernel(query_ref, keys_ref, bias_ref, state_ref, out_ref):
-    for source in range(query_ref.shape[0]):
-        top, total, accum = attend_keys(
-            heads_of(query_ref, source), keys_ref, bias_ref, load_state(state_ref, source)
-        )
+def last_kernel(ready_ref, keys_ref, bias_ref, state_ref, out_ref):
+    for source in range(ready_ref.shape[0]):
+        state = load_state(state_ref, source)
+        top, total, accum = attend_keys(ready_ref[source], keys_ref, bias_ref, state)
         out_ref[source, :HD] = accum.astype(jnp.bfloat16)
         row = lax.broadcasted_iota(jnp.int32, (out_ref.shape[1] - HD, accum.shape[1]), 0)
         rest = jnp.zeros(row.shape, jnp.float32)
@@ -311,11 +311,11 @@
     taken = lax.all_to_all(sent, "z", 0, 0)
     queries = lax.all_gather(query, "x", axis=0)
     state = jax.ShapeDtypeStruct((n_x, HD + 8, 4 * BLK), jnp.float32)
-    parts = pl.pallas_call(
+    parts, queries = pl.pallas_call(
         own_kernel,
-        out_shape=state,
+        out_shape=(state, jax.ShapeDtypeStruct((n_x, 2 * HD, 4 * BLK), jnp.bfloat16)),
         in_specs=[VMEM] * 2 + [smem],
-        out_specs=VMEM,
+        out_specs=(VMEM, VMEM),
         compiler_params=params,
         name="attend_own",
     )(queries, own, place)

time: 160 us -> 160 us (level)
  no operation moved by 1% of the time
where the time goes in v8:
time: 160 us; the launch traced here: 159 us
  blocking collectives  71 us (44%)
  Pallas kernels  26.1 us (16%)
  waiting for transfers between devices  24.6 us (15%)
  starting transfers between devices  23.5 us (15%)
  between operations  13.5 us (8%)
    all_to_all x1, blocking collectives, body(): parts = lax.all_to_all(partial, 'x', 0, 0)  16.6 us
    all_gather x1, blocking collectives, body(): queries = lax.all_gather(query, 'x', axis=0)  13.2 us
    all_to_all x1, blocking collectives, body(): parts = lax.all_to_all(parts, 'x', 0, 0)  10.1 us
    all_to_all x2, waiting for transfers between devices, over_x(): own = lax.all_to_all(copies, 'x', 0, 0, tiled=True)  9.3 us
    all_gather x1, blocking collectives, body(): low = lax.all_gather(low, SEG, axis=0)  8.74 us
    all_gather x1, blocking collectives, body(): weights = lax.all_gather(packed, 'yh', axis=0)  8.38 us
    all_to_all x1, starting transfers between devices, body(): taken = lax.all_to_all(sent, 'z', 0, 0)  7.94 us
    all_gather x1, blocking collectives, body(): high = lax.all_gather(high, SEG, axis=0)  7.62 us
  transfers between devices with their start and end apart: 7, of which 6 were waited for; matrix products, arithmetic and copies ran while one was open for 0% of the time, Pallas kernels for 9%

profile of v8, /device:TPU:32, one launch (start us, length us, event | category | flops | bytes accessed | tf_op | source)
XLA Modules:
  0.0 159.3 jit_solution(17404762557771591516)
XLA Ops:
  6.5 0.0 all-gather.8.cloned.1.call-start
  6.5 1.6 pack.1
  8.1 8.4 %all-gather.3 = bf16[368,256]{1,0:T(8,128)(2,1)} all-gather(bf16[184,256]{1,0:T(8,128)(2,1)} %pack.1), channel_id=5, replica_groups=mesh['yl'=2,'core'=2,'z'=16,'yh'=2,'x'=4] {'yh'}, dimensions={0}, use_global_device_ids=true | all-gather | bytes 282624 | tf_op jit(solution)/shard_map/all_gather | solution.py:235
  16.5 0.0 all-gather.8.cloned.1.call-update
  16.5 1.8 %split.1 = (bf16[368,256]{1,0:T(8,128)(2,1)}, bf16[352,256]{1,0:T(8,128)(2,1)}) custom-call(bf16[720,256]{1,0:T(8,128)(2,1)} %bitcast.25), custom_call_target="tpu_custom_call" | custom-call | tf_op jit(solution)/shard_map/split/pallas_call | solution.py:241
  18.3 0.1 pad_add_fusion.place_ref
  18.3 7.6 %all-gather.1 = bf16[1408,256]{1,0:T(8,128)(2,1)S(1)} all-gather(bf16[352,256]{1,0:T(8,128)(2,1)} %get-tuple-element.18), channel_id=3, replica_groups=mesh['yl'=2,'core'=2,'z'=16,'yh'=2,'x'=4] {'yl','core'}, dimensions={0}, use_global_device_ids=true | all-gather | bytes 901120 | tf_op jit(solution)/shard_map/all_gather | solution.py:249
  26.0 8.7 %all-gather = bf16[1472,256]{1,0:T(8,128)(2,1)S(1)} all-gather(bf16[368,256]{1,0:T(8,128)(2,1)} %get-tuple-element.17), channel_id=2, replica_groups=mesh['yl'=2,'core'=2,'z'=16,'yh'=2,'x'=4] {'yl','core'}, dimensions={0}, use_global_device_ids=true | all-gather | bytes 942080 | tf_op jit(solution)/shard_map/all_gather | solution.py:248
  34.7 4.2 %merge.1 = (f32[4,180,256]{2,1,0:T(8,128)S(1)}, bf16[8,184,256]{2,1,0:T(8,128)(2,1)}) custom-call(bf16[4,368,256]{2,1,0:T(8,128)(2,1)S(1)} %bitcast.20, bf16[4,352,256]{2,1,0:T(8,128)(2,1)S(1)} %bitcast.21, bf16[3,720,720]{2,1,0:T(8,128)(2,1)} %weight_hbm.1, s32[2]{0:T(128)S(1)} %pad_add_fusion.place_ref), custom_call_target="tpu_custom_call" | custom-call | tf_op jit(solution)/shard_map/merge/pallas_call | solution.py:251
  38.9 16.6 %all_to_all.25.parts_ref = f32[4,180,256]{2,1,0:T(8,128)} all-to-all(f32[4,180,256]{2,1,0:T(8,128)S(1)} %get-tuple-element.20), channel_id=1, replica_groups=mesh['yl'=2,'core'=2,'z'=16,'yh'=2,'x'=4] {'x'}, dimensions={0} | all-to-all | bytes 1474560 | tf_op jit(solution)/shard_map/all_to_all | solution.py:267
  55.5 3.5 %all-to-all-start = ((bf16[8,184,256]{2,1,0:T(8,128)(2,1)}), bf16[8,184,256]{2,1,0:T(8,128)(2,1)S(1)}, u32[]{:S(2)}, u32[]{:S(2)}) async-start(bf16[8,184,256]{2,1,0:T(8,128)(2,1)} %get-tuple-element.19), calls=%async_computation | async-start | bytes 1507328 | tf_op jit(solution)/shard_map/all_to_all | solution.py:285
  59.0 1.8 %settle.1 = bf16[184,256]{1,0:T(8,128)(2,1)} custom-call(f32[4,180,256]{2,1,0:T(8,128)} %all_to_all.25.parts_ref), custom_call_target="tpu_custom_call" | custom-call | tf_op jit(solution)/shard_map/settle/pallas_call | solution.py:268
  60.8 6.4 %all-gather.2 = bf16[368,256]{1,0:T(8,128)(2,1)} all-gather(bf16[184,256]{1,0:T(8,128)(2,1)} %settle.1), channel_id=4, replica_groups=mesh['yl'=2,'core'=2,'z'=16,'yh'=2,'x'=4] {'yl'}, dimensions={0}, use_global_device_ids=true | all-gather | bytes 282624 | tf_op jit(solution)/shard_map/all_gather | solution.py:275
  67.2 1.8 %spread.1 = bf16[8,184,256]{2,1,0:T(8,128)(2,1)} custom-call(bf16[2,184,256]{2,1,0:T(8,128)(2,1)} %bitcast.23), custom_call_target="tpu_custom_call" | custom-call | tf_op jit(solution)/shard_map/spread/pallas_call | solution.py:276
  69.0 1.2 all-to-all-done.embed_own
  70.2 3.5 %all-to-all-start.2 = ((bf16[8,184,256]{2,1,0:T(8,128)(2,1)}), bf16[8,184,256]{2,1,0:T(8,128)(2,1)S(1)}, u32[]{:S(2)}, u32[]{:S(2)}) async-start(bf16[8,184,256]{2,1,0:T(8,128)(2,1)} %spread.1), calls=%async_computation.2 | async-start | bytes 1507328 | tf_op jit(solution)/shard_map/all_to_all | solution.py:285
  73.8 0.0 copy-start
  73.8 2.0 %collective-permute-start = (bf16[8,184,256]{2,1,0:T(8,128)(2,1)S(1)}, bf16[8,184,256]{2,1,0:T(8,128)(2,1)S(1)}, u32[]{:S(2)}, u32[]{:S(2)}) collective-permute-start(bf16[8,184,256]{2,1,0:T(8,128)(2,1)S(1)} %all-to-all-done.embed_own), channel_id=1, source_target_pairs={{0,128},{128,0},{1,129},{129,1},{2,130},{130,2},{3,131},{131,3},{4... | collective-permute-start | bytes 2261000 | tf_op jit(solution)/shard_map/ppermute | solution.py:286
  75.8 8.1 %all-to-all-done.2.merged_own = bf16[8,184,256]{2,1,0:T(8,128)(2,1)S(1)} async-done(((bf16[8,184,256]{2,1,0:T(8,128)(2,1)}), bf16[8,184,256]{2,1,0:T(8,128)(2,1)S(1)}, u32[]{:S(2)}, u32[]{:S(2)}) %all-to-all-start.2) | async-done | bytes 753696 | tf_op jit(solution)/shard_map/all_to_all | solution.py:285
  83.9 1.9 %collective-permute-start.1 = (bf16[8,184,256]{2,1,0:T(8,128)(2,1)S(1)}, bf16[8,184,256]{2,1,0:T(8,128)(2,1)S(1)}, u32[]{:S(2)}, u32[]{:S(2)}) collective-permute-start(bf16[8,184,256]{2,1,0:T(8,128)(2,1)S(1)} %all-to-all-done.2.merged_own), channel_id=1, source_target_pairs={{0,128},{128,0},{1,129},{129,1},{2,130},{130,2},{3,131},{131,3},{4... | collective-permute-start | bytes 2261000 | tf_op jit(solution)/shard_map/ppermute | solution.py:286
  85.8 0.0 collective-permute-done.embed_other
  85.9 2.2 %collective-permute-done.1.merged_other = bf16[8,184,256]{2,1,0:T(8,128)(2,1)S(1)} collective-permute-done((bf16[8,184,256]{2,1,0:T(8,128)(2,1)S(1)}, bf16[8,184,256]{2,1,0:T(8,128)(2,1)S(1)}, u32[]{:S(2)}, u32[]{:S(2)}) %collective-permute-start.1) | collective-permute-done | bytes 753696 | tf_op jit(solution)/shard_map/ppermute | solution.py:286
  88.0 7.3 %all-gather.8.cloned.1.call-done.weights_hbm = bf16[32,184,256]{2,1,0:T(8,128)(2,1)} async-done(((bf16[2,184,256]{2,1,0:T(8,128)(2,1)}), bf16[32,184,256]{2,1,0:T(8,128)(2,1)}) %all-gather.8.cloned.1.call-update) | async-done | bytes 3014672 | tf_op jit(solution)/shard_map/all_gather | solution.py:236
  95.4 4.5 %project.1 = (bf16[128,256]{1,0:T(8,128)(2,1)S(1)}, bf16[16,64,128]{2,1,0:T(8,128)(2,1)}, bf16[64,128]{1,0:T(8,128)(2,1)S(1)}) custom-call(bf16[8,184,256]{2,1,0:T(8,128)(2,1)S(1)} %all-to-all-done.embed_own, bf16[8,184,256]{2,1,0:T(8,128)(2,1)S(1)} %collective-permute-done.embed_other, bf16[8,184,256]{2,1,0:T(8,128)(2,1)S(1)} %all-to-all-done.2.merged_own, ...), custom_call_target="tpu_custom_call" | custom-call | tf_op jit(solution)/shard_map/project/pallas_call | solution.py:294
  99.9 7.9 %all-to-all-start.3 = ((bf16[16,64,128]{2,1,0:T(8,128)(2,1)}), bf16[16,64,128]{2,1,0:T(8,128)(2,1)S(1)}, u32[]{:S(2)}, u32[]{:S(2)}) async-start(bf16[16,64,128]{2,1,0:T(8,128)(2,1)} %get-tuple-element.21), calls=%async_computation.3 | async-start | bytes 524288 | tf_op jit(solution)/shard_map/all_to_all | solution.py:311
  107.9 0.0 copy-done
  107.9 0.1 reshape.10
  108.0 0.1 dynamic_slice.3
  108.1 0.1 broadcast_bitcast_fusion
  108.1 0.1 slice_select_fusion
  108.2 0.1 copy.9
  108.3 13.2 %all-gather.5 = bf16[512,256]{1,0:T(8,128)(2,1)S(1)} all-gather(bf16[128,256]{1,0:T(8,128)(2,1)S(1)} %get-tuple-element.22), channel_id=7, replica_groups=mesh['yl'=2,'core'=2,'z'=16,'yh'=2,'x'=4] {'x'}, dimensions={0}, use_global_device_ids=true | all-gather | bytes 327680 | tf_op jit(solution)/shard_map/all_gather | solution.py:312
  121.5 1.5 attend_own.1
  123.0 3.2 %all-to-all-done.3.keys_ref = bf16[16,64,128]{2,1,0:T(8,128)(2,1)S(1)} async-done(((bf16[16,64,128]{2,1,0:T(8,128)(2,1)}), bf16[16,64,128]{2,1,0:T(8,128)(2,1)S(1)}, u32[]{:S(2)}, u32[]{:S(2)}) %all-to-all-start.3) | async-done | bytes 262176 | tf_op jit(solution)/shard_map/all_to_all | solution.py:311
  126.2 4.6 %collective-permute-start.2 = (bf16[16,64,128]{2,1,0:T(8,128)(2,1)S(1)}, bf16[16,64,128]{2,1,0:T(8,128)(2,1)S(1)}, u32[]{:S(2)}, u32[]{:S(2)}) collective-permute-start(bf16[16,64,128]{2,1,0:T(8,128)(2,1)S(1)} %all-to-all-done.3.keys_ref), channel_id=1, source_target_pairs={{0,4},{4,0},{1,5},{5,1},{2,6},{6,2},{3,7},{7,3},{8,12},{12,8},{9,1... | collective-permute-start | bytes 786440 | tf_op jit(solution)/shard_map/ppermute | solution.py:323
  130.8 0.1 compare_select_fusion
  130.9 3.6 %attend_more.2.state_ref = f32[4,72,512]{2,1,0:T(8,128)S(1)} custom-call(bf16[4,128,512]{2,1,0:T(8,128)(2,1)S(1)} %get-tuple-element.26.ready_ref, bf16[16,64,128]{2,1,0:T(8,128)(2,1)S(1)} %all-to-all-done.3.keys_ref, f32[16,512]{1,0:T(8,128)S(1)} %get-tuple-element.29.bias_ref, f32[4,72,512]{2,1,0:T(8,128)S(1)} %get-tuple-element.28.state_ref), custom_call_target="tpu_custom_call" | custom-call | flops 536870912 | bytes 2097152 | tf_op jit(solution)/shard_map/attend_more/pallas_call | solution.py:338
  134.5 2.5 %collective-permute-done.2.keys_ref = bf16[16,64,128]{2,1,0:T(8,128)(2,1)S(1)} collective-permute-done((bf16[16,64,128]{2,1,0:T(8,128)(2,1)S(1)}, bf16[16,64,128]{2,1,0:T(8,128)(2,1)S(1)}, u32[]{:S(2)}, u32[]{:S(2)}) %collective-permute-start.2) | collective-permute-done | bytes 262176 | tf_op jit(solution)/shard_map/ppermute | solution.py:323
  137.0 3.6 %attend_more.3 = bf16[4,80,512]{2,1,0:T(8,128)(2,1)S(1)} custom-call(bf16[4,128,512]{2,1,0:T(8,128)(2,1)S(1)} %get-tuple-element.26.ready_ref, bf16[16,64,128]{2,1,0:T(8,128)(2,1)S(1)} %collective-permute-done.2.keys_ref, f32[16,512]{1,0:T(8,128)S(1)} %get-tuple-element.30.bias_ref, f32[4,72,512]{2,1,0:T(8,128)S(1)} %attend_more.2.state_ref), custom_call_target="tpu_custom_call" | custom-call | flops 536870912 | bytes 2097152 | tf_op jit(solution)/shard_map/attend_more/pallas_call | solution.py:338
  140.6 10.1 %all_to_all.26.parts_ref = bf16[4,80,512]{2,1,0:T(8,128)(2,1)} all-to-all(bf16[4,80,512]{2,1,0:T(8,128)(2,1)S(1)} %attend_more.3), channel_id=1, replica_groups=mesh['yl'=2,'core'=2,'z'=16,'yh'=2,'x'=4] {'x'}, dimensions={0} | all-to-all | bytes 655360 | tf_op jit(solution)/shard_map/all_to_all | solution.py:347
  150.7 1.8 %combine.1 = bf16[256,128]{1,0:T(8,128)(2,1)} custom-call(bf16[4,80,512]{2,1,0:T(8,128)(2,1)} %all_to_all.26.parts_ref), custom_call_target="tpu_custom_call" | custom-call | tf_op jit(solution)/shard_map/combine/pallas_call | solution.py:348
  (2 shorter events, 0.0 us)
Async XLA Ops:
  6.5 88.8 %all-gather.8.cloned.1.call-start = ((), (), s32[]{:S(2)}) async-start(), calls=%async_computation.5 | async-start | bytes 3203072 | tf_op jit(solution)/shard_map/all_gather | solution.py:236
  55.5 14.8 %all-to-all-start = ((bf16[8,184,256]{2,1,0:T(8,128)(2,1)}), bf16[8,184,256]{2,1,0:T(8,128)(2,1)S(1)}, u32[]{:S(2)}, u32[]{:S(2)}) async-start(bf16[8,184,256]{2,1,0:T(8,128)(2,1)} %get-tuple-element.19), calls=%async_computation | async-start | bytes 1507328 | tf_op jit(solution)/shard_map/all_to_all | solution.py:285
  70.2 13.7 %all-to-all-start.2 = ((bf16[8,184,256]{2,1,0:T(8,128)(2,1)}), bf16[8,184,256]{2,1,0:T(8,128)(2,1)S(1)}, u32[]{:S(2)}, u32[]{:S(2)}) async-start(bf16[8,184,256]{2,1,0:T(8,128)(2,1)} %spread.1), calls=%async_computation.2 | async-start | bytes 1507328 | tf_op jit(solution)/shard_map/all_to_all | solution.py:285
  73.8 34.1 %copy-start = (s32[64]{0:T(128)S(1)}, s32[64]{0:T(128)}, u32[]{:S(2)}) copy-start(s32[64]{0:T(128)} %param.11) | copy-start | bytes 772
  73.8 12.1 %collective-permute-start = (bf16[8,184,256]{2,1,0:T(8,128)(2,1)S(1)}, bf16[8,184,256]{2,1,0:T(8,128)(2,1)S(1)}, u32[]{:S(2)}, u32[]{:S(2)}) collective-permute-start(bf16[8,184,256]{2,1,0:T(8,128)(2,1)S(1)} %all-to-all-done.embed_own), channel_id=1, source_target_pairs={{0,128},{128,0},{1,129},{129,1},{2,130},{130,2},{3,131},{131,3},{4... | collective-permute-start | bytes 2261000 | tf_op jit(solution)/shard_map/ppermute | solution.py:286
  83.9 4.1 %collective-permute-start.1 = (bf16[8,184,256]{2,1,0:T(8,128)(2,1)S(1)}, bf16[8,184,256]{2,1,0:T(8,128)(2,1)S(1)}, u32[]{:S(2)}, u32[]{:S(2)}) collective-permute-start(bf16[8,184,256]{2,1,0:T(8,128)(2,1)S(1)} %all-to-all-done.2.merged_own), channel_id=1, source_target_pairs={{0,128},{128,0},{1,129},{129,1},{2,130},{130,2},{3,131},{131,3},{4... | collective-permute-start | bytes 2261000 | tf_op jit(solution)/shard_map/ppermute | solution.py:286
  99.9 26.3 %all-to-all-start.3 = ((bf16[16,64,128]{2,1,0:T(8,128)(2,1)}), bf16[16,64,128]{2,1,0:T(8,128)(2,1)S(1)}, u32[]{:S(2)}, u32[]{:S(2)}) async-start(bf16[16,64,128]{2,1,0:T(8,128)(2,1)} %get-tuple-element.21), calls=%async_computation.3 | async-start | bytes 524288 | tf_op jit(solution)/shard_map/all_to_all | solution.py:311
  126.2 10.8 %collective-permute-start.2 = (bf16[16,64,128]{2,1,0:T(8,128)(2,1)S(1)}, bf16[16,64,128]{2,1,0:T(8,128)(2,1)S(1)}, u32[]{:S(2)}, u32[]{:S(2)}) collective-permute-start(bf16[16,64,128]{2,1,0:T(8,128)(2,1)S(1)} %all-to-all-done.3.keys_ref), channel_id=1, source_target_pairs={{0,4},{4,0},{1,5},{5,1},{2,6},{6,2},{3,7},{7,3},{8,12},{12,8},{9,1... | collective-permute-start | bytes 786440 | tf_op jit(solution)/shard_map/ppermute | solution.py:323
Sparse Core Ops, SparseCore 0:
  16.6 78.7 all-gather.7
